TPU v7x, 32 devices: a whole 2x2x4 slice. The times are simulated.
32 devices in a mesh: seq: 4 (over y, x), mp: 8 (over z, core).
Axes of the slice: x: 2, y: 2, z: 4, core: 2. Of those that a mesh axis runs over, the one named last changes fastest.
Arguments:
- tokens: bfloat16 [512, 4096], P('seq', 'mp'), may hold values from -68 to 68
- w_qkv: bfloat16 [3, 4096, 4096], P(None, None, 'mp'), may hold values from -0.09375 to 0.09375
- w_pos: bfloat16 [4096, 4096], P(None, 'mp'), may hold values from -0.09375 to 0.09375
- w_out: bfloat16 [4096, 4096], P('mp'), may hold values from -0.09375 to 0.09375
- content_bias: float32 [32, 128], P('mp'), may hold values from -4 to 4
- position_bias: float32 [32, 128], P('mp'), may hold values from -4 to 4
- doc_ids: int32 [512], P('seq'), may hold values from 0 to 3, never falling along the last dimension, each value on 1 to 256 neighbouring positions
Outputs:
- attn_out: bfloat16 [512, 4096], P('seq', 'mp')
All inputs are finite; a program needn't handle non-finite values.
Results may differ from a plain program's by a relative error of at most 0.0067.
Values may be sent and summed in bfloat16 or wider, within the bound.
No kernel may reach another device: no remote copies, remote signals or barrier semaphores. Data moves between devices by JAX's collectives and lax.ppermute only.
A program may use at most 64 MiB of HBM per device.

v0:
```python
import jax
import jax.numpy as jnp
from jax import lax
from jax.sharding import PartitionSpec as P


def passed_along(value, axis, steps):
    count = lax.axis_size(axis)
    initial, last = (max(0, -steps), min(count, count - steps))
    return lax.ppermute(value, axis, [(source, source + steps) for source in range(initial, last)])


def sinus_table(count, width):
    place = jnp.arange(count, dtype=jnp.float32)[:, None]
    freqs = 1.0 / 10000.0 ** (jnp.arange(0, width, 2, dtype=jnp.float32) / width)
    angle = place * freqs[None, :]
    return jnp.concatenate([jnp.sin(angle), jnp.cos(angle)], axis=1).astype(jnp.bfloat16)


def relative_skew(reversed_scores):
    heads_here, rows, span = reversed_scores.shape
    padded = jnp.concatenate(
        [reversed_scores, jnp.zeros((heads_here, rows, rows), jnp.float32)], axis=2
    )
    width = span + rows
    flat = padded.reshape(heads_here, rows * width)
    sliced = flat[:, rows - 1 : rows - 1 + rows * (width - 1)]
    return sliced.reshape(heads_here, rows, width - 1)[:, :, :span]


def attend(query_content, query_pos, keys, values, rel_keys, allowed, heads_here, head_dim):
    rows = query_content.shape[0]
    span = keys.shape[0]
    qc_heads = query_content.reshape(rows, heads_here, head_dim)
    qp_heads = query_pos.reshape(rows, heads_here, head_dim)
    key_heads = keys.reshape(span, heads_here, head_dim)
    val_heads = values.reshape(span, heads_here, head_dim)
    rel_heads = rel_keys[::-1].reshape(span, heads_here, head_dim)
    content = jnp.einsum("ihd,jhd->hij", qc_heads, key_heads, preferred_element_type=jnp.float32)
    reversed_scores = jnp.einsum(
        "ihd,rhd->hir", qp_heads, rel_heads, preferred_element_type=jnp.float32
    )
    pos = relative_skew(reversed_scores)
    score = (content + pos) * (1.0 / jnp.sqrt(jnp.float32(head_dim)))
    score = jnp.where(allowed[None], score, jnp.float32(-1e30))
    top = jnp.max(score, axis=2, keepdims=True)
    expo = jnp.where(allowed[None], jnp.exp(score - top), jnp.float32(0.0))
    weights = (expo / jnp.sum(expo, axis=2, keepdims=True)).astype(jnp.bfloat16)
    out = jnp.einsum("hij,jhd->ihd", weights, val_heads, preferred_element_type=jnp.float32)
    return out.astype(jnp.bfloat16).reshape(rows, heads_here * head_dim)


def shards(tokens, w_qkv, w_pos, w_out, content_bias, position_bias, doc_ids):
    seg_rows = tokens.shape[0]
    full_width = w_qkv.shape[1]
    local_width = w_qkv.shape[2]
    heads_here = content_bias.shape[0]
    head_dim = content_bias.shape[1]
    proj = jnp.einsum(
        "tf,cfw->ctw",
        lax.all_gather(tokens, "mp", axis=1, tiled=True),
        w_qkv,
        preferred_element_type=jnp.float32,
    )
    query_content = (proj[0] + content_bias.reshape(local_width)[None, :]).astype(jnp.bfloat16)
    query_pos = (proj[0] + position_bias.reshape(local_width)[None, :]).astype(jnp.bfloat16)
    key_rows = proj[1].astype(jnp.bfloat16)
    value_rows = proj[2].astype(jnp.bfloat16)
    mem_keys, mem_values, mem_doc = passed_along((key_rows, value_rows, doc_ids), "seq", 1)
    keys = jnp.concatenate([mem_keys, key_rows], axis=0)
    values = jnp.concatenate([mem_values, value_rows], axis=0)
    key_doc = jnp.concatenate([mem_doc, doc_ids], axis=0)
    rel_keys = jnp.dot(
        sinus_table(2 * seg_rows, full_width), w_pos, preferred_element_type=jnp.float32
    ).astype(jnp.bfloat16)
    key_place = jnp.arange(2 * seg_rows, dtype=jnp.int32)
    reach = key_place[None, :] <= jnp.arange(seg_rows, dtype=jnp.int32)[:, None] + seg_rows
    exists = (lax.axis_index("seq") > 0) | (key_place >= seg_rows)
    allowed = reach & exists[None, :] & (key_doc[None, :] == doc_ids[:, None])
    head_out = attend(
        query_content, query_pos, keys, values, rel_keys, allowed, heads_here, head_dim
    )
    term = jnp.dot(head_out, w_out, preferred_element_type=jnp.float32)
    result = lax.psum_scatter(term, "mp", scatter_dimension=1, tiled=True)
    return result.astype(jnp.bfloat16)


def solution(mesh):
    in_specs = (
        P("seq", "mp"),
        P(None, None, "mp"),
        P(None, "mp"),
        P("mp", None),
        P("mp", None),
        P("mp", None),
        P("seq"),
    )
    out_specs = P("seq", "mp")
    return jax.shard_map(shards, mesh=mesh, in_specs=in_specs, out_specs=out_specs, check_vma=False)
```

profile of v0, /device:TPU:0, one launch (start us, length us, event | category | flops | bytes accessed | tf_op | source)
XLA Modules:
  0.0 101.3 jit_solution(8567334906748220211)
XLA Ops:
  6.5 0.7 all-gather.2.cloned.1.call-update
  7.3 0.0 reduce-scatter.2.cloned.1.call-start
  7.3 4.8 %collective-permute-start.1 = (s32[128]{0:T(128)}, s32[128]{0:T(128)S(1)}, u32[]{:S(2)}, u32[]{:S(2)}) collective-permute-start(s32[128]{0:T(128)} %param.13), channel_id=1, source_target_pairs={{0,8},{8,16},{16,24},{1,9},{9,17},{17,25},{2,10},{10,18},{18,26},{... | collective-permute-start | bytes 1544 | tf_op jit(solution)/shard_map/ppermute | solution.py:10
  12.2 7.8 %sine_convert_fusion = (bf16[256,2048]{1,0:T(8,128)(2,1)S(1)}, bf16[256,2048]{1,0:T(8,128)(2,1)S(1)}) fusion(f32[2048]{0:T(1024)S(1)} %negate_power_fusion), kind=kLoop, calls=%fused_computation.6 | loop fusion | flops 1572864 | bytes 2105344 | tf_op jit(solution)/shard_map/convert
  20.0 3.4 %fusion.10 = bf16[256,512]{1,0:T(8,128)(2,1)S(1)} fusion(bf16[4096,512]{1,0:T(8,128)(2,1)} %param.9, bf16[256,2048]{1,0:T(8,128)(2,1)S(1)} %get-tuple-element.8, bf16[256,2048]{1,0:T(8,128)(2,1)S(1)} %get-tuple-element.7), kind=kOutput, calls=%fused_computation.15 | convolution fusion | flops 1078067200 | bytes 6553600 | tf_op jit(solution)/shard_map/dot_general | solution.py:73
  23.4 0.3 rev.3
  23.8 0.1 fusion.21
  23.9 10.0 %all-gather.2.cloned.1.call-done = bf16[128,4096]{1,0:T(8,128)(2,1)} async-done(((bf16[128,512]{1,0:T(8,128)(2,1)}), bf16[128,4096]{1,0:T(8,128)(2,1)}) %all-gather.2.cloned.1.call-update) | async-done | bytes 1048592 | tf_op jit(solution)/shard_map/all_gather | solution.py:61
  33.9 6.7 %fusion.25 = (bf16[3,128,512]{1,2,0:T(8,128)(2,1)S(1)}, f32[3,128,512]{1,2,0:T(8,128)S(1)}) fusion(bf16[3,4096,512]{2,1,0:T(8,128)(2,1)} %param.8, bf16[128,4096]{1,0:T(8,128)(2,1)} %all-gather.2.cloned.1.call-done), kind=kOutput, calls=%fused_computation.42 | convolution fusion | flops 1610809344 | bytes 14811136 | tf_op jit(solution)/shard_map/tf,cfw->ctw/dot_general | solution.py:59
  40.7 3.1 %collective-permute-start = (bf16[128,512]{0,1:T(8,128)(2,1)S(1)}, bf16[128,512]{0,1:T(8,128)(2,1)S(1)}, u32[]{:S(2)}, u32[]{:S(2)}) collective-permute-start(bf16[128,512]{0,1:T(8,128)(2,1)S(1)} %get-tuple-element.6), channel_id=1, source_target_pairs={{0,8},{8,16},{16,24},{1,9},{9,17},{17,25},{2,10},{10,18},{18,26},{... | collective-permute-start | bytes 393224 | tf_op jit(solution)/shard_map/ppermute | solution.py:10
  43.8 3.5 %collective-permute-start.2 = (bf16[128,512]{0,1:T(8,128)(2,1)S(1)}, bf16[128,512]{0,1:T(8,128)(2,1)S(1)}, u32[]{:S(2)}, u32[]{:S(2)}) collective-permute-start(bf16[128,512]{0,1:T(8,128)(2,1)S(1)} %get-tuple-element.5), channel_id=1, source_target_pairs={{0,8},{8,16},{16,24},{1,9},{9,17},{17,25},{2,10},{10,18},{18,26},{... | collective-permute-start | bytes 393224 | tf_op jit(solution)/shard_map/ppermute | solution.py:10
  47.4 0.1 copy.14
  47.5 0.2 fusion.14
  47.8 0.1 pad_bitcast_fusion
  47.8 0.5 copy.21
  48.3 0.5 slice.26
  48.8 0.9 reshape.120
  49.7 0.5 collective-permute-done.2
  50.2 0.2 fusion.9
  50.5 0.3 fusion.26
  50.8 1.1 %convolution_convert_fusion = bf16[4,128,128]{2,1,0:T(8,128)(2,1)S(1)} fusion(bf16[256,4,128]{0,2,1:T(8,128)(2,1)S(1)} %bitcast.38, f32[4,128]{1,0:T(4,128)S(1)} %fusion.26, f32[4,128,256]{2,1,0:T(8,128)S(1)} %fusion.9, pred[128,256]{1,0:T(8,128)(4,1)S(1)} %fusion.21), kind=kOutput, calls=%fused_computation.16 | convolution fusion | flops 34145024 | bytes 952320 | tf_op jit(solution)/shard_map/hij,jhd->ihd/dot_general | solution.py:49
  51.8 4.3 %fusion.27 = f32[128,4096]{1,0:T(8,128)} fusion(bf16[128,512]{0,1:T(8,128)(2,1)S(1)} %bitcast.39, bf16[512,4096]{1,0:T(8,128)(2,1)} %param.10), kind=kOutput, calls=%fused_computation.44 | convolution fusion | flops 536870912 | bytes 6422528 | tf_op jit(solution)/shard_map/dot_general | solution.py:83
  56.1 36.7 %reduce-scatter.2.cloned.1.call-done = f32[128,512]{1,0:T(8,128)} async-done(((f32[128,4096]{1,0:T(8,128)}), f32[128,512]{1,0:T(8,128)}) %reduce-scatter.2.cloned.1.call-update) | async-done | bytes 262160 | tf_op jit(solution)/shard_map/reduce_scatter | solution.py:84
  92.8 1.6 %convert_element_type.40 = bf16[128,512]{1,0:T(8,128)(2,1)} convert(f32[128,512]{1,0:T(8,128)} %reduce-scatter.2.cloned.1.call-done) | non-fusion elementwise | flops 65536 | bytes 393216 | tf_op jit(solution)/shard_map/convert_element_type | solution.py:85
  (18 shorter events, 0.2 us)
Async XLA Ops:
  6.5 27.4 %all-gather.2.cloned.1.call-start = ((), (), s32[]{:S(2)}) async-start(), calls=%async_computation.1 | async-start | bytes 1179648 | tf_op jit(solution)/shard_map/all_gather | solution.py:61
  7.3 85.6 %reduce-scatter.2.cloned.1.call-start = ((), (), s32[]{:S(2)}) async-start(), calls=%async_computation.2 | async-start | bytes 2359296 | tf_op jit(solution)/shard_map/reduce_scatter | solution.py:84
  7.3 16.5 %collective-permute-start.1 = (s32[128]{0:T(128)}, s32[128]{0:T(128)S(1)}, u32[]{:S(2)}, u32[]{:S(2)}) collective-permute-start(s32[128]{0:T(128)} %param.13), channel_id=1, source_target_pairs={{0,8},{8,16},{16,24},{1,9},{9,17},{17,25},{2,10},{10,18},{18,26},{... | collective-permute-start | bytes 1544 | tf_op jit(solution)/shard_map/ppermute | solution.py:10
  20.0 3.8 %copy-start.2 = (s32[128]{0:T(128)S(1)}, s32[128]{0:T(128)}, u32[]{:S(2)}) copy-start(s32[128]{0:T(128)} %param.13) | copy-start | bytes 1540
  23.9 23.6 %copy-start = (f32[4,128]{1,0:T(4,128)S(1)}, f32[4,128]{1,0:T(4,128)}, u32[]{:S(2)}) copy-start(f32[4,128]{1,0:T(4,128)} %param.12) | copy-start | bytes 6148
  40.7 10.0 %collective-permute-start = (bf16[128,512]{0,1:T(8,128)(2,1)S(1)}, bf16[128,512]{0,1:T(8,128)(2,1)S(1)}, u32[]{:S(2)}, u32[]{:S(2)}) collective-permute-start(bf16[128,512]{0,1:T(8,128)(2,1)S(1)} %get-tuple-element.6), channel_id=1, source_target_pairs={{0,8},{8,16},{16,24},{1,9},{9,17},{17,25},{2,10},{10,18},{18,26},{... | collective-permute-start | bytes 393224 | tf_op jit(solution)/shard_map/ppermute | solution.py:10
  43.8 6.4 %collective-permute-start.2 = (bf16[128,512]{0,1:T(8,128)(2,1)S(1)}, bf16[128,512]{0,1:T(8,128)(2,1)S(1)}, u32[]{:S(2)}, u32[]{:S(2)}) collective-permute-start(bf16[128,512]{0,1:T(8,128)(2,1)S(1)} %get-tuple-element.5), channel_id=1, source_target_pairs={{0,8},{8,16},{16,24},{1,9},{9,17},{17,25},{2,10},{10,18},{18,26},{... | collective-permute-start | bytes 393224 | tf_op jit(solution)/shard_map/ppermute | solution.py:10
  47.4 2.9 %copy-start.1 = (f32[4,128]{1,0:T(4,128)S(1)}, f32[4,128]{1,0:T(4,128)}, u32[]{:S(2)}) copy-start(f32[4,128]{1,0:T(4,128)} %param.11) | copy-start | bytes 6148
Sparse Core Ops, SparseCore 0:
  9.0 24.8 all-gather.1
  56.2 36.5 reduce-scatter.1
where the time goes:
time: 102 us; the launch traced here: 101 us
  waiting for transfers between devices  47.9 us (47%)
  matrix products  15.9 us (16%)
  between operations  13.6 us (13%)
  starting transfers between devices  11.5 us (11%)
  other arithmetic  9.86 us (10%)
  local copies, waits for them, and re-layouts  2.48 us (2%)
    reduce_scatter x1, waiting for transfers between devices, shards(): result = lax.psum_scatter(term, 'mp', scatter_dimension=1, tiled=True)  36.7 us
    ppermute x3, starting transfers between devices, passed_along(): lax.ppermute(value, axis, [(source, source + steps) for source in range(i...  11.5 us
    all_gather x1, waiting for transfers between devices, shards(): lax.all_gather(tokens, 'mp', axis=1, tiled=True)  9.96 us
    another operation x1, other arithmetic  7.77 us
    dot_general x1, matrix products, shards(): jnp.einsum('tf,cfw->ctw', lax.all_gather(tokens, 'mp', axis=1, tiled=True...  6.74 us
    dot_general x1, matrix products, shards(): term = jnp.dot(head_out, w_out, preferred_element_type=jnp.float32)  4.27 us
    dot_general x1, matrix products, shards(): jnp.dot(sinus_table(2 * seg_rows, full_width), w_pos, preferred_element_t...  3.43 us
  transfers between devices with their start and end apart: 5, of which 3 were waited for; matrix products, arithmetic and copies ran while one was open for 14% of the time, Pallas kernels for 0%

commit v1 on v0

v1 whole, which is shorter than its diff:
```python
import functools

import jax
import jax.numpy as jnp
from jax import lax
from jax.experimental import pallas as pl
from jax.experimental.pallas import tpu as pltpu
from jax.sharding import PartitionSpec as P

BF16 = jnp.bfloat16
F32 = jnp.float32
VMEM_LIMIT = 40 * 1024 * 1024


def vmem_spec():
    return pl.BlockSpec(memory_space=pltpu.VMEM)


def hbm_spec():
    return pl.BlockSpec(memory_space=pl.ANY)


def call(kernel, out_shape, in_specs, scratch, flops, nbytes, name, transcendentals=0):
    outs = jax.tree.map(lambda _: vmem_spec(), out_shape)
    return pl.pallas_call(
        kernel,
        out_shape=out_shape,
        in_specs=in_specs,
        out_specs=outs,
        scratch_shapes=scratch,
        compiler_params=pltpu.CompilerParams(vmem_limit_bytes=VMEM_LIMIT),
        cost_estimate=pl.CostEstimate(
            flops=flops, bytes_accessed=nbytes, transcendentals=transcendentals
        ),
        name=name,
    )


def dot(a, b):
    return jnp.dot(a, b, preferred_element_type=F32)


def dot_nt(a, b):
    return lax.dot_general(a, b, (((1,), (1,)), ((), ())), preferred_element_type=F32)


def rel_kernel(parts, w_ref, out_ref, wbuf, table, sems):
    rows, cols = out_ref.shape
    width = w_ref.shape[0]
    half = width // 2
    depth = width // parts

    def copy(i):
        return pltpu.make_async_copy(
            w_ref.at[pl.ds(i * depth, depth)], wbuf.at[pl.ds(i * depth, depth)], sems.at[i]
        )

    for i in range(parts):
        copy(i).start()
    fine = 16
    coarse = rows // fine
    index = lax.broadcasted_iota(jnp.int32, (1, half), 1).astype(F32) * 2.0
    freqs = 1.0 / 10000.0 ** (index / width)
    low = (fine - 1 - lax.broadcasted_iota(jnp.int32, (fine, half), 0)).astype(F32) * freqs
    high = (lax.broadcasted_iota(jnp.int32, (coarse, half), 0) * fine).astype(F32) * freqs
    sin_low, cos_low = jnp.sin(low), jnp.cos(low)
    sin_high, cos_high = jnp.sin(high), jnp.cos(high)
    for a in range(coarse):
        sh, ch = sin_high[a : a + 1], cos_high[a : a + 1]
        first = (coarse - 1 - a) * fine
        table[first : first + fine, :half] = (sh * cos_low + ch * sin_low).astype(BF16)
        table[first : first + fine, half:] = (ch * cos_low - sh * sin_low).astype(BF16)
    total = jnp.zeros((rows, cols), F32)
    for i in range(parts):
        copy(i).wait()
        total = total + dot(
            table[:, i * depth : (i + 1) * depth], wbuf[i * depth : (i + 1) * depth]
        )
    out_ref[...] = total.astype(BF16)


def rel_keys_reversed(w_pos, rows):
    width, cols = w_pos.shape
    parts = 8
    return call(
        functools.partial(rel_kernel, parts),
        jax.ShapeDtypeStruct((rows, cols), BF16),
        [hbm_spec()],
        [
            pltpu.VMEM((width, cols), BF16),
            pltpu.VMEM((rows, width), BF16),
            pltpu.SemaphoreType.DMA((parts,)),
        ],
        2 * rows * width * cols,
        2 * width * cols,
        "rel_keys",
        4 * 16 * width,
    )(w_pos)


def kv_kernel(first, last, place_ref, mine_ref, other_ref, w_ref, *refs):
    refs = list(refs)
    acc_ref = None if first else refs.pop(0)
    out_ref, wbuf, sems = refs
    depth = mine_ref.shape[1]
    rows = mine_ref.shape[0]

    def copy(i, c):
        start = pl.multiple_of(place_ref[i] * depth, depth)
        return pltpu.make_async_copy(
            w_ref.at[c + 1, pl.ds(start, depth)], wbuf.at[c, i], sems.at[c, i]
        )

    for c in range(2):
        for i in range(2):
            copy(i, c).start()
    for c in range(2):
        total = None if first else acc_ref[c]
        for i, x_ref in enumerate((mine_ref, other_ref)):
            copy(i, c).wait()
            term = dot(x_ref[...], wbuf[c, i])
            total = term if total is None else total + term
        out_ref[c] = total.astype(out_ref.dtype)


def kv_step(place, mine, other, w_qkv, acc, last):
    rows, depth = mine.shape
    cols = w_qkv.shape[2]
    first = acc is None
    args = [place, mine, other, w_qkv] + ([] if first else [acc])
    specs = [pl.BlockSpec(memory_space=pltpu.SMEM), vmem_spec(), vmem_spec(), hbm_spec()]
    specs += [] if first else [vmem_spec()]
    return call(
        functools.partial(kv_kernel, first, last),
        jax.ShapeDtypeStruct((2, rows, cols), BF16 if last else F32),
        specs,
        [pltpu.VMEM((2, 2, depth, cols), BF16), pltpu.SemaphoreType.DMA((2, 2))],
        8 * rows * depth * cols,
        8 * depth * cols,
        "kv_step",
    )(*args)


def q_kernel(count, place_ref, *refs):
    x_refs = refs[:count]
    w_ref, cb_ref, pb_ref, qc_ref, qp_ref, wbuf, sems = refs[count:]
    depth = x_refs[0].shape[1]

    def copy(i):
        start = pl.multiple_of(place_ref[i] * depth, depth)
        return pltpu.make_async_copy(w_ref.at[0, pl.ds(start, depth)], wbuf.at[i], sems.at[i])

    for i in range(count):
        copy(i).start()
    total = None
    for i in range(count):
        copy(i).wait()
        term = dot(x_refs[i][...], wbuf[i])
        total = term if total is None else total + term
    qc_ref[...] = (total + cb_ref[...]).astype(BF16)
    qp_ref[...] = (total + pb_ref[...]).astype(BF16)


def queries(places, chunks, w_qkv, content_bias, position_bias):
    count = len(chunks)
    rows, depth = chunks[0].shape
    cols = w_qkv.shape[2]
    out = jax.ShapeDtypeStruct((rows, cols), BF16)
    return call(
        functools.partial(q_kernel, count),
        (out, out),
        [pl.BlockSpec(memory_space=pltpu.SMEM)]
        + [vmem_spec()] * count
        + [hbm_spec(), vmem_spec(), vmem_spec()],
        [pltpu.VMEM((count, depth, cols), BF16), pltpu.SemaphoreType.DMA((count,))],
        2 * count * rows * depth * cols,
        2 * count * depth * cols,
        "queries",
    )(places, *chunks, w_qkv, content_bias.reshape(1, cols), position_bias.reshape(1, cols))


def attend_kernel(
    heads, blocks, place_ref, qc_ref, qp_ref, mem_ref, own_ref, rel_ref, qdoc_ref, kdoc_ref, w_ref,
    away_ref, keep_ref, wbuf, head_out, sems,
):
    rows = qc_ref.shape[0]
    head_dim = qc_ref.shape[1] // heads
    width = away_ref.shape[2]
    half = blocks // 2

    def copy(b):
        start = pl.multiple_of(place_ref[b] * width, width)
        return pltpu.make_async_copy(w_ref.at[:, pl.ds(start, width)], wbuf.at[b], sems.at[b])

    for b in range(blocks):
        copy(b).start()
    span = 2 * rows
    query = lax.broadcasted_iota(jnp.int32, (rows, span), 0)
    key = lax.broadcasted_iota(jnp.int32, (rows, span), 1)
    allowed = (key <= query + rows) & (kdoc_ref[...] == qdoc_ref[...])
    scale = 1.0 / (float(head_dim) ** 0.5)
    for h in range(heads):
        part = slice(h * head_dim, (h + 1) * head_dim)
        qc = qc_ref[:, part]
        content = jnp.concatenate(
            [dot_nt(qc, mem_ref[0, :, part]), dot_nt(qc, own_ref[0, :, part])], axis=1
        )
        pos = pltpu.roll(
            dot_nt(qp_ref[:, part], rel_ref[:, part]), rows + 1, 1, stride=1, stride_axis=0
        )
        score = jnp.where(allowed, (content + pos) * scale, -1e30)
        top = jnp.max(score, axis=1, keepdims=True)
        expo = jnp.where(allowed, jnp.exp(score - top), 0.0)
        weights = (expo / jnp.sum(expo, axis=1, keepdims=True)).astype(BF16)
        out = dot(weights[:, :rows], mem_ref[1, :, part])
        out = out + dot(weights[:, rows:], own_ref[1, :, part])
        head_out[:, part] = out.astype(BF16)
    for b in range(half):
        copy(b).wait()
        away_ref[b] = dot(head_out[...], wbuf[b]).astype(BF16)
    for b in range(half):
        copy(half + b).wait()
        keep_ref[b] = dot(head_out[...], wbuf[half + b])


def attend(places, query_content, query_pos, mem, own, rel, qdoc, kdoc, w_out, heads):
    rows, cols = query_content.shape
    blocks = places.shape[0]
    width = w_out.shape[1] // blocks
    half = blocks // 2
    return call(
        functools.partial(attend_kernel, heads, blocks),
        (
            jax.ShapeDtypeStruct((half, rows, width), BF16),
            jax.ShapeDtypeStruct((half, rows, width), F32),
        ),
        [pl.BlockSpec(memory_space=pltpu.SMEM)] + [vmem_spec()] * 7 + [hbm_spec()],
        [
            pltpu.VMEM((blocks, cols, width), BF16),
            pltpu.VMEM((rows, cols), BF16),
            pltpu.SemaphoreType.DMA((blocks,)),
        ],
        2 * rows * cols * w_out.shape[1] + 12 * rows * rows * cols,
        2 * cols * w_out.shape[1],
        "attend",
    )(places, query_content, query_pos, mem, own, rel, qdoc, kdoc, w_out)


def shards(tokens, w_qkv, w_pos, w_out, content_bias, position_bias, doc_ids):
    rows = tokens.shape[0]
    heads = content_bias.shape[0]
    count = lax.axis_size("mp")
    chips = count // 2
    segments = lax.axis_size("seq")
    me = lax.axis_index("mp")
    chip, core = me // 2, me % 2

    def across(value, k):
        return lax.ppermute(value, "mp", [(i, (i + 2 * k) % count) for i in range(count)])

    def swap(value):
        return lax.ppermute(value, "mp", [(i, i ^ 1) for i in range(count)])

    def onward(value):
        return lax.ppermute(value, "seq", [(i, i + 1) for i in range(segments - 1)])

    mine = [tokens] + [across(tokens, k) for k in range(1, chips)]
    other = [swap(chunk) for chunk in mine]
    mem_doc = onward(doc_ids)
    mem_doc = jnp.where(lax.axis_index("seq") > 0, mem_doc, -1)
    kdoc = jnp.concatenate([mem_doc, doc_ids]).reshape(1, 2 * rows)
    qdoc = doc_ids.reshape(rows, 1)
    rel = rel_keys_reversed(w_pos, 2 * rows)

    sources = [(chip - k) % chips for k in range(chips)]
    place = [jnp.stack([2 * s + core, 2 * s + 1 - core]) for s in sources]
    acc = None
    for k in range(chips):
        acc = kv_step(place[k], mine[k], other[k], w_qkv, acc, k == chips - 1)
    mem = onward(acc)
    query_content, query_pos = queries(
        jnp.concatenate(place),
        [chunk for pair in zip(mine, other) for chunk in pair],
        w_qkv,
        content_bias,
        position_bias,
    )
    targets = [(chip + k) % chips for k in range(chips)]
    columns = jnp.stack([2 * t + 1 - core for t in targets] + [2 * t + core for t in targets])
    away, keep = attend(
        columns, query_content, query_pos, mem, acc, rel, qdoc, kdoc, w_out, heads
    )
    total = keep + swap(away).astype(F32)
    result = total[0]
    for k in range(1, chips):
        result = result + across(total[k].astype(BF16), k).astype(F32)
    return result.astype(BF16)


def solution(mesh):
    in_specs = (
        P("seq", "mp"),
        P(None, None, "mp"),
        P(None, "mp"),
        P("mp", None),
        P("mp", None),
        P("mp", None),
        P("seq"),
    )
    out_specs = P("seq", "mp")
    return jax.shard_map(shards, mesh=mesh, in_specs=in_specs, out_specs=out_specs, check_vma=False)
```

time: 102 us -> 67.1 us (0.66)
  waiting for transfers between devices: 47.9 us -> 16.4 us
  Pallas kernels: 0 us -> 16.4 us
  matrix products: 15.9 us -> 0 us
  between operations: 13.6 us -> 0.3 us
  local copies, waits for them, and re-layouts: 2.48 us -> 12.5 us
  other arithmetic: 9.86 us -> 1.23 us
  starting transfers between devices: 11.5 us -> 20.1 us
    reduce_scatter x1 -> x0, waiting for transfers between devices: 36.7 us -> none  [shards(): result = lax.psum_scatter(term, 'mp', scatter_dimension=1, tiled=True)]
    pallas_call x0 -> x7, Pallas kernels: none -> 16.4 us  [the longest x4 5.89 us: kv_step(): call(functools.partial(kv_kernel, first, last), jax.ShapeDtypeStruct((2,...]
    dot_general x6 -> x0, matrix products: 15.9 us -> none  [the longest x1 6.74 us: shards(): jnp.einsum('tf,cfw->ctw', lax.all_gather(tokens, 'mp', axis=1, tiled=True...]
    ppermute x3 -> x13, waiting for transfers between devices: 0.46 us -> 16.4 us  [the longest x6 14.7 us: across(): lax.ppermute(value, 'mp', [(i, (i + 2 * k) % count) for i in range(count)])]
    unnamed x8 -> x16, local copies, waits for them, and re-layouts: 0.58 us -> 11.5 us
    all_gather x1 -> x0, waiting for transfers between devices: 9.96 us -> none  [shards(): lax.all_gather(tokens, 'mp', axis=1, tiled=True)]
    ppermute x3 -> x13, starting transfers between devices: 11.5 us -> 20.1 us  [the longest x6 12.4 us: across(): lax.ppermute(value, 'mp', [(i, (i + 2 * k) % count) for i in range(count)])]
    another operation x1 -> x5, other arithmetic: 7.77 us -> 0.49 us  [the longest x4 0.3 us: shards(): place = [jnp.stack([2 * s + core, 2 * s + 1 - core]) for s in sources]]
  transfers between devices with their start and end apart: 5 -> 13, of which waited for: 3 -> 6; matrix products, arithmetic and copies ran while one was open for 14% -> 2% of each run, Pallas kernels for 0% -> 17%
where the time goes in v1:
time: 67.1 us; the launch traced here: 66.8 us
  starting transfers between devices  20.1 us (30%)
  waiting for transfers between devices  16.4 us (24%)
  Pallas kernels  16.4 us (24%)
  local copies, waits for them, and re-layouts  12.5 us (19%)
  other arithmetic  1.23 us (2%)
    ppermute x6, waiting for transfers between devices, across(): lax.ppermute(value, 'mp', [(i, (i + 2 * k) % count) for i in range(count)])  14.7 us
    ppermute x6, starting transfers between devices, across(): lax.ppermute(value, 'mp', [(i, (i + 2 * k) % count) for i in range(count)])  12.4 us
    unnamed x16, local copies, waits for them, and re-layouts  11.5 us
    ppermute x2, starting transfers between devices, onward(): return lax.ppermute(value, 'seq', [(i, i + 1) for i in range(segments - 1)])  6.79 us
    pallas_call x4, Pallas kernels, kv_step(): call(functools.partial(kv_kernel, first, last), jax.ShapeDtypeStruct((2,...  5.89 us
    pallas_call x1, Pallas kernels, attend(): call(functools.partial(attend_kernel, heads, blocks), (jax.ShapeDtypeStru...  4.73 us
    pallas_call x1, Pallas kernels, rel_keys_reversed(): call(functools.partial(rel_kernel, parts), jax.ShapeDtypeStruct((rows, co...  3.73 us
    pallas_call x1, Pallas kernels, queries(): call(functools.partial(q_kernel, count), (out, out), [pl.BlockSpec(memory...  2.01 us
  transfers between devices with their start and end apart: 13, of which 6 were waited for; matrix products, arithmetic and copies ran while one was open for 2% of the time, Pallas kernels for 17%

profile of v1, /device:TPU:0, one launch (start us, length us, event | category | flops | bytes accessed | tf_op | source)
XLA Modules:
  0.0 66.8 jit_solution(6636635555043454332)
XLA Ops:
  0.0 5.0 %collective-permute-start.5 = (bf16[128,512]{1,0:T(8,128)(2,1)}, bf16[128,512]{1,0:T(8,128)(2,1)S(1)}, u32[]{:S(2)}, u32[]{:S(2)}) collective-permute-start(bf16[128,512]{1,0:T(8,128)(2,1)} %mine_ref.1), channel_id=1, source_target_pairs={{0,6},{1,7},{2,0},{3,1},{4,2},{5,3},{6,4},{7,5},{8,14},{9,15},{10,... | collective-permute-start | bytes 393224 | tf_op jit(solution)/shard_map/ppermute | solution.py:259
  5.1 1.0 %collective-permute-start.1 = (bf16[128,512]{1,0:T(8,128)(2,1)}, bf16[128,512]{1,0:T(8,128)(2,1)S(1)}, u32[]{:S(2)}, u32[]{:S(2)}) collective-permute-start(bf16[128,512]{1,0:T(8,128)(2,1)} %mine_ref.1), channel_id=1, source_target_pairs={{0,2},{1,3},{2,4},{3,5},{4,6},{5,7},{6,0},{7,1},{8,10},{9,11},{10,... | collective-permute-start | bytes 393224 | tf_op jit(solution)/shard_map/ppermute | solution.py:259
  6.1 3.4 %collective-permute-start.8 = (s32[128]{0:T(128)}, s32[128]{0:T(128)S(1)}, u32[]{:S(2)}, u32[]{:S(2)}) collective-permute-start(s32[128]{0:T(128)} %param.13), channel_id=1, source_target_pairs={{0,8},{8,16},{16,24},{1,9},{9,17},{17,25},{2,10},{10,18},{18,26},{... | collective-permute-start | bytes 1544 | tf_op jit(solution)/shard_map/ppermute | solution.py:265
  9.7 4.9 %collective-permute-done.1.refs_2_.mine_ref = bf16[128,512]{1,0:T(8,128)(2,1)S(1)} collective-permute-done((bf16[128,512]{1,0:T(8,128)(2,1)}, bf16[128,512]{1,0:T(8,128)(2,1)S(1)}, u32[]{:S(2)}, u32[]{:S(2)}) %collective-permute-start.1) | collective-permute-done | bytes 131104 | tf_op jit(solution)/shard_map/ppermute | solution.py:259
  14.8 0.8 %copy.8.qdoc_ref = s32[128,1]{1,0:T(8,128)S(1)} copy(s32[128,1]{0,1:T(1,128)} %bitcast.37) | data formatting | bytes 1024 | tf_op jit(solution)/shard_map/reshape | solution.py:272
  16.5 2.2 %copy-done.2 = bf16[4096,512]{1,0:T(8,128)(2,1)S(1)} copy-done((bf16[4096,512]{1,0:T(8,128)(2,1)S(1)}, bf16[4096,512]{1,0:T(8,128)(2,1)}, u32[]{:S(2)}) %copy-start.2) | copy-done | bytes 4194328
  18.7 3.7 %rel_keys.1.rel_ref = bf16[256,512]{1,0:T(8,128)(2,1)S(1)} custom-call(bf16[4096,512]{1,0:T(8,128)(2,1)S(1)} %copy-done.2), custom_call_target="tpu_custom_call" | custom-call | flops 1073741824 | bytes 4194304 | tf_op jit(solution)/shard_map/rel_keys/pallas_call | solution.py:85
  22.4 4.6 %copy-done = bf16[3,4096,512]{2,1,0:T(8,128)(2,1)S(1)} copy-done((bf16[3,4096,512]{2,1,0:T(8,128)(2,1)S(1)}, bf16[3,4096,512]{2,1,0:T(8,128)(2,1)}, u32[]{:S(2)}) %copy-start) | copy-done | bytes 12582936
  27.0 1.4 %kv_step.4.refs_0_ = f32[2,128,512]{2,1,0:T(8,128)S(1)} custom-call(s32[2]{0:T(128)S(1)} %pad_add_fusion.4.place_ref, bf16[128,512]{1,0:T(8,128)(2,1)S(1)} %copy-done.4, bf16[128,512]{1,0:T(8,128)(2,1)S(1)} %collective-permute-done.refs_1_.other_ref, bf16[3,4096,512]{2,1,0:T(8,128)(2,1)S(1)} %copy-done), custom_call_target="tpu_custom_call" | custom-call | flops 268435456 | bytes 2097152 | tf_op jit(solution)/shard_map/kv_step/pallas_call | solution.py:133
  28.5 1.5 %kv_step.5.refs_0_ = f32[2,128,512]{2,1,0:T(8,128)S(1)} custom-call(s32[2]{0:T(128)S(1)} %pad_add_fusion.3.place_ref, bf16[128,512]{1,0:T(8,128)(2,1)S(1)} %collective-permute-done.1.refs_2_.mine_ref, bf16[128,512]{1,0:T(8,128)(2,1)S(1)} %collective-permute-done.2.refs_3_.other_ref, bf16[3,4096,512]{2,1,0:T(8,128)(2,1)S(1)} %copy-done, ...), custom_call_target="tpu_custom_call" | custom-call | flops 268435456 | bytes 2097152 | tf_op jit(solution)/shard_map/kv_step/pallas_call | solution.py:133
  30.0 1.5 %kv_step.6.refs_0_ = f32[2,128,512]{2,1,0:T(8,128)S(1)} custom-call(s32[2]{0:T(128)S(1)} %pad_add_fusion.2.place_ref, bf16[128,512]{1,0:T(8,128)(2,1)S(1)} %collective-permute-done.3.refs_4_.mine_ref, bf16[128,512]{1,0:T(8,128)(2,1)S(1)} %collective-permute-done.4.refs_5_.other_ref, bf16[3,4096,512]{2,1,0:T(8,128)(2,1)S(1)} %copy-done, ...), custom_call_target="tpu_custom_call" | custom-call | flops 268435456 | bytes 2097152 | tf_op jit(solution)/shard_map/kv_step/pallas_call | solution.py:133
  31.5 1.5 %kv_step.7.own_ref = bf16[2,128,512]{2,1,0:T(8,128)(2,1)S(1)} custom-call(s32[2]{0:T(128)S(1)} %pad_add_fusion.1.place_ref, bf16[128,512]{1,0:T(8,128)(2,1)S(1)} %collective-permute-done.5.refs_6_.mine_ref, bf16[128,512]{1,0:T(8,128)(2,1)S(1)} %collective-permute-done.6.refs_7_.other_ref, bf16[3,4096,512]{2,1,0:T(8,128)(2,1)S(1)} %copy-done, ...), custom_call_target="tpu_custom_call" | custom-call | flops 268435456 | bytes 2097152 | tf_op jit(solution)/shard_map/kv_step/pallas_call | solution.py:133
  33.0 3.4 %collective-permute-start.7 = (bf16[2,128,512]{2,1,0:T(8,128)(2,1)S(1)}, bf16[2,128,512]{2,1,0:T(8,128)(2,1)S(1)}, u32[]{:S(2)}, u32[]{:S(2)}) collective-permute-start(bf16[2,128,512]{2,1,0:T(8,128)(2,1)S(1)} %kv_step.7.own_ref), channel_id=1, source_target_pairs={{0,8},{8,16},{16,24},{1,9},{9,17},{17,25},{2,10},{10,18},{18,26},{... | collective-permute-start | bytes 786440 | tf_op jit(solution)/shard_map/ppermute | solution.py:265
  36.5 4.6 %copy-done.1 = bf16[3,4096,512]{2,1,0:T(8,128)(2,1)S(1)} copy-done((bf16[3,4096,512]{2,1,0:T(8,128)(2,1)S(1)}, bf16[3,4096,512]{2,1,0:T(8,128)(2,1)}, u32[]{:S(2)}) %copy-start.1) | copy-done | bytes 12582936
  41.1 2.0 %queries.1 = (bf16[128,512]{1,0:T(8,128)(2,1)S(1)}, bf16[128,512]{1,0:T(8,128)(2,1)S(1)}) custom-call(s32[8]{0:T(128)S(1)} %concatenate.7.place_ref, bf16[128,512]{1,0:T(8,128)(2,1)S(1)} %copy-done.4, bf16[128,512]{1,0:T(8,128)(2,1)S(1)} %collective-permute-done.refs_1_.other_ref, bf16[128,512]{1,0:T(8,128)(2,1)S(1)} %collective-permute-done.1.refs_2_.mine_ref, ...), custom_call_target="tpu_custom_call" | custom-call | flops 536870912 | bytes 4194304 | tf_op jit(solution)/shard_map/queries/pallas_call | solution.py:169
  43.2 4.7 %attend.1 = (bf16[4,128,512]{2,1,0:T(8,128)(2,1)S(1)}, f32[4,128,512]{2,1,0:T(8,128)S(1)}) custom-call(s32[8]{0:T(128)S(1)} %stack.67.place_ref, bf16[128,512]{1,0:T(8,128)(2,1)S(1)} %get-tuple-element.9.qc_ref, bf16[128,512]{1,0:T(8,128)(2,1)S(1)} %get-tuple-element.10.qp_ref, bf16[2,128,512]{2,1,0:T(8,128)(2,1)S(1)} %collective-permute-done.7.mem_ref, ...), custom_call_target="tpu_custom_call" | custom-call | flops 637534208 | bytes 4194304 | tf_op jit(solution)/shard_map/attend/pallas_call | solution.py:231
  48.3 1.7 %collective-permute-done.9 = bf16[4,128,512]{2,1,0:T(8,128)(2,1)S(1)} collective-permute-done((bf16[4,128,512]{2,1,0:T(8,128)(2,1)S(1)}, bf16[4,128,512]{2,1,0:T(8,128)(2,1)S(1)}, u32[]{:S(2)}, u32[]{:S(2)}) %collective-permute-start.9) | collective-permute-done | bytes 524320 | tf_op jit(solution)/shard_map/ppermute | solution.py:262
  50.2 2.5 %collective-permute-start.10 = (bf16[128,512]{1,0:T(8,128)(2,1)S(1)}, bf16[128,512]{1,0:T(8,128)(2,1)S(1)}, u32[]{:S(2)}, u32[]{:S(2)}) collective-permute-start(bf16[128,512]{1,0:T(8,128)(2,1)S(1)} %get-tuple-element.15), channel_id=1, source_target_pairs={{0,2},{1,3},{2,4},{3,5},{4,6},{5,7},{6,0},{7,1},{8,10},{9,11},{10,... | collective-permute-start | bytes 393224 | tf_op jit(solution)/shard_map/ppermute | solution.py:259
  52.7 1.3 %collective-permute-start.12 = (bf16[128,512]{1,0:T(8,128)(2,1)S(1)}, bf16[128,512]{1,0:T(8,128)(2,1)S(1)}, u32[]{:S(2)}, u32[]{:S(2)}) collective-permute-start(bf16[128,512]{1,0:T(8,128)(2,1)S(1)} %get-tuple-element.16), channel_id=1, source_target_pairs={{0,6},{1,7},{2,0},{3,1},{4,2},{5,3},{6,4},{7,5},{8,14},{9,15},{10,... | collective-permute-start | bytes 393224 | tf_op jit(solution)/shard_map/ppermute | solution.py:259
  54.1 2.5 %collective-permute-start.11 = (bf16[128,512]{1,0:T(8,128)(2,1)S(1)}, bf16[128,512]{1,0:T(8,128)(2,1)S(1)}, u32[]{:S(2)}, u32[]{:S(2)}) collective-permute-start(bf16[128,512]{1,0:T(8,128)(2,1)S(1)} %get-tuple-element.17), channel_id=1, source_target_pairs={{0,4},{1,5},{2,6},{3,7},{4,0},{5,1},{6,2},{7,3},{8,12},{9,13},{10,... | collective-permute-start | bytes 393224 | tf_op jit(solution)/shard_map/ppermute | solution.py:259
  56.6 1.8 %collective-permute-done.10 = bf16[128,512]{1,0:T(8,128)(2,1)S(1)} collective-permute-done((bf16[128,512]{1,0:T(8,128)(2,1)S(1)}, bf16[128,512]{1,0:T(8,128)(2,1)S(1)}, u32[]{:S(2)}, u32[]{:S(2)}) %collective-permute-start.10) | collective-permute-done | bytes 131104 | tf_op jit(solution)/shard_map/ppermute | solution.py:259
  58.4 2.2 %collective-permute-done.12 = bf16[128,512]{1,0:T(8,128)(2,1)S(1)} collective-permute-done((bf16[128,512]{1,0:T(8,128)(2,1)S(1)}, bf16[128,512]{1,0:T(8,128)(2,1)S(1)}, u32[]{:S(2)}, u32[]{:S(2)}) %collective-permute-start.12) | collective-permute-done | bytes 131104 | tf_op jit(solution)/shard_map/ppermute | solution.py:259
  60.6 5.5 %collective-permute-done.11 = bf16[128,512]{1,0:T(8,128)(2,1)S(1)} collective-permute-done((bf16[128,512]{1,0:T(8,128)(2,1)S(1)}, bf16[128,512]{1,0:T(8,128)(2,1)S(1)}, u32[]{:S(2)}, u32[]{:S(2)}) %collective-permute-start.11) | collective-permute-done | bytes 131104 | tf_op jit(solution)/shard_map/ppermute | solution.py:259
  66.1 0.7 %fusion.3 = bf16[128,512]{1,0:T(8,128)(2,1)} fusion(f32[4,128,512]{2,1,0:T(8,128)S(1)} %get-tuple-element.14, bf16[128,512]{1,0:T(8,128)(2,1)S(1)} %collective-permute-done.12, bf16[128,512]{1,0:T(8,128)(2,1)S(1)} %collective-permute-done.11, bf16[128,512]{1,0:T(8,128)(2,1)S(1)} %collective-permute-done.10), kind=kLoop, calls=%fused_computation.5 | loop fusion | flops 458752 | bytes 786432 | tf_op jit(solution)/shard_map/convert_element_type | solution.py:297
  (37 shorter events, 2.0 us)
Async XLA Ops:
  0.0 22.4 %copy-start.4 = (bf16[128,512]{1,0:T(8,128)(2,1)S(1)}, bf16[128,512]{1,0:T(8,128)(2,1)}, u32[]{:S(2)}) copy-start(bf16[128,512]{1,0:T(8,128)(2,1)} %mine_ref.1) | copy-start | bytes 393220
  0.0 15.7 %collective-permute-start.5 = (bf16[128,512]{1,0:T(8,128)(2,1)}, bf16[128,512]{1,0:T(8,128)(2,1)S(1)}, u32[]{:S(2)}, u32[]{:S(2)}) collective-permute-start(bf16[128,512]{1,0:T(8,128)(2,1)} %mine_ref.1), channel_id=1, source_target_pairs={{0,6},{1,7},{2,0},{3,1},{4,2},{5,3},{6,4},{7,5},{8,14},{9,15},{10,... | collective-permute-start | bytes 393224 | tf_op jit(solution)/shard_map/ppermute | solution.py:259
  5.1 11.4 %collective-permute-start.3 = (bf16[128,512]{1,0:T(8,128)(2,1)}, bf16[128,512]{1,0:T(8,128)(2,1)S(1)}, u32[]{:S(2)}, u32[]{:S(2)}) collective-permute-start(bf16[128,512]{1,0:T(8,128)(2,1)} %mine_ref.1), channel_id=1, source_target_pairs={{0,4},{1,5},{2,6},{3,7},{4,0},{5,1},{6,2},{7,3},{8,12},{9,13},{10,... | collective-permute-start | bytes 393224 | tf_op jit(solution)/shard_map/ppermute | solution.py:259
  5.1 9.6 %collective-permute-start.1 = (bf16[128,512]{1,0:T(8,128)(2,1)}, bf16[128,512]{1,0:T(8,128)(2,1)S(1)}, u32[]{:S(2)}, u32[]{:S(2)}) collective-permute-start(bf16[128,512]{1,0:T(8,128)(2,1)} %mine_ref.1), channel_id=1, source_target_pairs={{0,2},{1,3},{2,4},{3,5},{4,6},{5,7},{6,0},{7,1},{8,10},{9,11},{10,... | collective-permute-start | bytes 393224 | tf_op jit(solution)/shard_map/ppermute | solution.py:259
  6.1 16.3 %collective-permute-start = (bf16[128,512]{1,0:T(8,128)(2,1)}, bf16[128,512]{1,0:T(8,128)(2,1)S(1)}, u32[]{:S(2)}, u32[]{:S(2)}) collective-permute-start(bf16[128,512]{1,0:T(8,128)(2,1)} %mine_ref.1), channel_id=1, source_target_pairs={{0,1},{1,0},{2,3},{3,2},{4,5},{5,4},{6,7},{7,6},{8,9},{9,8},{10,11... | collective-permute-start | bytes 393224 | tf_op jit(solution)/shard_map/ppermute | solution.py:262
  6.1 30.3 %collective-permute-start.8 = (s32[128]{0:T(128)}, s32[128]{0:T(128)S(1)}, u32[]{:S(2)}, u32[]{:S(2)}) collective-permute-start(s32[128]{0:T(128)} %param.13), channel_id=1, source_target_pairs={{0,8},{8,16},{16,24},{1,9},{9,17},{17,25},{2,10},{10,18},{18,26},{... | collective-permute-start | bytes 1544 | tf_op jit(solution)/shard_map/ppermute | solution.py:265
  14.6 13.8 %collective-permute-start.2 = (bf16[128,512]{1,0:T(8,128)(2,1)S(1)}, bf16[128,512]{1,0:T(8,128)(2,1)S(1)}, u32[]{:S(2)}, u32[]{:S(2)}) collective-permute-start(bf16[128,512]{1,0:T(8,128)(2,1)S(1)} %collective-permute-done.1.refs_2_.mine_ref), channel_id=1, source_target_pairs={{0,1},{1,0},{2,3},{3,2},{4,5},{5,4},{6,7},{7,6},{8,9},{9,8},{10,11... | collective-permute-start | bytes 393224 | tf_op jit(solution)/shard_map/ppermute | solution.py:262
  15.7 15.8 %collective-permute-start.6 = (bf16[128,512]{1,0:T(8,128)(2,1)S(1)}, bf16[128,512]{1,0:T(8,128)(2,1)S(1)}, u32[]{:S(2)}, u32[]{:S(2)}) collective-permute-start(bf16[128,512]{1,0:T(8,128)(2,1)S(1)} %collective-permute-done.5.refs_6_.mine_ref), channel_id=1, source_target_pairs={{0,1},{1,0},{2,3},{3,2},{4,5},{5,4},{6,7},{7,6},{8,9},{9,8},{10,11... | collective-permute-start | bytes 393224 | tf_op jit(solution)/shard_map/ppermute | solution.py:262
  16.5 13.5 %collective-permute-start.4 = (bf16[128,512]{1,0:T(8,128)(2,1)S(1)}, bf16[128,512]{1,0:T(8,128)(2,1)S(1)}, u32[]{:S(2)}, u32[]{:S(2)}) collective-permute-start(bf16[128,512]{1,0:T(8,128)(2,1)S(1)} %collective-permute-done.3.refs_4_.mine_ref), channel_id=1, source_target_pairs={{0,1},{1,0},{2,3},{3,2},{4,5},{5,4},{6,7},{7,6},{8,9},{9,8},{10,11... | collective-permute-start | bytes 393224 | tf_op jit(solution)/shard_map/ppermute | solution.py:262
  16.5 2.2 %copy-start.2 = (bf16[4096,512]{1,0:T(8,128)(2,1)S(1)}, bf16[4096,512]{1,0:T(8,128)(2,1)}, u32[]{:S(2)}) copy-start(bf16[4096,512]{1,0:T(8,128)(2,1)} %w_ref.10) | copy-start | bytes 12582916
  22.4 4.6 %copy-start = (bf16[3,4096,512]{2,1,0:T(8,128)(2,1)S(1)}, bf16[3,4096,512]{2,1,0:T(8,128)(2,1)}, u32[]{:S(2)}) copy-start(bf16[3,4096,512]{2,1,0:T(8,128)(2,1)} %w_ref.9) | copy-start | bytes 37748740
  31.4 5.0 %copy-start.7 = (s32[128]{0:T(128)S(1)}, s32[128]{0:T(128)}, u32[]{:S(2)}) copy-start(s32[128]{0:T(128)} %param.13) | copy-start | bytes 1540
  31.5 5.0 %copy-start.5 = (f32[4,128]{1,0:T(4,128)S(1)}, f32[4,128]{1,0:T(4,128)}, u32[]{:S(2)}) copy-start(f32[4,128]{1,0:T(4,128)} %param.11) | copy-start | bytes 6148
  31.5 5.0 %copy-start.6 = (f32[4,128]{1,0:T(4,128)S(1)}, f32[4,128]{1,0:T(4,128)}, u32[]{:S(2)}) copy-start(f32[4,128]{1,0:T(4,128)} %param.12) | copy-start | bytes 6148
  33.0 10.1 %collective-permute-start.7 = (bf16[2,128,512]{2,1,0:T(8,128)(2,1)S(1)}, bf16[2,128,512]{2,1,0:T(8,128)(2,1)S(1)}, u32[]{:S(2)}, u32[]{:S(2)}) collective-permute-start(bf16[2,128,512]{2,1,0:T(8,128)(2,1)S(1)} %kv_step.7.own_ref), channel_id=1, source_target_pairs={{0,8},{8,16},{16,24},{1,9},{9,17},{17,25},{2,10},{10,18},{18,26},{... | collective-permute-start | bytes 786440 | tf_op jit(solution)/shard_map/ppermute | solution.py:265
  36.5 4.6 %copy-start.1 = (bf16[3,4096,512]{2,1,0:T(8,128)(2,1)S(1)}, bf16[3,4096,512]{2,1,0:T(8,128)(2,1)}, u32[]{:S(2)}) copy-start(bf16[3,4096,512]{2,1,0:T(8,128)(2,1)} %w_ref.9) | copy-start | bytes 37748740
  41.0 2.2 %copy-start.3 = (bf16[512,4096]{1,0:T(8,128)(2,1)S(1)}, bf16[512,4096]{1,0:T(8,128)(2,1)}, u32[]{:S(2)}) copy-start(bf16[512,4096]{1,0:T(8,128)(2,1)} %w_ref.11) | copy-start | bytes 12582916
  48.0 2.0 %collective-permute-start.9 = (bf16[4,128,512]{2,1,0:T(8,128)(2,1)S(1)}, bf16[4,128,512]{2,1,0:T(8,128)(2,1)S(1)}, u32[]{:S(2)}, u32[]{:S(2)}) collective-permute-start(bf16[4,128,512]{2,1,0:T(8,128)(2,1)S(1)} %get-tuple-element.12), channel_id=1, source_target_pairs={{0,1},{1,0},{2,3},{3,2},{4,5},{5,4},{6,7},{7,6},{8,9},{9,8},{10,11... | collective-permute-start | bytes 1572872 | tf_op jit(solution)/shard_map/ppermute | solution.py:262
  50.2 8.2 %collective-permute-start.10 = (bf16[128,512]{1,0:T(8,128)(2,1)S(1)}, bf16[128,512]{1,0:T(8,128)(2,1)S(1)}, u32[]{:S(2)}, u32[]{:S(2)}) collective-permute-start(bf16[128,512]{1,0:T(8,128)(2,1)S(1)} %get-tuple-element.15), channel_id=1, source_target_pairs={{0,2},{1,3},{2,4},{3,5},{4,6},{5,7},{6,0},{7,1},{8,10},{9,11},{10,... | collective-permute-start | bytes 393224 | tf_op jit(solution)/shard_map/ppermute | solution.py:259
  52.7 7.9 %collective-permute-start.12 = (bf16[128,512]{1,0:T(8,128)(2,1)S(1)}, bf16[128,512]{1,0:T(8,128)(2,1)S(1)}, u32[]{:S(2)}, u32[]{:S(2)}) collective-permute-start(bf16[128,512]{1,0:T(8,128)(2,1)S(1)} %get-tuple-element.16), channel_id=1, source_target_pairs={{0,6},{1,7},{2,0},{3,1},{4,2},{5,3},{6,4},{7,5},{8,14},{9,15},{10,... | collective-permute-start | bytes 393224 | tf_op jit(solution)/shard_map/ppermute | solution.py:259
  54.1 12.1 %collective-permute-start.11 = (bf16[128,512]{1,0:T(8,128)(2,1)S(1)}, bf16[128,512]{1,0:T(8,128)(2,1)S(1)}, u32[]{:S(2)}, u32[]{:S(2)}) collective-permute-start(bf16[128,512]{1,0:T(8,128)(2,1)S(1)} %get-tuple-element.17), channel_id=1, source_target_pairs={{0,4},{1,5},{2,6},{3,7},{4,0},{5,1},{6,2},{7,3},{8,12},{9,13},{10,... | collective-permute-start | bytes 393224 | tf_op jit(solution)/shard_map/ppermute | solution.py:259

commit v2 on v1

v2 whole, which is shorter than its diff:
```python
import functools

import jax
import jax.numpy as jnp
from jax import lax
from jax.experimental import pallas as pl
from jax.experimental.pallas import tpu as pltpu
from jax.sharding import PartitionSpec as P

BF16 = jnp.bfloat16
F32 = jnp.float32
VMEM_LIMIT = 24 * 1024 * 1024


def vmem_spec():
    return pl.BlockSpec(memory_space=pltpu.VMEM)


def hbm_spec():
    return pl.BlockSpec(memory_space=pl.ANY)


def in_hbm(value):
    return pltpu.with_memory_space_constraint(value, pltpu.HBM)


def call(kernel, out_shape, in_specs, scratch, flops, nbytes, name, transcendentals=0):
    outs = jax.tree.map(lambda _: vmem_spec(), out_shape)
    return pl.pallas_call(
        kernel,
        out_shape=out_shape,
        in_specs=in_specs,
        out_specs=outs,
        scratch_shapes=scratch,
        compiler_params=pltpu.CompilerParams(vmem_limit_bytes=VMEM_LIMIT),
        cost_estimate=pl.CostEstimate(
            flops=flops, bytes_accessed=nbytes, transcendentals=transcendentals
        ),
        name=name,
    )


def dot(a, b):
    return jnp.dot(a, b, preferred_element_type=F32)


def dot_nt(a, b):
    return lax.dot_general(a, b, (((1,), (1,)), ((), ())), preferred_element_type=F32)


def load_kernel(parts, w_pos, w_qkv, w_out, rel_ref, qkv_ref, out_ref, wbuf, table, sems):
    rows, cols = rel_ref.shape
    width = w_pos.shape[0]
    half = width // 2
    depth = width // parts

    def pos_copy(i):
        part = pl.ds(i * depth, depth)
        return pltpu.make_async_copy(w_pos.at[part], wbuf.at[part], sems.at[i])

    copies = [pos_copy(i) for i in range(parts)]
    for c in (1, 2, 0):
        copies.append(pltpu.make_async_copy(w_qkv.at[c], qkv_ref.at[c], sems.at[parts + c]))
    copies.append(pltpu.make_async_copy(w_out, out_ref, sems.at[parts + 3]))
    for item in copies:
        item.start()
    fine = 16
    coarse = rows // fine
    index = lax.broadcasted_iota(jnp.int32, (1, half), 1).astype(F32) * 2.0
    freqs = 1.0 / 10000.0 ** (index / width)
    low = (fine - 1 - lax.broadcasted_iota(jnp.int32, (fine, half), 0)).astype(F32) * freqs
    high = (lax.broadcasted_iota(jnp.int32, (coarse, half), 0) * fine).astype(F32) * freqs
    sin_low, cos_low = jnp.sin(low), jnp.cos(low)
    sin_high, cos_high = jnp.sin(high), jnp.cos(high)
    for a in range(coarse):
        sh, ch = sin_high[a : a + 1], cos_high[a : a + 1]
        first = (coarse - 1 - a) * fine
        table[first : first + fine, :half] = (sh * cos_low + ch * sin_low).astype(BF16)
        table[first : first + fine, half:] = (ch * cos_low - sh * sin_low).astype(BF16)
    total = jnp.zeros((rows, cols), F32)
    for i in range(parts):
        copies[i].wait()
        total = total + dot(
            table[:, i * depth : (i + 1) * depth], wbuf[i * depth : (i + 1) * depth]
        )
    rel_ref[...] = total.astype(BF16)
    for item in copies[parts:]:
        item.wait()


def load(w_pos, w_qkv, w_out, rows):
    width, cols = w_pos.shape
    parts = 8
    return call(
        functools.partial(load_kernel, parts),
        (
            pltpu.VMEM((rows, cols), BF16),
            pltpu.VMEM(w_qkv.shape, BF16),
            pltpu.VMEM(w_out.shape, BF16),
        ),
        [hbm_spec()] * 3,
        [
            pltpu.VMEM((width, cols), BF16),
            pltpu.VMEM((rows, width), BF16),
            pltpu.SemaphoreType.DMA((parts + 4,)),
        ],
        2 * rows * width * cols,
        20 * width * cols,
        "load",
        4 * 16 * width,
    )(in_hbm(w_pos), in_hbm(w_qkv), in_hbm(w_out))


def kv_kernel(first, last, back, mine_ref, other_ref, w_ref, *refs):
    refs = list(refs)
    acc_ref = None if first else refs.pop(0)
    doc_ref = refs.pop(0) if last else None
    (out_ref,) = refs
    rows, depth = mine_ref.shape
    core, place = here(back)
    for c in range(2):
        total = None if first else acc_ref[c]
        for i, x_ref in enumerate((mine_ref, other_ref)):
            start = pl.multiple_of(row_block(core, place, i) * depth, depth)
            term = dot(x_ref[...], w_ref[c + 1, pl.ds(start, depth)])
            total = term if total is None else total + term
        if last:
            out_ref[c * rows : (c + 1) * rows] = total.astype(BF16)
        else:
            out_ref[c] = total
    if last:
        out_ref[2 * rows :] = jnp.zeros((16, out_ref.shape[1]), BF16)
        out_ref[2 * rows :, :rows] = jnp.broadcast_to(doc_ref[...], (16, rows)).astype(BF16)


def here(back):
    me = lax.axis_index("mp")
    chips = lax.axis_size("mp") // 2
    return lax.rem(me, 2), lax.rem(me // 2 + chips - back, chips)


def row_block(core, place, i):
    return 2 * place + (core if i == 0 else 1 - core)


def kv_step(back, mine, other, w_qkv, acc, docs):
    rows, depth = mine.shape
    cols = w_qkv.shape[2]
    first, last = acc is None, docs is not None
    args = [mine, other, w_qkv] + ([] if first else [acc]) + ([docs] if last else [])
    out = pltpu.VMEM((2 * rows + 16, cols), BF16) if last else pltpu.VMEM((2, rows, cols), F32)
    return call(
        functools.partial(kv_kernel, first, last, back),
        out,
        [vmem_spec()] * len(args),
        [],
        8 * rows * depth * cols,
        8 * depth * cols,
        "kv_step",
    )(*args)


def q_kernel(count, *refs):
    x_refs = refs[:count]
    w_ref, cb_ref, pb_ref, qc_ref, qp_ref = refs[count:]
    depth = x_refs[0].shape[1]
    total = None
    for i in range(count):
        core, place = here(i // 2)
        start = pl.multiple_of(row_block(core, place, i % 2) * depth, depth)
        term = dot(x_refs[i][...], w_ref[0, pl.ds(start, depth)])
        total = term if total is None else total + term
    qc_ref[...] = (total + cb_ref[...]).astype(BF16)
    qp_ref[...] = (total + pb_ref[...]).astype(BF16)


def queries(chunks, w_qkv, content_bias, position_bias):
    count = len(chunks)
    rows, depth = chunks[0].shape
    cols = w_qkv.shape[2]
    out = pltpu.VMEM((rows, cols), BF16)
    return call(
        functools.partial(q_kernel, count),
        (out, out),
        [vmem_spec()] * (count + 3),
        [],
        2 * count * rows * depth * cols,
        2 * count * depth * cols,
        "queries",
    )(*chunks, w_qkv, content_bias.reshape(1, cols), position_bias.reshape(1, cols))


def attend_kernel(
    heads, qc_ref, qp_ref, mem_ref, own_ref, rel_ref, doc_ref, w_ref, away_ref, keep_ref, head_out
):
    rows = qc_ref.shape[0]
    head_dim = qc_ref.shape[1] // heads
    chips, _, width = away_ref.shape
    span = 2 * rows
    query = lax.broadcasted_iota(jnp.int32, (rows, span), 0)
    key = lax.broadcasted_iota(jnp.int32, (rows, span), 1)
    own_doc = jnp.broadcast_to(doc_ref[...], (rows, rows))
    mem_doc = jnp.broadcast_to(mem_ref[2 * rows : 2 * rows + 1, :rows].astype(F32), (rows, rows))
    query_doc = own_doc.T
    same = jnp.concatenate([mem_doc, own_doc], axis=1) == jnp.concatenate(
        [query_doc, query_doc], axis=1
    )
    allowed = (key <= query + rows) & same
    scale = 1.0 / (float(head_dim) ** 0.5)
    for h in range(heads):
        part = slice(h * head_dim, (h + 1) * head_dim)
        qc = qc_ref[:, part]
        content = jnp.concatenate(
            [dot_nt(qc, mem_ref[:rows, part]), dot_nt(qc, own_ref[:rows, part])], axis=1
        )
        pos = pltpu.roll(
            dot_nt(qp_ref[:, part], rel_ref[:, part]), rows + 1, 1, stride=1, stride_axis=0
        )
        score = jnp.where(allowed, (content + pos) * scale, -1e30)
        top = jnp.max(score, axis=1, keepdims=True)
        expo = jnp.where(allowed, jnp.exp(score - top), 0.0)
        weights = (expo / jnp.sum(expo, axis=1, keepdims=True)).astype(BF16)
        out = dot(weights[:, :rows], mem_ref[rows:span, part])
        out = out + dot(weights[:, rows:], own_ref[rows:span, part])
        head_out[:, part] = out.astype(BF16)
    core, chip = here(0)
    for away in (True, False):
        for k in range(chips):
            block = 2 * lax.rem(chip + k, chips) + (1 - core if away else core)
            start = pl.multiple_of(block * width, width)
            term = dot(head_out[...], w_ref[:, pl.ds(start, width)])
            if away:
                away_ref[k] = term.astype(BF16)
            else:
                keep_ref[k] = term


def attend(query_content, query_pos, mem, own, rel, docs, w_out, heads, count):
    rows, cols = query_content.shape
    width = w_out.shape[1] // count
    half = count // 2
    return call(
        functools.partial(attend_kernel, heads),
        (pltpu.VMEM((half, rows, width), BF16), pltpu.VMEM((half, rows, width), F32)),
        [vmem_spec()] * 7,
        [pltpu.VMEM((rows, cols), BF16)],
        2 * rows * cols * w_out.shape[1] + 12 * rows * rows * cols,
        2 * cols * w_out.shape[1],
        "attend",
    )(query_content, query_pos, mem, own, rel, docs, w_out)


def shards(tokens, w_qkv, w_pos, w_out, content_bias, position_bias, doc_ids):
    rows = tokens.shape[0]
    heads = content_bias.shape[0]
    count = lax.axis_size("mp")
    chips = count // 2
    segments = lax.axis_size("seq")

    def across(value, k):
        return lax.ppermute(value, "mp", [(i, (i + 2 * k) % count) for i in range(count)])

    def swap(value):
        return lax.ppermute(value, "mp", [(i, i ^ 1) for i in range(count)])

    def onward(value):
        return lax.ppermute(value, "seq", [(i, i + 1) for i in range(segments - 1)])

    mine = [tokens] + [across(tokens, k) for k in range(1, chips)]
    other = [swap(chunk) for chunk in mine]
    docs = (doc_ids + 1).astype(F32).reshape(1, rows)
    rel, w_qkv, w_out = load(w_pos, w_qkv, w_out, 2 * rows)
    own = None
    for k in range(chips):
        own = kv_step(k, mine[k], other[k], w_qkv, own, docs if k == chips - 1 else None)
    mem = onward(own)
    query_content, query_pos = queries(
        [chunk for pair in zip(mine, other) for chunk in pair], w_qkv, content_bias, position_bias
    )
    away, keep = attend(
        query_content, query_pos, mem, own, rel, docs, w_out, heads, count
    )
    total = keep + swap(away).astype(F32)
    result = total[0]
    for k in range(1, chips):
        result = result + across(total[k].astype(BF16), k).astype(F32)
    return result.astype(BF16)


def solution(mesh):
    in_specs = (
        P("seq", "mp"),
        P(None, None, "mp"),
        P(None, "mp"),
        P("mp", None),
        P("mp", None),
        P("mp", None),
        P("seq"),
    )
    out_specs = P("seq", "mp")
    return jax.shard_map(shards, mesh=mesh, in_specs=in_specs, out_specs=out_specs, check_vma=False)
```

time: 67.1 us -> 54.8 us (0.82)
  local copies, waits for them, and re-layouts: 12.5 us -> 0.04 us
  waiting for transfers between devices: 16.4 us -> 23.3 us
  Pallas kernels: 16.4 us -> 12.1 us
  starting transfers between devices: 20.1 us -> 16.7 us
    unnamed x16 -> x6, local copies, waits for them, and re-layouts: 11.5 us -> 0.02 us
    ppermute x2 -> x1, waiting for transfers between devices: 0.01 us -> 5.3 us  [onward(): return lax.ppermute(value, 'seq', [(i, i + 1) for i in range(segments - 1)])]
    pallas_call x7, Pallas kernels: 16.4 us -> 12.1 us  [the longest x1 7.16 us: load(): call(functools.partial(load_kernel, parts), (pltpu.VMEM((rows, cols), BF1...]
    ppermute x2 -> x1, starting transfers between devices: 6.79 us -> 3.4 us  [onward(): return lax.ppermute(value, 'seq', [(i, i + 1) for i in range(segments - 1)])]
    ppermute x6, waiting for transfers between devices: 14.7 us -> 16.1 us  [across(): lax.ppermute(value, 'mp', [(i, (i + 2 * k) % count) for i in range(count)])]
    reshape x1 -> x0, local copies, waits for them, and re-layouts: 0.76 us -> none  [shards(): qdoc = doc_ids.reshape(rows, 1)]
  transfers between devices with their start and end apart: 13 -> 12, of which waited for: 6 -> 7; matrix products, arithmetic and copies ran while one was open for 2% -> 1% of each run, Pallas kernels for 17% -> 17%
where the time goes in v2:
time: 54.8 us; the launch traced here: 53.9 us
  waiting for transfers between devices  23.3 us (43%)
  starting transfers between devices  16.7 us (30%)
  Pallas kernels  12.1 us (22%)
  other arithmetic  1.59 us (3%)
    ppermute x6, waiting for transfers between devices, across(): lax.ppermute(value, 'mp', [(i, (i + 2 * k) % count) for i in range(count)])  16.1 us
    ppermute x6, starting transfers between devices, across(): lax.ppermute(value, 'mp', [(i, (i + 2 * k) % count) for i in range(count)])  12.7 us
    pallas_call x1, Pallas kernels, load(): call(functools.partial(load_kernel, parts), (pltpu.VMEM((rows, cols), BF1...  7.16 us
    ppermute x1, waiting for transfers between devices, onward(): return lax.ppermute(value, 'seq', [(i, i + 1) for i in range(segments - 1)])  5.3 us
    ppermute x1, starting transfers between devices, onward(): return lax.ppermute(value, 'seq', [(i, i + 1) for i in range(segments - 1)])  3.4 us
    pallas_call x1, Pallas kernels, attend(): call(functools.partial(attend_kernel, heads), (pltpu.VMEM((half, rows, wi...  2.32 us
    ppermute x5, waiting for transfers between devices, swap(): return lax.ppermute(value, 'mp', [(i, i ^ 1) for i in range(count)])  1.91 us
    pallas_call x4, Pallas kernels, kv_step(): call(functools.partial(kv_kernel, first, last, back), out, [vmem_spec()]...  1.85 us
  transfers between devices with their start and end apart: 12, of which 7 were waited for; matrix products, arithmetic and copies ran while one was open for 1% of the time, Pallas kernels for 17%

profile of v2, /device:TPU:0, one launch (start us, length us, event | category | flops | bytes accessed | tf_op | source)
XLA Modules:
  0.0 53.9 jit_solution(10751837410006077276)
XLA Ops:
  0.0 3.0 %collective-permute-start.1 = (bf16[128,512]{1,0:T(8,128)(2,1)}, bf16[128,512]{1,0:T(8,128)(2,1)S(1)}, u32[]{:S(2)}, u32[]{:S(2)}) collective-permute-start(bf16[128,512]{1,0:T(8,128)(2,1)} %mine_ref.1), channel_id=1, source_target_pairs={{0,2},{1,3},{2,4},{3,5},{4,6},{5,7},{6,0},{7,1},{8,10},{9,11},{10,... | collective-permute-start | bytes 393224 | tf_op jit(solution)/shard_map/ppermute | solution.py:261
  3.0 2.6 %collective-permute-start.3 = (bf16[128,512]{1,0:T(8,128)(2,1)}, bf16[128,512]{1,0:T(8,128)(2,1)S(1)}, u32[]{:S(2)}, u32[]{:S(2)}) collective-permute-start(bf16[128,512]{1,0:T(8,128)(2,1)} %mine_ref.1), channel_id=1, source_target_pairs={{0,4},{1,5},{2,6},{3,7},{4,0},{5,1},{6,2},{7,3},{8,12},{9,13},{10,... | collective-permute-start | bytes 393224 | tf_op jit(solution)/shard_map/ppermute | solution.py:261
  5.6 1.3 %collective-permute-start.5 = (bf16[128,512]{1,0:T(8,128)(2,1)}, bf16[128,512]{1,0:T(8,128)(2,1)S(1)}, u32[]{:S(2)}, u32[]{:S(2)}) collective-permute-start(bf16[128,512]{1,0:T(8,128)(2,1)} %mine_ref.1), channel_id=1, source_target_pairs={{0,6},{1,7},{2,0},{3,1},{4,2},{5,3},{6,4},{7,5},{8,14},{9,15},{10,... | collective-permute-start | bytes 393224 | tf_op jit(solution)/shard_map/ppermute | solution.py:261
  7.0 2.3 %collective-permute-done.1.refs_2_.mine_ref = bf16[128,512]{1,0:T(8,128)(2,1)S(1)} collective-permute-done((bf16[128,512]{1,0:T(8,128)(2,1)}, bf16[128,512]{1,0:T(8,128)(2,1)S(1)}, u32[]{:S(2)}, u32[]{:S(2)}) %collective-permute-start.1) | collective-permute-done | bytes 131104 | tf_op jit(solution)/shard_map/ppermute | solution.py:261
  9.3 0.7 %convert_bitcast_fusion.refs_1_.doc_ref = f32[1,128]{1,0:T(1,128)S(1)} fusion(s32[128]{0:T(128)} %param.13), kind=kLoop, calls=%fused_computation.9 | loop fusion | flops 256 | bytes 1024 | tf_op jit(solution)/shard_map/reshape | solution.py:271
  10.0 4.5 %collective-permute-done.3.refs_4_.mine_ref = bf16[128,512]{1,0:T(8,128)(2,1)S(1)} collective-permute-done((bf16[128,512]{1,0:T(8,128)(2,1)}, bf16[128,512]{1,0:T(8,128)(2,1)S(1)}, u32[]{:S(2)}, u32[]{:S(2)}) %collective-permute-start.3) | collective-permute-done | bytes 131104 | tf_op jit(solution)/shard_map/ppermute | solution.py:261
  14.5 0.5 collective-permute-start.6
  15.0 7.2 %load.1 = (bf16[256,512]{1,0:T(8,128)(2,1)S(1)}, bf16[3,4096,512]{2,1,0:T(8,128)(2,1)S(1)}, bf16[512,4096]{1,0:T(8,128)(2,1)S(1)}) custom-call(bf16[4096,512]{1,0:T(8,128)(2,1)} %w_pos.1, bf16[3,4096,512]{2,1,0:T(8,128)(2,1)} %w_qkv.1, bf16[512,4096]{1,0:T(8,128)(2,1)} %w_out.1), custom_call_target="tpu_custom_call" | custom-call | flops 1073741824 | bytes 41943040 | tf_op jit(solution)/shard_map/load/pallas_call | solution.py:94
  22.2 0.5 kv_step.4.refs_0_
  22.7 0.5 kv_step.5.refs_0_
  23.2 0.5 kv_step.6.refs_0_
  23.7 0.5 kv_step.7.own_ref
  24.1 3.4 %collective-permute-start.7 = (bf16[272,512]{1,0:T(8,128)(2,1)S(1)}, bf16[272,512]{1,0:T(8,128)(2,1)S(1)}, u32[]{:S(2)}, u32[]{:S(2)}) collective-permute-start(bf16[272,512]{1,0:T(8,128)(2,1)S(1)} %kv_step.7.own_ref), channel_id=1, source_target_pairs={{0,8},{8,16},{16,24},{1,9},{9,17},{17,25},{2,10},{10,18},{18,26},{... | collective-permute-start | bytes 835592 | tf_op jit(solution)/shard_map/ppermute | solution.py:267
  27.6 0.7 %queries.1 = (bf16[128,512]{1,0:T(8,128)(2,1)S(1)}, bf16[128,512]{1,0:T(8,128)(2,1)S(1)}) custom-call(bf16[128,512]{1,0:T(8,128)(2,1)S(1)} %copy-done, bf16[128,512]{1,0:T(8,128)(2,1)S(1)} %collective-permute-done.refs_1_.other_ref, bf16[128,512]{1,0:T(8,128)(2,1)S(1)} %collective-permute-done.1.refs_2_.mine_ref, ...), custom_call_target="tpu_custom_call" | custom-call | flops 536870912 | bytes 4194304 | tf_op jit(solution)/shard_map/queries/pallas_call | solution.py:182
  28.3 5.3 %collective-permute-done.7.mem_ref = bf16[272,512]{1,0:T(8,128)(2,1)S(1)} collective-permute-done((bf16[272,512]{1,0:T(8,128)(2,1)S(1)}, bf16[272,512]{1,0:T(8,128)(2,1)S(1)}, u32[]{:S(2)}, u32[]{:S(2)}) %collective-permute-start.7) | collective-permute-done | bytes 278560 | tf_op jit(solution)/shard_map/ppermute | solution.py:267
  33.6 2.3 %attend.1 = (bf16[4,128,512]{2,1,0:T(8,128)(2,1)S(1)}, f32[4,128,512]{2,1,0:T(8,128)S(1)}) custom-call(bf16[128,512]{1,0:T(8,128)(2,1)S(1)} %get-tuple-element.13.qc_ref, bf16[128,512]{1,0:T(8,128)(2,1)S(1)} %get-tuple-element.14.qp_ref, bf16[272,512]{1,0:T(8,128)(2,1)S(1)} %collective-permute-done.7.mem_ref, bf16[272,512]{1,0:T(8,128)(2,1)S(1)} %kv_step.7.own_ref, ...), custom_call_target="tpu_custom_call" | custom-call | flops 637534208 | bytes 4194304 | tf_op jit(solution)/shard_map/attend/pallas_call | solution.py:242
  36.0 1.9 %collective-permute-done.8 = bf16[4,128,512]{2,1,0:T(8,128)(2,1)S(1)} collective-permute-done((bf16[4,128,512]{2,1,0:T(8,128)(2,1)S(1)}, bf16[4,128,512]{2,1,0:T(8,128)(2,1)S(1)}, u32[]{:S(2)}, u32[]{:S(2)}) %collective-permute-start.8) | collective-permute-done | bytes 524320 | tf_op jit(solution)/shard_map/ppermute | solution.py:264
  37.9 0.2 fusion.4
  38.2 2.8 %collective-permute-start.10 = (bf16[128,512]{1,0:T(8,128)(2,1)S(1)}, bf16[128,512]{1,0:T(8,128)(2,1)S(1)}, u32[]{:S(2)}, u32[]{:S(2)}) collective-permute-start(bf16[128,512]{1,0:T(8,128)(2,1)S(1)} %get-tuple-element.23), channel_id=1, source_target_pairs={{0,4},{1,5},{2,6},{3,7},{4,0},{5,1},{6,2},{7,3},{8,12},{9,13},{10,... | collective-permute-start | bytes 393224 | tf_op jit(solution)/shard_map/ppermute | solution.py:261
  40.9 2.9 %collective-permute-start.11 = (bf16[128,512]{1,0:T(8,128)(2,1)S(1)}, bf16[128,512]{1,0:T(8,128)(2,1)S(1)}, u32[]{:S(2)}, u32[]{:S(2)}) collective-permute-start(bf16[128,512]{1,0:T(8,128)(2,1)S(1)} %get-tuple-element.22), channel_id=1, source_target_pairs={{0,6},{1,7},{2,0},{3,1},{4,2},{5,3},{6,4},{7,5},{8,14},{9,15},{10,... | collective-permute-start | bytes 393224 | tf_op jit(solution)/shard_map/ppermute | solution.py:261
  43.9 2.9 %collective-permute-done.10 = bf16[128,512]{1,0:T(8,128)(2,1)S(1)} collective-permute-done((bf16[128,512]{1,0:T(8,128)(2,1)S(1)}, bf16[128,512]{1,0:T(8,128)(2,1)S(1)}, u32[]{:S(2)}, u32[]{:S(2)}) %collective-permute-start.10) | collective-permute-done | bytes 131104 | tf_op jit(solution)/shard_map/ppermute | solution.py:261
  46.8 0.9 %collective-permute-done.11 = bf16[128,512]{1,0:T(8,128)(2,1)S(1)} collective-permute-done((bf16[128,512]{1,0:T(8,128)(2,1)S(1)}, bf16[128,512]{1,0:T(8,128)(2,1)S(1)}, u32[]{:S(2)}, u32[]{:S(2)}) %collective-permute-start.11) | collective-permute-done | bytes 131104 | tf_op jit(solution)/shard_map/ppermute | solution.py:261
  47.8 5.4 %collective-permute-done.9 = bf16[128,512]{1,0:T(8,128)(2,1)S(1)} collective-permute-done((bf16[128,512]{1,0:T(8,128)(2,1)S(1)}, bf16[128,512]{1,0:T(8,128)(2,1)S(1)}, u32[]{:S(2)}, u32[]{:S(2)}) %collective-permute-start.9) | collective-permute-done | bytes 131104 | tf_op jit(solution)/shard_map/ppermute | solution.py:261
  53.2 0.7 %fusion.3 = bf16[128,512]{1,0:T(8,128)(2,1)} fusion(f32[4,128,512]{2,1,0:T(8,128)S(1)} %get-tuple-element.20, bf16[128,512]{1,0:T(8,128)(2,1)S(1)} %collective-permute-done.11, bf16[128,512]{1,0:T(8,128)(2,1)S(1)} %collective-permute-done.10, bf16[128,512]{1,0:T(8,128)(2,1)S(1)} %collective-permute-done.9), kind=kLoop, calls=%fused_computation.5 | loop fusion | flops 458752 | bytes 786432 | tf_op jit(solution)/shard_map/convert_element_type | solution.py:287
  (17 shorter events, 0.1 us)
Async XLA Ops:
  0.0 9.3 %collective-permute-start.1 = (bf16[128,512]{1,0:T(8,128)(2,1)}, bf16[128,512]{1,0:T(8,128)(2,1)S(1)}, u32[]{:S(2)}, u32[]{:S(2)}) collective-permute-start(bf16[128,512]{1,0:T(8,128)(2,1)} %mine_ref.1), channel_id=1, source_target_pairs={{0,2},{1,3},{2,4},{3,5},{4,6},{5,7},{6,0},{7,1},{8,10},{9,11},{10,... | collective-permute-start | bytes 393224 | tf_op jit(solution)/shard_map/ppermute | solution.py:261
  3.0 19.1 %collective-permute-start = (bf16[128,512]{1,0:T(8,128)(2,1)}, bf16[128,512]{1,0:T(8,128)(2,1)S(1)}, u32[]{:S(2)}, u32[]{:S(2)}) collective-permute-start(bf16[128,512]{1,0:T(8,128)(2,1)} %mine_ref.1), channel_id=1, source_target_pairs={{0,1},{1,0},{2,3},{3,2},{4,5},{5,4},{6,7},{7,6},{8,9},{9,8},{10,11... | collective-permute-start | bytes 393224 | tf_op jit(solution)/shard_map/ppermute | solution.py:264
  3.0 11.5 %collective-permute-start.3 = (bf16[128,512]{1,0:T(8,128)(2,1)}, bf16[128,512]{1,0:T(8,128)(2,1)S(1)}, u32[]{:S(2)}, u32[]{:S(2)}) collective-permute-start(bf16[128,512]{1,0:T(8,128)(2,1)} %mine_ref.1), channel_id=1, source_target_pairs={{0,4},{1,5},{2,6},{3,7},{4,0},{5,1},{6,2},{7,3},{8,12},{9,13},{10,... | collective-permute-start | bytes 393224 | tf_op jit(solution)/shard_map/ppermute | solution.py:261
  5.6 8.9 %collective-permute-start.5 = (bf16[128,512]{1,0:T(8,128)(2,1)}, bf16[128,512]{1,0:T(8,128)(2,1)S(1)}, u32[]{:S(2)}, u32[]{:S(2)}) collective-permute-start(bf16[128,512]{1,0:T(8,128)(2,1)} %mine_ref.1), channel_id=1, source_target_pairs={{0,6},{1,7},{2,0},{3,1},{4,2},{5,3},{6,4},{7,5},{8,14},{9,15},{10,... | collective-permute-start | bytes 393224 | tf_op jit(solution)/shard_map/ppermute | solution.py:261
  9.3 13.4 %collective-permute-start.2 = (bf16[128,512]{1,0:T(8,128)(2,1)S(1)}, bf16[128,512]{1,0:T(8,128)(2,1)S(1)}, u32[]{:S(2)}, u32[]{:S(2)}) collective-permute-start(bf16[128,512]{1,0:T(8,128)(2,1)S(1)} %collective-permute-done.1.refs_2_.mine_ref), channel_id=1, source_target_pairs={{0,1},{1,0},{2,3},{3,2},{4,5},{5,4},{6,7},{7,6},{8,9},{9,8},{10,11... | collective-permute-start | bytes 393224 | tf_op jit(solution)/shard_map/ppermute | solution.py:264
  10.0 12.2 %copy-start = (bf16[128,512]{1,0:T(8,128)(2,1)S(1)}, bf16[128,512]{1,0:T(8,128)(2,1)}, u32[]{:S(2)}) copy-start(bf16[128,512]{1,0:T(8,128)(2,1)} %mine_ref.1) | copy-start | bytes 393220
  14.5 8.7 %collective-permute-start.4 = (bf16[128,512]{1,0:T(8,128)(2,1)S(1)}, bf16[128,512]{1,0:T(8,128)(2,1)S(1)}, u32[]{:S(2)}, u32[]{:S(2)}) collective-permute-start(bf16[128,512]{1,0:T(8,128)(2,1)S(1)} %collective-permute-done.3.refs_4_.mine_ref), channel_id=1, source_target_pairs={{0,1},{1,0},{2,3},{3,2},{4,5},{5,4},{6,7},{7,6},{8,9},{9,8},{10,11... | collective-permute-start | bytes 393224 | tf_op jit(solution)/shard_map/ppermute | solution.py:264
  14.5 9.2 %collective-permute-start.6 = (bf16[128,512]{1,0:T(8,128)(2,1)S(1)}, bf16[128,512]{1,0:T(8,128)(2,1)S(1)}, u32[]{:S(2)}, u32[]{:S(2)}) collective-permute-start(bf16[128,512]{1,0:T(8,128)(2,1)S(1)} %collective-permute-done.5.refs_6_.mine_ref), channel_id=1, source_target_pairs={{0,1},{1,0},{2,3},{3,2},{4,5},{5,4},{6,7},{7,6},{8,9},{9,8},{10,11... | collective-permute-start | bytes 393224 | tf_op jit(solution)/shard_map/ppermute | solution.py:264
  23.6 3.9 %copy-start.1 = (f32[4,128]{1,0:T(4,128)S(1)}, f32[4,128]{1,0:T(4,128)}, u32[]{:S(2)}) copy-start(f32[4,128]{1,0:T(4,128)} %param.11) | copy-start | bytes 6148
  23.6 3.9 %copy-start.2 = (f32[4,128]{1,0:T(4,128)S(1)}, f32[4,128]{1,0:T(4,128)}, u32[]{:S(2)}) copy-start(f32[4,128]{1,0:T(4,128)} %param.12) | copy-start | bytes 6148
  24.1 9.5 %collective-permute-start.7 = (bf16[272,512]{1,0:T(8,128)(2,1)S(1)}, bf16[272,512]{1,0:T(8,128)(2,1)S(1)}, u32[]{:S(2)}, u32[]{:S(2)}) collective-permute-start(bf16[272,512]{1,0:T(8,128)(2,1)S(1)} %kv_step.7.own_ref), channel_id=1, source_target_pairs={{0,8},{8,16},{16,24},{1,9},{9,17},{17,25},{2,10},{10,18},{18,26},{... | collective-permute-start | bytes 835592 | tf_op jit(solution)/shard_map/ppermute | solution.py:267
  35.9 2.0 %collective-permute-start.8 = (bf16[4,128,512]{2,1,0:T(8,128)(2,1)S(1)}, bf16[4,128,512]{2,1,0:T(8,128)(2,1)S(1)}, u32[]{:S(2)}, u32[]{:S(2)}) collective-permute-start(bf16[4,128,512]{2,1,0:T(8,128)(2,1)S(1)} %get-tuple-element.18), channel_id=1, source_target_pairs={{0,1},{1,0},{2,3},{3,2},{4,5},{5,4},{6,7},{7,6},{8,9},{9,8},{10,11... | collective-permute-start | bytes 1572872 | tf_op jit(solution)/shard_map/ppermute | solution.py:264
  38.2 8.7 %collective-permute-start.10 = (bf16[128,512]{1,0:T(8,128)(2,1)S(1)}, bf16[128,512]{1,0:T(8,128)(2,1)S(1)}, u32[]{:S(2)}, u32[]{:S(2)}) collective-permute-start(bf16[128,512]{1,0:T(8,128)(2,1)S(1)} %get-tuple-element.23), channel_id=1, source_target_pairs={{0,4},{1,5},{2,6},{3,7},{4,0},{5,1},{6,2},{7,3},{8,12},{9,13},{10,... | collective-permute-start | bytes 393224 | tf_op jit(solution)/shard_map/ppermute | solution.py:261
  40.9 6.8 %collective-permute-start.11 = (bf16[128,512]{1,0:T(8,128)(2,1)S(1)}, bf16[128,512]{1,0:T(8,128)(2,1)S(1)}, u32[]{:S(2)}, u32[]{:S(2)}) collective-permute-start(bf16[128,512]{1,0:T(8,128)(2,1)S(1)} %get-tuple-element.22), channel_id=1, source_target_pairs={{0,6},{1,7},{2,0},{3,1},{4,2},{5,3},{6,4},{7,5},{8,14},{9,15},{10,... | collective-permute-start | bytes 393224 | tf_op jit(solution)/shard_map/ppermute | solution.py:261
  43.9 9.3 %collective-permute-start.9 = (bf16[128,512]{1,0:T(8,128)(2,1)S(1)}, bf16[128,512]{1,0:T(8,128)(2,1)S(1)}, u32[]{:S(2)}, u32[]{:S(2)}) collective-permute-start(bf16[128,512]{1,0:T(8,128)(2,1)S(1)} %get-tuple-element.21), channel_id=1, source_target_pairs={{0,2},{1,3},{2,4},{3,5},{4,6},{5,7},{6,0},{7,1},{8,10},{9,11},{10,... | collective-permute-start | bytes 393224 | tf_op jit(solution)/shard_map/ppermute | solution.py:261

commit v3 on v2

--- a/solution.py
+++ b/solution.py
@@ -104,10 +104,9 @@
             pltpu.VMEM((rows, width), BF16),
             pltpu.SemaphoreType.DMA((parts + 4,)),
         ],
-        2 * rows * width * cols,
-        20 * width * cols,
+        rows * width,
+        rows * width,
         "load",
-        4 * 16 * width,
     )(in_hbm(w_pos), in_hbm(w_qkv), in_hbm(w_out))
 
 
@@ -154,8 +153,8 @@
         out,
         [vmem_spec()] * len(args),
         [],
-        8 * rows * depth * cols,
-        8 * depth * cols,
+        rows * depth,
+        rows * depth,
         "kv_step",
     )(*args)
 
@@ -267,9 +266,12 @@
         return lax.ppermute(value, "seq", [(i, i + 1) for i in range(segments - 1)])
 
     mine = [tokens] + [across(tokens, k) for k in range(1, chips)]
-    other = [swap(chunk) for chunk in mine]
+    other = [swap(tokens)]
     docs = (doc_ids + 1).astype(F32).reshape(1, rows)
     rel, w_qkv, w_out = load(w_pos, w_qkv, w_out, 2 * rows)
+    for k in range(1, chips):
+        mine[k], rel = lax.optimization_barrier((mine[k], rel))
+        other.append(swap(mine[k]))
     own = None
     for k in range(chips):
         own = kv_step(k, mine[k], other[k], w_qkv, own, docs if k == chips - 1 else None)

time: 54.8 us -> 47.3 us (0.86)
  waiting for transfers between devices: 23.3 us -> 16.8 us
  other arithmetic: 1.59 us -> 0.94 us
    ppermute x6, waiting for transfers between devices: 16.1 us -> 9.29 us  [across(): lax.ppermute(value, 'mp', [(i, (i + 2 * k) % count) for i in range(count)])]
    reshape x1, other arithmetic: 0.66 us -> 0.01 us  [shards(): docs = (doc_ids + 1).astype(F32).reshape(1, rows)]
    ppermute x5, starting transfers between devices: 0.59 us -> 1.16 us  [swap(): return lax.ppermute(value, 'mp', [(i, i ^ 1) for i in range(count)])]
  transfers between devices with their start and end apart: 12 -> 12, of which waited for: 7 -> 4; matrix products, arithmetic and copies ran while one was open for 1% -> 0% of each run, Pallas kernels for 17% -> 20%
where the time goes in v3:
time: 47.3 us; the launch traced here: 46.7 us
  waiting for transfers between devices  16.8 us (36%)
  starting transfers between devices  16.7 us (35%)
  Pallas kernels  12.1 us (26%)
  other arithmetic  0.94 us (2%)
    ppermute x6, starting transfers between devices, across(): lax.ppermute(value, 'mp', [(i, (i + 2 * k) % count) for i in range(count)])  12.2 us
    ppermute x6, waiting for transfers between devices, across(): lax.ppermute(value, 'mp', [(i, (i + 2 * k) % count) for i in range(count)])  9.29 us
    pallas_call x1, Pallas kernels, load(): call(functools.partial(load_kernel, parts), (pltpu.VMEM((rows, cols), BF1...  7.16 us
    ppermute x1, waiting for transfers between devices, onward(): return lax.ppermute(value, 'seq', [(i, i + 1) for i in range(segments - 1)])  5.6 us
    ppermute x1, starting transfers between devices, onward(): return lax.ppermute(value, 'seq', [(i, i + 1) for i in range(segments - 1)])  3.4 us
    pallas_call x1, Pallas kernels, attend(): call(functools.partial(attend_kernel, heads), (pltpu.VMEM((half, rows, wi...  2.33 us
    ppermute x5, waiting for transfers between devices, swap(): return lax.ppermute(value, 'mp', [(i, i ^ 1) for i in range(count)])  1.91 us
    pallas_call x4, Pallas kernels, kv_step(): call(functools.partial(kv_kernel, first, last, back), out, [vmem_spec()]...  1.85 us
  transfers between devices with their start and end apart: 12, of which 4 were waited for; matrix products, arithmetic and copies ran while one was open for 0% of the time, Pallas kernels for 20%

profile of v3, /device:TPU:0, one launch (start us, length us, event | category | flops | bytes accessed | tf_op | source)
XLA Modules:
  0.0 46.7 jit_solution(12441959501988823081)
XLA Ops:
  0.0 3.0 %collective-permute-start.1 = (bf16[128,512]{1,0:T(8,128)(2,1)}, bf16[128,512]{1,0:T(8,128)(2,1)S(1)}, u32[]{:S(2)}, u32[]{:S(2)}) collective-permute-start(bf16[128,512]{1,0:T(8,128)(2,1)} %mine_ref.1), channel_id=1, source_target_pairs={{0,2},{1,3},{2,4},{3,5},{4,6},{5,7},{6,0},{7,1},{8,10},{9,11},{10,... | collective-permute-start | bytes 393224 | tf_op jit(solution)/shard_map/ppermute | solution.py:260
  3.0 2.6 %collective-permute-start.3 = (bf16[128,512]{1,0:T(8,128)(2,1)}, bf16[128,512]{1,0:T(8,128)(2,1)S(1)}, u32[]{:S(2)}, u32[]{:S(2)}) collective-permute-start(bf16[128,512]{1,0:T(8,128)(2,1)} %mine_ref.1), channel_id=1, source_target_pairs={{0,4},{1,5},{2,6},{3,7},{4,0},{5,1},{6,2},{7,3},{8,12},{9,13},{10,... | collective-permute-start | bytes 393224 | tf_op jit(solution)/shard_map/ppermute | solution.py:260
  5.6 1.3 %collective-permute-start.5 = (bf16[128,512]{1,0:T(8,128)(2,1)}, bf16[128,512]{1,0:T(8,128)(2,1)S(1)}, u32[]{:S(2)}, u32[]{:S(2)}) collective-permute-start(bf16[128,512]{1,0:T(8,128)(2,1)} %mine_ref.1), channel_id=1, source_target_pairs={{0,6},{1,7},{2,0},{3,1},{4,2},{5,3},{6,4},{7,5},{8,14},{9,15},{10,... | collective-permute-start | bytes 393224 | tf_op jit(solution)/shard_map/ppermute | solution.py:260
  7.0 7.2 %load.1 = (bf16[256,512]{1,0:T(8,128)(2,1)S(1)}, bf16[3,4096,512]{2,1,0:T(8,128)(2,1)S(1)}, bf16[512,4096]{1,0:T(8,128)(2,1)S(1)}) custom-call(bf16[4096,512]{1,0:T(8,128)(2,1)} %w_pos.1, bf16[3,4096,512]{2,1,0:T(8,128)(2,1)} %w_qkv.1, bf16[512,4096]{1,0:T(8,128)(2,1)} %w_out.1), custom_call_target="tpu_custom_call" | custom-call | flops 1048576 | bytes 1048576 | tf_op jit(solution)/shard_map/load/pallas_call | solution.py:94
  14.2 0.6 %collective-permute-start.2 = (bf16[128,512]{1,0:T(8,128)(2,1)S(1)}, bf16[128,512]{1,0:T(8,128)(2,1)S(1)}, u32[]{:S(2)}, u32[]{:S(2)}) collective-permute-start(bf16[128,512]{1,0:T(8,128)(2,1)S(1)} %collective-permute-done.1.refs_2_.mine_ref), channel_id=1, source_target_pairs={{0,1},{1,0},{2,3},{3,2},{4,5},{5,4},{6,7},{7,6},{8,9},{9,8},{10,11... | collective-permute-start | bytes 393224 | tf_op jit(solution)/shard_map/ppermute | solution.py:263
  14.7 0.1 collective-permute-start.4
  14.8 0.4 collective-permute-start.6
  15.3 0.5 kv_step.4.refs_0_
  15.7 0.5 %kv_step.5.refs_0_ = f32[2,128,512]{2,1,0:T(8,128)S(1)} custom-call(bf16[128,512]{1,0:T(8,128)(2,1)S(1)} %collective-permute-done.1.refs_2_.mine_ref, bf16[128,512]{1,0:T(8,128)(2,1)S(1)} %collective-permute-done.2.refs_3_.other_ref, bf16[3,4096,512]{2,1,0:T(8,128)(2,1)S(1)} %get-tuple-element.24.refs_8_.w_ref, f32[2,128,512]{2,1,0:T(8,128)S(1)} %kv_step.4.refs_0_), custom_call_target="tpu_custom_call" | custom-call | flops 65536 | bytes 65536 | tf_op jit(solution)/shard_map/kv_step/pallas_call | solution.py:151
  16.2 0.5 kv_step.6.refs_0_
  16.7 0.0 copy-start.1
  16.7 0.5 kv_step.7.own_ref
  17.2 3.4 %collective-permute-start.7 = (bf16[272,512]{1,0:T(8,128)(2,1)S(1)}, bf16[272,512]{1,0:T(8,128)(2,1)S(1)}, u32[]{:S(2)}, u32[]{:S(2)}) collective-permute-start(bf16[272,512]{1,0:T(8,128)(2,1)S(1)} %kv_step.7.own_ref), channel_id=1, source_target_pairs={{0,8},{8,16},{16,24},{1,9},{9,17},{17,25},{2,10},{10,18},{18,26},{... | collective-permute-start | bytes 835592 | tf_op jit(solution)/shard_map/ppermute | solution.py:266
  20.6 0.7 %queries.1 = (bf16[128,512]{1,0:T(8,128)(2,1)S(1)}, bf16[128,512]{1,0:T(8,128)(2,1)S(1)}) custom-call(bf16[128,512]{1,0:T(8,128)(2,1)S(1)} %copy-done, bf16[128,512]{1,0:T(8,128)(2,1)S(1)} %collective-permute-done.refs_1_.other_ref, bf16[128,512]{1,0:T(8,128)(2,1)S(1)} %collective-permute-done.1.refs_2_.mine_ref, ...), custom_call_target="tpu_custom_call" | custom-call | flops 536870912 | bytes 4194304 | tf_op jit(solution)/shard_map/queries/pallas_call | solution.py:181
  21.4 5.6 %collective-permute-done.7.mem_ref = bf16[272,512]{1,0:T(8,128)(2,1)S(1)} collective-permute-done((bf16[272,512]{1,0:T(8,128)(2,1)S(1)}, bf16[272,512]{1,0:T(8,128)(2,1)S(1)}, u32[]{:S(2)}, u32[]{:S(2)}) %collective-permute-start.7) | collective-permute-done | bytes 278560 | tf_op jit(solution)/shard_map/ppermute | solution.py:266
  27.0 2.3 %attend.1 = (bf16[4,128,512]{2,1,0:T(8,128)(2,1)S(1)}, f32[4,128,512]{2,1,0:T(8,128)S(1)}) custom-call(bf16[128,512]{1,0:T(8,128)(2,1)S(1)} %get-tuple-element.25.qc_ref, bf16[128,512]{1,0:T(8,128)(2,1)S(1)} %get-tuple-element.26.qp_ref, bf16[272,512]{1,0:T(8,128)(2,1)S(1)} %collective-permute-done.7.mem_ref, bf16[272,512]{1,0:T(8,128)(2,1)S(1)} %kv_step.7.own_ref, ...), custom_call_target="tpu_custom_call" | custom-call | flops 637534208 | bytes 4194304 | tf_op jit(solution)/shard_map/attend/pallas_call | solution.py:241
  29.3 0.1 collective-permute-start.8
  29.4 1.9 %collective-permute-done.8 = bf16[4,128,512]{2,1,0:T(8,128)(2,1)S(1)} collective-permute-done((bf16[4,128,512]{2,1,0:T(8,128)(2,1)S(1)}, bf16[4,128,512]{2,1,0:T(8,128)(2,1)S(1)}, u32[]{:S(2)}, u32[]{:S(2)}) %collective-permute-start.8) | collective-permute-done | bytes 524320 | tf_op jit(solution)/shard_map/ppermute | solution.py:263
  31.3 0.2 fusion.4
  31.5 1.9 %collective-permute-start.10 = (bf16[128,512]{1,0:T(8,128)(2,1)S(1)}, bf16[128,512]{1,0:T(8,128)(2,1)S(1)}, u32[]{:S(2)}, u32[]{:S(2)}) collective-permute-start(bf16[128,512]{1,0:T(8,128)(2,1)S(1)} %get-tuple-element.35), channel_id=1, source_target_pairs={{0,4},{1,5},{2,6},{3,7},{4,0},{5,1},{6,2},{7,3},{8,12},{9,13},{10,... | collective-permute-start | bytes 393224 | tf_op jit(solution)/shard_map/ppermute | solution.py:260
  33.5 3.3 %collective-permute-start.11 = (bf16[128,512]{1,0:T(8,128)(2,1)S(1)}, bf16[128,512]{1,0:T(8,128)(2,1)S(1)}, u32[]{:S(2)}, u32[]{:S(2)}) collective-permute-start(bf16[128,512]{1,0:T(8,128)(2,1)S(1)} %get-tuple-element.34), channel_id=1, source_target_pairs={{0,6},{1,7},{2,0},{3,1},{4,2},{5,3},{6,4},{7,5},{8,14},{9,15},{10,... | collective-permute-start | bytes 393224 | tf_op jit(solution)/shard_map/ppermute | solution.py:260
  36.7 4.6 %collective-permute-done.10 = bf16[128,512]{1,0:T(8,128)(2,1)S(1)} collective-permute-done((bf16[128,512]{1,0:T(8,128)(2,1)S(1)}, bf16[128,512]{1,0:T(8,128)(2,1)S(1)}, u32[]{:S(2)}, u32[]{:S(2)}) %collective-permute-start.10) | collective-permute-done | bytes 131104 | tf_op jit(solution)/shard_map/ppermute | solution.py:260
  41.3 4.7 %collective-permute-done.9 = bf16[128,512]{1,0:T(8,128)(2,1)S(1)} collective-permute-done((bf16[128,512]{1,0:T(8,128)(2,1)S(1)}, bf16[128,512]{1,0:T(8,128)(2,1)S(1)}, u32[]{:S(2)}, u32[]{:S(2)}) %collective-permute-start.9) | collective-permute-done | bytes 131104 | tf_op jit(solution)/shard_map/ppermute | solution.py:260
  46.0 0.7 %fusion.3 = bf16[128,512]{1,0:T(8,128)(2,1)} fusion(f32[4,128,512]{2,1,0:T(8,128)S(1)} %get-tuple-element.32, bf16[128,512]{1,0:T(8,128)(2,1)S(1)} %collective-permute-done.11, bf16[128,512]{1,0:T(8,128)(2,1)S(1)} %collective-permute-done.10, bf16[128,512]{1,0:T(8,128)(2,1)S(1)} %collective-permute-done.9), kind=kLoop, calls=%fused_computation.5 | loop fusion | flops 458752 | bytes 786432 | tf_op jit(solution)/shard_map/convert_element_type | solution.py:289
  (19 shorter events, 0.1 us)
Async XLA Ops:
  0.0 15.3 %copy-start = (bf16[128,512]{1,0:T(8,128)(2,1)S(1)}, bf16[128,512]{1,0:T(8,128)(2,1)}, u32[]{:S(2)}) copy-start(bf16[128,512]{1,0:T(8,128)(2,1)} %mine_ref.1) | copy-start | bytes 393220
  0.0 15.2 %copy-start.3 = (s32[128]{0:T(128)S(1)}, s32[128]{0:T(128)}, u32[]{:S(2)}) copy-start(s32[128]{0:T(128)} %param.13) | copy-start | bytes 1540
  0.0 14.1 %collective-permute-start.1 = (bf16[128,512]{1,0:T(8,128)(2,1)}, bf16[128,512]{1,0:T(8,128)(2,1)S(1)}, u32[]{:S(2)}, u32[]{:S(2)}) collective-permute-start(bf16[128,512]{1,0:T(8,128)(2,1)} %mine_ref.1), channel_id=1, source_target_pairs={{0,2},{1,3},{2,4},{3,5},{4,6},{5,7},{6,0},{7,1},{8,10},{9,11},{10,... | collective-permute-start | bytes 393224 | tf_op jit(solution)/shard_map/ppermute | solution.py:260
  3.0 11.7 %collective-permute-start.3 = (bf16[128,512]{1,0:T(8,128)(2,1)}, bf16[128,512]{1,0:T(8,128)(2,1)S(1)}, u32[]{:S(2)}, u32[]{:S(2)}) collective-permute-start(bf16[128,512]{1,0:T(8,128)(2,1)} %mine_ref.1), channel_id=1, source_target_pairs={{0,4},{1,5},{2,6},{3,7},{4,0},{5,1},{6,2},{7,3},{8,12},{9,13},{10,... | collective-permute-start | bytes 393224 | tf_op jit(solution)/shard_map/ppermute | solution.py:260
  5.6 9.2 %collective-permute-start.5 = (bf16[128,512]{1,0:T(8,128)(2,1)}, bf16[128,512]{1,0:T(8,128)(2,1)S(1)}, u32[]{:S(2)}, u32[]{:S(2)}) collective-permute-start(bf16[128,512]{1,0:T(8,128)(2,1)} %mine_ref.1), channel_id=1, source_target_pairs={{0,6},{1,7},{2,0},{3,1},{4,2},{5,3},{6,4},{7,5},{8,14},{9,15},{10,... | collective-permute-start | bytes 393224 | tf_op jit(solution)/shard_map/ppermute | solution.py:260
  7.0 8.3 %collective-permute-start = (bf16[128,512]{1,0:T(8,128)(2,1)}, bf16[128,512]{1,0:T(8,128)(2,1)S(1)}, u32[]{:S(2)}, u32[]{:S(2)}) collective-permute-start(bf16[128,512]{1,0:T(8,128)(2,1)} %mine_ref.1), channel_id=1, source_target_pairs={{0,1},{1,0},{2,3},{3,2},{4,5},{5,4},{6,7},{7,6},{8,9},{9,8},{10,11... | collective-permute-start | bytes 393224 | tf_op jit(solution)/shard_map/ppermute | solution.py:263
  14.2 1.6 %collective-permute-start.2 = (bf16[128,512]{1,0:T(8,128)(2,1)S(1)}, bf16[128,512]{1,0:T(8,128)(2,1)S(1)}, u32[]{:S(2)}, u32[]{:S(2)}) collective-permute-start(bf16[128,512]{1,0:T(8,128)(2,1)S(1)} %collective-permute-done.1.refs_2_.mine_ref), channel_id=1, source_target_pairs={{0,1},{1,0},{2,3},{3,2},{4,5},{5,4},{6,7},{7,6},{8,9},{9,8},{10,11... | collective-permute-start | bytes 393224 | tf_op jit(solution)/shard_map/ppermute | solution.py:263
  14.7 1.5 %collective-permute-start.4 = (bf16[128,512]{1,0:T(8,128)(2,1)S(1)}, bf16[128,512]{1,0:T(8,128)(2,1)S(1)}, u32[]{:S(2)}, u32[]{:S(2)}) collective-permute-start(bf16[128,512]{1,0:T(8,128)(2,1)S(1)} %collective-permute-done.3.refs_4_.mine_ref), channel_id=1, source_target_pairs={{0,1},{1,0},{2,3},{3,2},{4,5},{5,4},{6,7},{7,6},{8,9},{9,8},{10,11... | collective-permute-start | bytes 393224 | tf_op jit(solution)/shard_map/ppermute | solution.py:263
  14.8 1.9 %collective-permute-start.6 = (bf16[128,512]{1,0:T(8,128)(2,1)S(1)}, bf16[128,512]{1,0:T(8,128)(2,1)S(1)}, u32[]{:S(2)}, u32[]{:S(2)}) collective-permute-start(bf16[128,512]{1,0:T(8,128)(2,1)S(1)} %collective-permute-done.5.refs_6_.mine_ref), channel_id=1, source_target_pairs={{0,1},{1,0},{2,3},{3,2},{4,5},{5,4},{6,7},{7,6},{8,9},{9,8},{10,11... | collective-permute-start | bytes 393224 | tf_op jit(solution)/shard_map/ppermute | solution.py:263
  16.7 3.9 %copy-start.1 = (f32[4,128]{1,0:T(4,128)S(1)}, f32[4,128]{1,0:T(4,128)}, u32[]{:S(2)}) copy-start(f32[4,128]{1,0:T(4,128)} %param.11) | copy-start | bytes 6148
  16.7 3.9 %copy-start.2 = (f32[4,128]{1,0:T(4,128)S(1)}, f32[4,128]{1,0:T(4,128)}, u32[]{:S(2)}) copy-start(f32[4,128]{1,0:T(4,128)} %param.12) | copy-start | bytes 6148
  17.2 9.8 %collective-permute-start.7 = (bf16[272,512]{1,0:T(8,128)(2,1)S(1)}, bf16[272,512]{1,0:T(8,128)(2,1)S(1)}, u32[]{:S(2)}, u32[]{:S(2)}) collective-permute-start(bf16[272,512]{1,0:T(8,128)(2,1)S(1)} %kv_step.7.own_ref), channel_id=1, source_target_pairs={{0,8},{8,16},{16,24},{1,9},{9,17},{17,25},{2,10},{10,18},{18,26},{... | collective-permute-start | bytes 835592 | tf_op jit(solution)/shard_map/ppermute | solution.py:266
  29.3 2.0 %collective-permute-start.8 = (bf16[4,128,512]{2,1,0:T(8,128)(2,1)S(1)}, bf16[4,128,512]{2,1,0:T(8,128)(2,1)S(1)}, u32[]{:S(2)}, u32[]{:S(2)}) collective-permute-start(bf16[4,128,512]{2,1,0:T(8,128)(2,1)S(1)} %get-tuple-element.30), channel_id=1, source_target_pairs={{0,1},{1,0},{2,3},{3,2},{4,5},{5,4},{6,7},{7,6},{8,9},{9,8},{10,11... | collective-permute-start | bytes 1572872 | tf_op jit(solution)/shard_map/ppermute | solution.py:263
  31.5 9.8 %collective-permute-start.10 = (bf16[128,512]{1,0:T(8,128)(2,1)S(1)}, bf16[128,512]{1,0:T(8,128)(2,1)S(1)}, u32[]{:S(2)}, u32[]{:S(2)}) collective-permute-start(bf16[128,512]{1,0:T(8,128)(2,1)S(1)} %get-tuple-element.35), channel_id=1, source_target_pairs={{0,4},{1,5},{2,6},{3,7},{4,0},{5,1},{6,2},{7,3},{8,12},{9,13},{10,... | collective-permute-start | bytes 393224 | tf_op jit(solution)/shard_map/ppermute | solution.py:260
  33.5 7.8 %collective-permute-start.11 = (bf16[128,512]{1,0:T(8,128)(2,1)S(1)}, bf16[128,512]{1,0:T(8,128)(2,1)S(1)}, u32[]{:S(2)}, u32[]{:S(2)}) collective-permute-start(bf16[128,512]{1,0:T(8,128)(2,1)S(1)} %get-tuple-element.34), channel_id=1, source_target_pairs={{0,6},{1,7},{2,0},{3,1},{4,2},{5,3},{6,4},{7,5},{8,14},{9,15},{10,... | collective-permute-start | bytes 393224 | tf_op jit(solution)/shard_map/ppermute | solution.py:260
  36.7 9.3 %collective-permute-start.9 = (bf16[128,512]{1,0:T(8,128)(2,1)S(1)}, bf16[128,512]{1,0:T(8,128)(2,1)S(1)}, u32[]{:S(2)}, u32[]{:S(2)}) collective-permute-start(bf16[128,512]{1,0:T(8,128)(2,1)S(1)} %get-tuple-element.33), channel_id=1, source_target_pairs={{0,2},{1,3},{2,4},{3,5},{4,6},{5,7},{6,0},{7,1},{8,10},{9,11},{10,... | collective-permute-start | bytes 393224 | tf_op jit(solution)/shard_map/ppermute | solution.py:260

commit v4 on v3

v4 whole, which is shorter than its diff:
```python
import functools

import jax
import jax.numpy as jnp
from jax import lax
from jax.experimental import pallas as pl
from jax.experimental.pallas import tpu as pltpu
from jax.sharding import PartitionSpec as P

BF16 = jnp.bfloat16
F32 = jnp.float32
VMEM_LIMIT = 24 * 1024 * 1024


def vmem_spec():
    return pl.BlockSpec(memory_space=pltpu.VMEM)


def hbm_spec():
    return pl.BlockSpec(memory_space=pl.ANY)


def in_hbm(value):
    return pltpu.with_memory_space_constraint(value, pltpu.HBM)


def call(kernel, out_shape, in_specs, scratch, flops, nbytes, name, transcendentals=0):
    outs = jax.tree.map(lambda _: vmem_spec(), out_shape)
    return pl.pallas_call(
        kernel,
        out_shape=out_shape,
        in_specs=in_specs,
        out_specs=outs,
        scratch_shapes=scratch,
        compiler_params=pltpu.CompilerParams(vmem_limit_bytes=VMEM_LIMIT),
        cost_estimate=pl.CostEstimate(
            flops=flops, bytes_accessed=nbytes, transcendentals=transcendentals
        ),
        name=name,
    )


def dot(a, b):
    return jnp.dot(a, b, preferred_element_type=F32)


def dot_nt(a, b):
    return lax.dot_general(a, b, (((1,), (1,)), ((), ())), preferred_element_type=F32)


def load_kernel(parts, w_pos, w_qkv, w_out, rel_ref, qkv_ref, out_ref, wbuf, table, sems):
    rows, cols = rel_ref.shape
    width = w_pos.shape[0]
    half = width // 2
    depth = width // parts

    def pos_copy(i):
        part = pl.ds(i * depth, depth)
        return pltpu.make_async_copy(w_pos.at[part], wbuf.at[part], sems.at[i])

    copies = [pos_copy(i) for i in range(parts)]
    for c in (1, 2, 0):
        copies.append(pltpu.make_async_copy(w_qkv.at[c], qkv_ref.at[c], sems.at[parts + c]))
    copies.append(pltpu.make_async_copy(w_out, out_ref, sems.at[parts + 3]))
    for item in copies:
        item.start()
    fine = 16
    coarse = rows // fine
    index = lax.broadcasted_iota(jnp.int32, (1, half), 1).astype(F32) * 2.0
    freqs = 1.0 / 10000.0 ** (index / width)
    low = (fine - 1 - lax.broadcasted_iota(jnp.int32, (fine, half), 0)).astype(F32) * freqs
    high = (lax.broadcasted_iota(jnp.int32, (coarse, half), 0) * fine).astype(F32) * freqs
    sin_low, cos_low = jnp.sin(low), jnp.cos(low)
    sin_high, cos_high = jnp.sin(high), jnp.cos(high)
    for a in range(coarse):
        sh, ch = sin_high[a : a + 1], cos_high[a : a + 1]
        first = (coarse - 1 - a) * fine
        table[first : first + fine, :half] = (sh * cos_low + ch * sin_low).astype(BF16)
        table[first : first + fine, half:] = (ch * cos_low - sh * sin_low).astype(BF16)
    total = jnp.zeros((rows, cols), F32)
    for i in range(parts):
        copies[i].wait()
        total = total + dot(
            table[:, i * depth : (i + 1) * depth], wbuf[i * depth : (i + 1) * depth]
        )
    rel_ref[...] = total.astype(BF16)
    for item in copies[parts:]:
        item.wait()


def load(w_pos, w_qkv, w_out, rows):
    width, cols = w_pos.shape
    parts = 8
    return call(
        functools.partial(load_kernel, parts),
        (
            pltpu.VMEM((rows, cols), BF16),
            pltpu.VMEM(w_qkv.shape, BF16),
            pltpu.VMEM(w_out.shape, BF16),
        ),
        [hbm_spec()] * 3,
        [
            pltpu.VMEM((width, cols), BF16),
            pltpu.VMEM((rows, width), BF16),
            pltpu.SemaphoreType.DMA((parts + 4,)),
        ],
        rows * width,
        rows * width,
        "load",
    )(in_hbm(w_pos), in_hbm(w_qkv), in_hbm(w_out))


def here(back):
    me = lax.axis_index("mp")
    chips = lax.axis_size("mp") // 2
    return lax.rem(me, 2), lax.rem(me // 2 + chips - back, chips)


def row_block(core, place, i):
    return 2 * place + (core if i == 0 else 1 - core)


def kv_kernel(first, last, back, mine_ref, other_ref, w_ref, *refs):
    refs = list(refs)
    acc_ref = None if first else refs.pop(0)
    doc_ref = refs.pop(0) if last else None
    rows, depth = mine_ref.shape
    core, place = here(back)
    for c in range(2):
        total = None if first else acc_ref[c]
        for i, x_ref in enumerate((mine_ref, other_ref)):
            start = pl.multiple_of(row_block(core, place, i) * depth, depth)
            term = dot(x_ref[...], w_ref[c + 1, pl.ds(start, depth)])
            total = term if total is None else total + term
        if last:
            refs[c][:rows] = total.astype(BF16)
        else:
            refs[0][c] = total
    if last:
        key_ref = refs[0]
        key_ref[rows:] = jnp.zeros((16, key_ref.shape[1]), BF16)
        key_ref[rows:, :rows] = jnp.broadcast_to(doc_ref[...], (16, rows)).astype(BF16)


def kv_step(back, mine, other, w_qkv, acc, docs):
    rows, depth = mine.shape
    cols = w_qkv.shape[2]
    first, last = acc is None, docs is not None
    args = [mine, other, w_qkv] + ([] if first else [acc]) + ([docs] if last else [])
    out = pltpu.VMEM((2, rows, cols), F32)
    if last:
        out = (pltpu.VMEM((rows + 16, cols), BF16), pltpu.VMEM((rows, cols), BF16))
    return call(
        functools.partial(kv_kernel, first, last, back),
        out,
        [vmem_spec()] * len(args),
        [],
        rows * depth,
        rows * depth,
        "kv_step",
    )(*args)


def q_kernel(count, heads, *refs):
    x_refs = refs[:count]
    w_ref, cb_ref, pb_ref, key_ref, rel_ref, doc_ref, qc_ref, score_ref = refs[count:]
    rows, depth = x_refs[0].shape
    head_dim = qc_ref.shape[1] // heads
    total = None
    for i in range(count):
        core, place = here(i // 2)
        start = pl.multiple_of(row_block(core, place, i % 2) * depth, depth)
        term = dot(x_refs[i][...], w_ref[0, pl.ds(start, depth)])
        total = term if total is None else total + term
    query_content = (total + cb_ref[...]).astype(BF16)
    query_pos = (total + pb_ref[...]).astype(BF16)
    qc_ref[...] = query_content
    query = lax.broadcasted_iota(jnp.int32, (rows, rows), 0)
    key = lax.broadcasted_iota(jnp.int32, (rows, rows), 1)
    own_doc = jnp.broadcast_to(doc_ref[...], (rows, rows))
    allowed = (key <= query) & (own_doc == own_doc.T)
    scale = 1.0 / (float(head_dim) ** 0.5)
    for h in range(heads):
        part = slice(h * head_dim, (h + 1) * head_dim)
        pos = pltpu.roll(
            dot_nt(query_pos[:, part], rel_ref[:, part]), rows + 1, 1, stride=1, stride_axis=0
        )
        content = dot_nt(query_content[:, part], key_ref[:rows, part])
        score_ref[h, :, :rows] = pos[:, :rows]
        score_ref[h, :, rows:] = jnp.where(allowed, (content + pos[:, rows:]) * scale, -1e30)


def queries(chunks, w_qkv, content_bias, position_bias, own_key, rel, docs):
    count = len(chunks)
    rows, depth = chunks[0].shape
    cols = w_qkv.shape[2]
    heads = content_bias.shape[0]
    return call(
        functools.partial(q_kernel, count, heads),
        (pltpu.VMEM((rows, cols), BF16), pltpu.VMEM((heads, rows, 2 * rows), F32)),
        [vmem_spec()] * (count + 6),
        [],
        2 * count * rows * depth * cols,
        2 * count * depth * cols,
        "queries",
    )(
        *chunks,
        w_qkv,
        content_bias.reshape(1, cols),
        position_bias.reshape(1, cols),
        own_key,
        rel,
        docs,
    )


def weigh_kernel(qc_ref, score_ref, mem_ref, val_ref, doc_ref, weight_ref, out_ref):
    heads, rows, _ = score_ref.shape
    head_dim = qc_ref.shape[1] // heads
    exists = jnp.minimum(lax.axis_index("seq"), 1).astype(F32)
    mem_doc = jnp.broadcast_to(mem_ref[rows : rows + 1, :rows].astype(F32) * exists, (rows, rows))
    allowed = mem_doc == jnp.broadcast_to(doc_ref[...], (rows, rows)).T
    scale = 1.0 / (float(head_dim) ** 0.5)
    for h in range(heads):
        part = slice(h * head_dim, (h + 1) * head_dim)
        content = dot_nt(qc_ref[:, part], mem_ref[:rows, part])
        mem = jnp.where(allowed, (content + score_ref[h, :, :rows]) * scale, -1e30)
        own = score_ref[h, :, rows:]
        top = jnp.maximum(
            jnp.max(mem, axis=1, keepdims=True), jnp.max(own, axis=1, keepdims=True)
        )
        mem = jnp.where(mem > -1e29, jnp.exp(mem - top), 0.0)
        own = jnp.where(own > -1e29, jnp.exp(own - top), 0.0)
        total = jnp.sum(mem, axis=1, keepdims=True) + jnp.sum(own, axis=1, keepdims=True)
        weight_ref[h] = (mem / total).astype(BF16)
        out_ref[:, part] = dot((own / total).astype(BF16), val_ref[:, part])


def weigh(query_content, score, mem_key, own_val, docs):
    rows, cols = query_content.shape
    heads = score.shape[0]
    return call(
        weigh_kernel,
        (pltpu.VMEM((heads, rows, rows), BF16), pltpu.VMEM((rows, cols), F32)),
        [vmem_spec()] * 5,
        [],
        8 * rows * rows * cols,
        8 * rows * cols,
        "weigh",
    )(query_content, score, mem_key, own_val, docs)


def blocks_out(offsets, head_out, w_ref, away_ref, keep_ref):
    width = away_ref.shape[2]
    core, chip = here(0)
    chips = lax.axis_size("mp") // 2
    for away in (True, False):
        for i, k in enumerate(offsets):
            block = 2 * lax.rem(chip + k, chips) + (1 - core if away else core)
            start = pl.multiple_of(block * width, width)
            term = dot(head_out, w_ref[:, pl.ds(start, width)])
            if away:
                away_ref[i] = term.astype(BF16)
            else:
                keep_ref[i] = term


def mix_kernel(offsets, weight_ref, out_ref, mem_ref, w_ref, head_ref, away_ref, keep_ref):
    heads, rows, _ = weight_ref.shape
    head_dim = out_ref.shape[1] // heads
    for h in range(heads):
        part = slice(h * head_dim, (h + 1) * head_dim)
        out = out_ref[:, part] + dot(weight_ref[h], mem_ref[:, part])
        head_ref[:, part] = out.astype(BF16)
    blocks_out(offsets, head_ref[...], w_ref, away_ref, keep_ref)


def rest_kernel(offsets, head_ref, w_ref, away_ref, keep_ref):
    blocks_out(offsets, head_ref[...], w_ref, away_ref, keep_ref)


def block_shapes(offsets, rows, width):
    count = len(offsets)
    return (pltpu.VMEM((count, rows, width), BF16), pltpu.VMEM((count, rows, width), F32))


def mix(offsets, weights, out, mem_val, w_out, width):
    rows, cols = out.shape
    return call(
        functools.partial(mix_kernel, offsets),
        (pltpu.VMEM((rows, cols), BF16),) + block_shapes(offsets, rows, width),
        [vmem_spec()] * 4,
        [],
        4 * rows * cols * width * len(offsets),
        4 * cols * width * len(offsets),
        "mix",
    )(weights, out, mem_val, w_out)


def rest(offsets, head_out, w_out, width):
    rows, cols = head_out.shape
    return call(
        functools.partial(rest_kernel, offsets),
        block_shapes(offsets, rows, width),
        [vmem_spec()] * 2,
        [],
        4 * rows * cols * width * len(offsets),
        4 * cols * width * len(offsets),
        "rest",
    )(head_out, w_out)


def shards(tokens, w_qkv, w_pos, w_out, content_bias, position_bias, doc_ids):
    rows = tokens.shape[0]
    count = lax.axis_size("mp")
    chips = count // 2
    segments = lax.axis_size("seq")
    width = w_out.shape[1] // count

    def across(value, k):
        return lax.ppermute(value, "mp", [(i, (i + 2 * k) % count) for i in range(count)])

    def swap(value):
        return lax.ppermute(value, "mp", [(i, i ^ 1) for i in range(count)])

    def onward(value):
        return lax.ppermute(value, "seq", [(i, (i + 1) % segments) for i in range(segments)])

    mine = [tokens] + [across(tokens, k) for k in range(1, chips)]
    other = [swap(tokens)]
    docs = (doc_ids + 1).astype(F32).reshape(1, rows)
    rel, w_qkv, w_out = load(w_pos, w_qkv, w_out, 2 * rows)
    for k in range(1, chips):
        mine[k], rel = lax.optimization_barrier((mine[k], rel))
        other.append(swap(mine[k]))
    acc = None
    for k in range(chips):
        acc = kv_step(k, mine[k], other[k], w_qkv, acc, docs if k == chips - 1 else None)
    own_key, own_val = acc
    mem_key, mem_val = onward(own_key), onward(own_val)
    query_content, score = queries(
        [chunk for pair in zip(mine, other) for chunk in pair],
        w_qkv,
        content_bias,
        position_bias,
        own_key,
        rel,
        docs,
    )
    weights, out = weigh(query_content, score, mem_key, own_val, docs)
    first = [chips // 2]
    others = [k for k in range(chips) if k not in first]
    head_out, away, keep = mix(first, weights, out, mem_val, w_out, width)
    total = {first[0]: keep[0] + swap(away)[0].astype(F32)}
    away, keep = rest(others, head_out, w_out, width)
    away = swap(away).astype(F32)
    for i, k in enumerate(others):
        total[k] = keep[i] + away[i]
    result = total[0]
    for k in first + others:
        if k > 0:
            result = result + across(total[k].astype(BF16), k).astype(F32)
    return result.astype(BF16)


def solution(mesh):
    in_specs = (
        P("seq", "mp"),
        P(None, None, "mp"),
        P(None, "mp"),
        P("mp", None),
        P("mp", None),
        P("mp", None),
        P("seq"),
    )
    out_specs = P("seq", "mp")
    return jax.shard_map(shards, mesh=mesh, in_specs=in_specs, out_specs=out_specs, check_vma=False)
```

time: 47.3 us -> 43.9 us (0.928)
  waiting for transfers between devices: 16.8 us -> 12.7 us
  starting transfers between devices: 16.7 us -> 17.4 us
  Pallas kernels: 12.1 us -> 12.6 us
    ppermute x6, waiting for transfers between devices: 9.29 us -> 6.98 us  [across(): lax.ppermute(value, 'mp', [(i, (i + 2 * k) % count) for i in range(count)])]
    ppermute x1 -> x2, waiting for transfers between devices: 5.6 us -> 4.26 us  [onward(): lax.ppermute(value, 'seq', [(i, (i + 1) % segments) for i in range(segmen...]
    ppermute x6, starting transfers between devices: 12.2 us -> 12.7 us  [across(): lax.ppermute(value, 'mp', [(i, (i + 2 * k) % count) for i in range(count)])]
    ppermute x5 -> x6, starting transfers between devices: 1.16 us -> 1.65 us  [swap(): return lax.ppermute(value, 'mp', [(i, i ^ 1) for i in range(count)])]
    ppermute x5 -> x6, waiting for transfers between devices: 1.91 us -> 1.41 us  [swap(): return lax.ppermute(value, 'mp', [(i, i ^ 1) for i in range(count)])]
    pallas_call x2 -> x4, Pallas kernels: 3.07 us -> 3.54 us  [the longest x1 1.46 us: weigh(): call(weigh_kernel, (pltpu.VMEM((heads, rows, rows), BF16), pltpu.VMEM((ro...]
    ppermute x1 -> x2, starting transfers between devices: 3.4 us -> 3.03 us  [onward(): lax.ppermute(value, 'seq', [(i, (i + 1) % segments) for i in range(segmen...]
  transfers between devices with their start and end apart: 12 -> 14, of which waited for: 4 -> 5; matrix products, arithmetic and copies ran while one was open for 0% -> 0% of each run, Pallas kernels for 20% -> 25%
where the time goes in v4:
time: 43.9 us; the launch traced here: 43.8 us
  starting transfers between devices  17.4 us (40%)
  waiting for transfers between devices  12.7 us (29%)
  Pallas kernels  12.6 us (29%)
  other arithmetic  0.96 us (2%)
    ppermute x6, starting transfers between devices, across(): lax.ppermute(value, 'mp', [(i, (i + 2 * k) % count) for i in range(count)])  12.7 us
    pallas_call x1, Pallas kernels, load(): call(functools.partial(load_kernel, parts), (pltpu.VMEM((rows, cols), BF1...  7.16 us
    ppermute x6, waiting for transfers between devices, across(): lax.ppermute(value, 'mp', [(i, (i + 2 * k) % count) for i in range(count)])  6.98 us
    ppermute x2, waiting for transfers between devices, onward(): lax.ppermute(value, 'seq', [(i, (i + 1) % segments) for i in range(segmen...  4.26 us
    ppermute x2, starting transfers between devices, onward(): lax.ppermute(value, 'seq', [(i, (i + 1) % segments) for i in range(segmen...  3.03 us
    pallas_call x4, Pallas kernels, kv_step(): call(functools.partial(kv_kernel, first, last, back), out, [vmem_spec()]...  1.85 us
    ppermute x6, starting transfers between devices, swap(): return lax.ppermute(value, 'mp', [(i, i ^ 1) for i in range(count)])  1.65 us
    pallas_call x1, Pallas kernels, weigh(): call(weigh_kernel, (pltpu.VMEM((heads, rows, rows), BF16), pltpu.VMEM((ro...  1.46 us
  transfers between devices with their start and end apart: 14, of which 5 were waited for; matrix products, arithmetic and copies ran while one was open for 0% of the time, Pallas kernels for 25%

profile of v4, /device:TPU:0, one launch (start us, length us, event | category | flops | bytes accessed | tf_op | source)
XLA Modules:
  0.0 43.8 jit_solution(13218656204223206889)
XLA Ops:
  0.0 3.0 %collective-permute-start.1 = (bf16[128,512]{1,0:T(8,128)(2,1)}, bf16[128,512]{1,0:T(8,128)(2,1)S(1)}, u32[]{:S(2)}, u32[]{:S(2)}) collective-permute-start(bf16[128,512]{1,0:T(8,128)(2,1)} %refs_0_.1), channel_id=1, source_target_pairs={{0,2},{1,3},{2,4},{3,5},{4,6},{5,7},{6,0},{7,1},{8,10},{9,11},{10,... | collective-permute-start | bytes 393224 | tf_op jit(solution)/shard_map/ppermute | solution.py:321
  3.0 2.6 %collective-permute-start.3 = (bf16[128,512]{1,0:T(8,128)(2,1)}, bf16[128,512]{1,0:T(8,128)(2,1)S(1)}, u32[]{:S(2)}, u32[]{:S(2)}) collective-permute-start(bf16[128,512]{1,0:T(8,128)(2,1)} %refs_0_.1), channel_id=1, source_target_pairs={{0,4},{1,5},{2,6},{3,7},{4,0},{5,1},{6,2},{7,3},{8,12},{9,13},{10,... | collective-permute-start | bytes 393224 | tf_op jit(solution)/shard_map/ppermute | solution.py:321
  5.6 1.3 %collective-permute-start.5 = (bf16[128,512]{1,0:T(8,128)(2,1)}, bf16[128,512]{1,0:T(8,128)(2,1)S(1)}, u32[]{:S(2)}, u32[]{:S(2)}) collective-permute-start(bf16[128,512]{1,0:T(8,128)(2,1)} %refs_0_.1), channel_id=1, source_target_pairs={{0,6},{1,7},{2,0},{3,1},{4,2},{5,3},{6,4},{7,5},{8,14},{9,15},{10,... | collective-permute-start | bytes 393224 | tf_op jit(solution)/shard_map/ppermute | solution.py:321
  7.0 7.2 %load.1 = (bf16[256,512]{1,0:T(8,128)(2,1)S(1)}, bf16[3,4096,512]{2,1,0:T(8,128)(2,1)S(1)}, bf16[512,4096]{1,0:T(8,128)(2,1)S(1)}) custom-call(bf16[4096,512]{1,0:T(8,128)(2,1)} %w_pos.1, bf16[3,4096,512]{2,1,0:T(8,128)(2,1)} %w_qkv.1, bf16[512,4096]{1,0:T(8,128)(2,1)} %w_out.1), custom_call_target="tpu_custom_call" | custom-call | flops 1048576 | bytes 1048576 | tf_op jit(solution)/shard_map/load/pallas_call | solution.py:94
  14.2 0.6 %collective-permute-start.2 = (bf16[128,512]{1,0:T(8,128)(2,1)S(1)}, bf16[128,512]{1,0:T(8,128)(2,1)S(1)}, u32[]{:S(2)}, u32[]{:S(2)}) collective-permute-start(bf16[128,512]{1,0:T(8,128)(2,1)S(1)} %collective-permute-done.1.mine_ref.refs_2_), channel_id=1, source_target_pairs={{0,1},{1,0},{2,3},{3,2},{4,5},{5,4},{6,7},{7,6},{8,9},{9,8},{10,11... | collective-permute-start | bytes 393224 | tf_op jit(solution)/shard_map/ppermute | solution.py:324
  14.8 0.4 collective-permute-start.6
  15.3 0.5 %kv_step.4.refs_0_ = f32[2,128,512]{2,1,0:T(8,128)S(1)} custom-call(bf16[128,512]{1,0:T(8,128)(2,1)S(1)} %copy-done, bf16[128,512]{1,0:T(8,128)(2,1)S(1)} %collective-permute-done.other_ref.refs_1_, bf16[3,4096,512]{2,1,0:T(8,128)(2,1)S(1)} %get-tuple-element.31.w_ref.refs_8_), custom_call_target="tpu_custom_call" | custom-call | flops 65536 | bytes 65536 | tf_op jit(solution)/shard_map/kv_step/pallas_call | solution.py:153
  15.7 0.5 %kv_step.5.refs_0_ = f32[2,128,512]{2,1,0:T(8,128)S(1)} custom-call(bf16[128,512]{1,0:T(8,128)(2,1)S(1)} %collective-permute-done.1.mine_ref.refs_2_, bf16[128,512]{1,0:T(8,128)(2,1)S(1)} %collective-permute-done.2.other_ref.refs_3_, bf16[3,4096,512]{2,1,0:T(8,128)(2,1)S(1)} %get-tuple-element.31.w_ref.refs_8_, f32[2,128,512]{2,1,0:T(8,128)S(1)} %kv_step.4.refs_0_), custom_call_target="tpu_custom_call" | custom-call | flops 65536 | bytes 65536 | tf_op jit(solution)/shard_map/kv_step/pallas_call | solution.py:153
  16.2 0.5 %kv_step.6.refs_0_ = f32[2,128,512]{2,1,0:T(8,128)S(1)} custom-call(bf16[128,512]{1,0:T(8,128)(2,1)S(1)} %collective-permute-done.3.mine_ref.refs_4_, bf16[128,512]{1,0:T(8,128)(2,1)S(1)} %collective-permute-done.4.other_ref.refs_5_, bf16[3,4096,512]{2,1,0:T(8,128)(2,1)S(1)} %get-tuple-element.31.w_ref.refs_8_, f32[2,128,512]{2,1,0:T(8,128)S(1)} %kv_step.5.refs_0_), custom_call_target="tpu_custom_call" | custom-call | flops 65536 | bytes 65536 | tf_op jit(solution)/shard_map/kv_step/pallas_call | solution.py:153
  16.7 0.5 %kv_step.7 = (bf16[144,512]{1,0:T(8,128)(2,1)S(1)}, bf16[128,512]{1,0:T(8,128)(2,1)S(1)}) custom-call(bf16[128,512]{1,0:T(8,128)(2,1)S(1)} %collective-permute-done.5.mine_ref.refs_6_, bf16[128,512]{1,0:T(8,128)(2,1)S(1)} %collective-permute-done.6.other_ref.refs_7_, bf16[3,4096,512]{2,1,0:T(8,128)(2,1)S(1)} %get-tuple-element.31.w_ref.refs_8_, ...), custom_call_target="tpu_custom_call" | custom-call | flops 65536 | bytes 65536 | tf_op jit(solution)/shard_map/kv_step/pallas_call | solution.py:153
  17.2 1.5 %collective-permute-start.7 = (bf16[144,512]{1,0:T(8,128)(2,1)S(1)}, bf16[144,512]{1,0:T(8,128)(2,1)S(1)}, u32[]{:S(2)}, u32[]{:S(2)}) collective-permute-start(bf16[144,512]{1,0:T(8,128)(2,1)S(1)} %get-tuple-element.32.refs_11_), channel_id=1, source_target_pairs={{0,8},{8,16},{16,24},{24,0},{1,9},{9,17},{17,25},{25,1},{2,10},{10... | collective-permute-start | bytes 442376 | tf_op jit(solution)/shard_map/ppermute | solution.py:327
  18.7 1.5 %collective-permute-start.8 = (bf16[128,512]{1,0:T(8,128)(2,1)S(1)}, bf16[128,512]{1,0:T(8,128)(2,1)S(1)}, u32[]{:S(2)}, u32[]{:S(2)}) collective-permute-start(bf16[128,512]{1,0:T(8,128)(2,1)S(1)} %get-tuple-element.36.val_ref), channel_id=1, source_target_pairs={{0,8},{8,16},{16,24},{24,0},{1,9},{9,17},{17,25},{25,1},{2,10},{10... | collective-permute-start | bytes 393224 | tf_op jit(solution)/shard_map/ppermute | solution.py:327
  20.2 1.1 %queries.1 = (bf16[128,512]{1,0:T(8,128)(2,1)S(1)}, f32[4,128,256]{2,1,0:T(8,128)S(1)}) custom-call(bf16[128,512]{1,0:T(8,128)(2,1)S(1)} %copy-done, bf16[128,512]{1,0:T(8,128)(2,1)S(1)} %collective-permute-done.other_ref.refs_1_, bf16[128,512]{1,0:T(8,128)(2,1)S(1)} %collective-permute-done.1.mine_ref.refs_2_, ...), custom_call_target="tpu_custom_call" | custom-call | flops 536870912 | bytes 4194304 | tf_op jit(solution)/shard_map/queries/pallas_call | solution.py:198
  21.3 3.5 %collective-permute-done.7.mem_ref = bf16[144,512]{1,0:T(8,128)(2,1)S(1)} collective-permute-done((bf16[144,512]{1,0:T(8,128)(2,1)S(1)}, bf16[144,512]{1,0:T(8,128)(2,1)S(1)}, u32[]{:S(2)}, u32[]{:S(2)}) %collective-permute-start.7) | collective-permute-done | bytes 147488 | tf_op jit(solution)/shard_map/ppermute | solution.py:327
  24.8 1.5 %weigh.1 = (bf16[4,128,128]{2,1,0:T(8,128)(2,1)S(1)}, f32[128,512]{1,0:T(8,128)S(1)}) custom-call(bf16[128,512]{1,0:T(8,128)(2,1)S(1)} %get-tuple-element.34.qc_ref, f32[4,128,256]{2,1,0:T(8,128)S(1)} %get-tuple-element.35.score_ref, bf16[144,512]{1,0:T(8,128)(2,1)S(1)} %collective-permute-done.7.mem_ref, bf16[128,512]{1,0:T(8,128)(2,1)S(1)} %get-tuple-element.36.val_ref, ...), custom_call_target="tpu_custom_call" | custom-call | flops 67108864 | bytes 524288 | tf_op jit(solution)/shard_map/weigh/pallas_call | solution.py:242
  26.3 0.7 %collective-permute-done.8.mem_ref = bf16[128,512]{1,0:T(8,128)(2,1)S(1)} collective-permute-done((bf16[128,512]{1,0:T(8,128)(2,1)S(1)}, bf16[128,512]{1,0:T(8,128)(2,1)S(1)}, u32[]{:S(2)}, u32[]{:S(2)}) %collective-permute-start.8) | collective-permute-done | bytes 131104 | tf_op jit(solution)/shard_map/ppermute | solution.py:327
  27.4 0.6 %rest.1 = (bf16[3,128,512]{2,1,0:T(8,128)(2,1)S(1)}, f32[3,128,512]{2,1,0:T(8,128)S(1)}) custom-call(bf16[128,512]{1,0:T(8,128)(2,1)S(1)} %get-tuple-element.40.head_ref, bf16[512,4096]{1,0:T(8,128)(2,1)S(1)} %get-tuple-element.39.w_ref), custom_call_target="tpu_custom_call" | custom-call | flops 402653184 | bytes 3145728 | tf_op jit(solution)/shard_map/rest/pallas_call | solution.py:302
  28.1 0.5 %collective-permute-start.10 = (bf16[1,128,512]{2,1,0:T(8,128)(2,1)S(1)}, bf16[1,128,512]{2,1,0:T(8,128)(2,1)S(1)}, u32[]{:S(2)}, u32[]{:S(2)}) collective-permute-start(bf16[1,128,512]{2,1,0:T(8,128)(2,1)S(1)} %get-tuple-element.44), channel_id=1, source_target_pairs={{0,1},{1,0},{2,3},{3,2},{4,5},{5,4},{6,7},{7,6},{8,9},{9,8},{10,11... | collective-permute-start | bytes 393224 | tf_op jit(solution)/shard_map/ppermute | solution.py:324
  28.6 1.4 %collective-permute-done.10 = bf16[1,128,512]{2,1,0:T(8,128)(2,1)S(1)} collective-permute-done((bf16[1,128,512]{2,1,0:T(8,128)(2,1)S(1)}, bf16[1,128,512]{2,1,0:T(8,128)(2,1)S(1)}, u32[]{:S(2)}, u32[]{:S(2)}) %collective-permute-start.10) | collective-permute-done | bytes 131104 | tf_op jit(solution)/shard_map/ppermute | solution.py:324
  30.1 1.9 %collective-permute-start.11 = (bf16[128,512]{1,0:T(8,128)(2,1)S(1)}, bf16[128,512]{1,0:T(8,128)(2,1)S(1)}, u32[]{:S(2)}, u32[]{:S(2)}) collective-permute-start(bf16[128,512]{1,0:T(8,128)(2,1)S(1)} %fusion.7), channel_id=1, source_target_pairs={{0,4},{1,5},{2,6},{3,7},{4,0},{5,1},{6,2},{7,3},{8,12},{9,13},{10,... | collective-permute-start | bytes 393224 | tf_op jit(solution)/shard_map/ppermute | solution.py:321
  32.2 2.6 %collective-permute-start.12 = (bf16[128,512]{1,0:T(8,128)(2,1)S(1)}, bf16[128,512]{1,0:T(8,128)(2,1)S(1)}, u32[]{:S(2)}, u32[]{:S(2)}) collective-permute-start(bf16[128,512]{1,0:T(8,128)(2,1)S(1)} %get-tuple-element.45), channel_id=1, source_target_pairs={{0,2},{1,3},{2,4},{3,5},{4,6},{5,7},{6,0},{7,1},{8,10},{9,11},{10,... | collective-permute-start | bytes 393224 | tf_op jit(solution)/shard_map/ppermute | solution.py:321
  34.7 1.3 %collective-permute-start.13 = (bf16[128,512]{1,0:T(8,128)(2,1)S(1)}, bf16[128,512]{1,0:T(8,128)(2,1)S(1)}, u32[]{:S(2)}, u32[]{:S(2)}) collective-permute-start(bf16[128,512]{1,0:T(8,128)(2,1)S(1)} %get-tuple-element.46), channel_id=1, source_target_pairs={{0,6},{1,7},{2,0},{3,1},{4,2},{5,3},{6,4},{7,5},{8,14},{9,15},{10,... | collective-permute-start | bytes 393224 | tf_op jit(solution)/shard_map/ppermute | solution.py:321
  36.1 6.6 %collective-permute-done.11 = bf16[128,512]{1,0:T(8,128)(2,1)S(1)} collective-permute-done((bf16[128,512]{1,0:T(8,128)(2,1)S(1)}, bf16[128,512]{1,0:T(8,128)(2,1)S(1)}, u32[]{:S(2)}, u32[]{:S(2)}) %collective-permute-start.11) | collective-permute-done | bytes 131104 | tf_op jit(solution)/shard_map/ppermute | solution.py:321
  43.0 0.7 %fusion.6 = bf16[128,512]{1,0:T(8,128)(2,1)} fusion(f32[3,128,512]{2,1,0:T(8,128)S(1)} %convert_element_type.41, bf16[128,512]{1,0:T(8,128)(2,1)S(1)} %collective-permute-done.13, bf16[128,512]{1,0:T(8,128)(2,1)S(1)} %collective-permute-done.12, bf16[128,512]{1,0:T(8,128)(2,1)S(1)} %collective-permute-done.11, f32[3,128,512]{2,1,0:T(8,128)S(1)} %get-tuple-element.41), kind=kLoop, calls=%fused_computation.9 | loop fusion | flops 524288 | bytes 1048576 | tf_op jit(solution)/shard_map/convert_element_type | solution.py:363
  (26 shorter events, 1.2 us)
Async XLA Ops:
  0.0 15.3 %copy-start = (bf16[128,512]{1,0:T(8,128)(2,1)S(1)}, bf16[128,512]{1,0:T(8,128)(2,1)}, u32[]{:S(2)}) copy-start(bf16[128,512]{1,0:T(8,128)(2,1)} %refs_0_.1) | copy-start | bytes 393220
  0.0 15.2 %copy-start.3 = (s32[128]{0:T(128)S(1)}, s32[128]{0:T(128)}, u32[]{:S(2)}) copy-start(s32[128]{0:T(128)} %param.13) | copy-start | bytes 1540
  0.0 14.1 %collective-permute-start.1 = (bf16[128,512]{1,0:T(8,128)(2,1)}, bf16[128,512]{1,0:T(8,128)(2,1)S(1)}, u32[]{:S(2)}, u32[]{:S(2)}) collective-permute-start(bf16[128,512]{1,0:T(8,128)(2,1)} %refs_0_.1), channel_id=1, source_target_pairs={{0,2},{1,3},{2,4},{3,5},{4,6},{5,7},{6,0},{7,1},{8,10},{9,11},{10,... | collective-permute-start | bytes 393224 | tf_op jit(solution)/shard_map/ppermute | solution.py:321
  3.0 11.7 %collective-permute-start.3 = (bf16[128,512]{1,0:T(8,128)(2,1)}, bf16[128,512]{1,0:T(8,128)(2,1)S(1)}, u32[]{:S(2)}, u32[]{:S(2)}) collective-permute-start(bf16[128,512]{1,0:T(8,128)(2,1)} %refs_0_.1), channel_id=1, source_target_pairs={{0,4},{1,5},{2,6},{3,7},{4,0},{5,1},{6,2},{7,3},{8,12},{9,13},{10,... | collective-permute-start | bytes 393224 | tf_op jit(solution)/shard_map/ppermute | solution.py:321
  5.6 9.2 %collective-permute-start.5 = (bf16[128,512]{1,0:T(8,128)(2,1)}, bf16[128,512]{1,0:T(8,128)(2,1)S(1)}, u32[]{:S(2)}, u32[]{:S(2)}) collective-permute-start(bf16[128,512]{1,0:T(8,128)(2,1)} %refs_0_.1), channel_id=1, source_target_pairs={{0,6},{1,7},{2,0},{3,1},{4,2},{5,3},{6,4},{7,5},{8,14},{9,15},{10,... | collective-permute-start | bytes 393224 | tf_op jit(solution)/shard_map/ppermute | solution.py:321
  7.0 8.3 %collective-permute-start = (bf16[128,512]{1,0:T(8,128)(2,1)}, bf16[128,512]{1,0:T(8,128)(2,1)S(1)}, u32[]{:S(2)}, u32[]{:S(2)}) collective-permute-start(bf16[128,512]{1,0:T(8,128)(2,1)} %refs_0_.1), channel_id=1, source_target_pairs={{0,1},{1,0},{2,3},{3,2},{4,5},{5,4},{6,7},{7,6},{8,9},{9,8},{10,11... | collective-permute-start | bytes 393224 | tf_op jit(solution)/shard_map/ppermute | solution.py:324
  14.2 1.6 %collective-permute-start.2 = (bf16[128,512]{1,0:T(8,128)(2,1)S(1)}, bf16[128,512]{1,0:T(8,128)(2,1)S(1)}, u32[]{:S(2)}, u32[]{:S(2)}) collective-permute-start(bf16[128,512]{1,0:T(8,128)(2,1)S(1)} %collective-permute-done.1.mine_ref.refs_2_), channel_id=1, source_target_pairs={{0,1},{1,0},{2,3},{3,2},{4,5},{5,4},{6,7},{7,6},{8,9},{9,8},{10,11... | collective-permute-start | bytes 393224 | tf_op jit(solution)/shard_map/ppermute | solution.py:324
  14.7 1.5 %collective-permute-start.4 = (bf16[128,512]{1,0:T(8,128)(2,1)S(1)}, bf16[128,512]{1,0:T(8,128)(2,1)S(1)}, u32[]{:S(2)}, u32[]{:S(2)}) collective-permute-start(bf16[128,512]{1,0:T(8,128)(2,1)S(1)} %collective-permute-done.3.mine_ref.refs_4_), channel_id=1, source_target_pairs={{0,1},{1,0},{2,3},{3,2},{4,5},{5,4},{6,7},{7,6},{8,9},{9,8},{10,11... | collective-permute-start | bytes 393224 | tf_op jit(solution)/shard_map/ppermute | solution.py:324
  14.8 1.9 %collective-permute-start.6 = (bf16[128,512]{1,0:T(8,128)(2,1)S(1)}, bf16[128,512]{1,0:T(8,128)(2,1)S(1)}, u32[]{:S(2)}, u32[]{:S(2)}) collective-permute-start(bf16[128,512]{1,0:T(8,128)(2,1)S(1)} %collective-permute-done.5.mine_ref.refs_6_), channel_id=1, source_target_pairs={{0,1},{1,0},{2,3},{3,2},{4,5},{5,4},{6,7},{7,6},{8,9},{9,8},{10,11... | collective-permute-start | bytes 393224 | tf_op jit(solution)/shard_map/ppermute | solution.py:324
  16.7 3.5 %copy-start.1 = (f32[4,128]{1,0:T(4,128)S(1)}, f32[4,128]{1,0:T(4,128)}, u32[]{:S(2)}) copy-start(f32[4,128]{1,0:T(4,128)} %param.11) | copy-start | bytes 6148
  16.7 3.5 %copy-start.2 = (f32[4,128]{1,0:T(4,128)S(1)}, f32[4,128]{1,0:T(4,128)}, u32[]{:S(2)}) copy-start(f32[4,128]{1,0:T(4,128)} %param.12) | copy-start | bytes 6148
  17.2 7.6 %collective-permute-start.7 = (bf16[144,512]{1,0:T(8,128)(2,1)S(1)}, bf16[144,512]{1,0:T(8,128)(2,1)S(1)}, u32[]{:S(2)}, u32[]{:S(2)}) collective-permute-start(bf16[144,512]{1,0:T(8,128)(2,1)S(1)} %get-tuple-element.32.refs_11_), channel_id=1, source_target_pairs={{0,8},{8,16},{16,24},{24,0},{1,9},{9,17},{17,25},{25,1},{2,10},{10... | collective-permute-start | bytes 442376 | tf_op jit(solution)/shard_map/ppermute | solution.py:327
  18.7 8.3 %collective-permute-start.8 = (bf16[128,512]{1,0:T(8,128)(2,1)S(1)}, bf16[128,512]{1,0:T(8,128)(2,1)S(1)}, u32[]{:S(2)}, u32[]{:S(2)}) collective-permute-start(bf16[128,512]{1,0:T(8,128)(2,1)S(1)} %get-tuple-element.36.val_ref), channel_id=1, source_target_pairs={{0,8},{8,16},{16,24},{24,0},{1,9},{9,17},{17,25},{25,1},{2,10},{10... | collective-permute-start | bytes 393224 | tf_op jit(solution)/shard_map/ppermute | solution.py:327
  28.1 3.9 %collective-permute-start.9 = (bf16[3,128,512]{2,1,0:T(8,128)(2,1)S(1)}, bf16[3,128,512]{2,1,0:T(8,128)(2,1)S(1)}, u32[]{:S(2)}, u32[]{:S(2)}) collective-permute-start(bf16[3,128,512]{2,1,0:T(8,128)(2,1)S(1)} %get-tuple-element.42), channel_id=1, source_target_pairs={{0,1},{1,0},{2,3},{3,2},{4,5},{5,4},{6,7},{7,6},{8,9},{9,8},{10,11... | collective-permute-start | bytes 1179656 | tf_op jit(solution)/shard_map/ppermute | solution.py:324
  28.1 1.9 %collective-permute-start.10 = (bf16[1,128,512]{2,1,0:T(8,128)(2,1)S(1)}, bf16[1,128,512]{2,1,0:T(8,128)(2,1)S(1)}, u32[]{:S(2)}, u32[]{:S(2)}) collective-permute-start(bf16[1,128,512]{2,1,0:T(8,128)(2,1)S(1)} %get-tuple-element.44), channel_id=1, source_target_pairs={{0,1},{1,0},{2,3},{3,2},{4,5},{5,4},{6,7},{7,6},{8,9},{9,8},{10,11... | collective-permute-start | bytes 393224 | tf_op jit(solution)/shard_map/ppermute | solution.py:324
  30.1 12.6 %collective-permute-start.11 = (bf16[128,512]{1,0:T(8,128)(2,1)S(1)}, bf16[128,512]{1,0:T(8,128)(2,1)S(1)}, u32[]{:S(2)}, u32[]{:S(2)}) collective-permute-start(bf16[128,512]{1,0:T(8,128)(2,1)S(1)} %fusion.7), channel_id=1, source_target_pairs={{0,4},{1,5},{2,6},{3,7},{4,0},{5,1},{6,2},{7,3},{8,12},{9,13},{10,... | collective-permute-start | bytes 393224 | tf_op jit(solution)/shard_map/ppermute | solution.py:321
  32.2 10.5 %collective-permute-start.12 = (bf16[128,512]{1,0:T(8,128)(2,1)S(1)}, bf16[128,512]{1,0:T(8,128)(2,1)S(1)}, u32[]{:S(2)}, u32[]{:S(2)}) collective-permute-start(bf16[128,512]{1,0:T(8,128)(2,1)S(1)} %get-tuple-element.45), channel_id=1, source_target_pairs={{0,2},{1,3},{2,4},{3,5},{4,6},{5,7},{6,0},{7,1},{8,10},{9,11},{10,... | collective-permute-start | bytes 393224 | tf_op jit(solution)/shard_map/ppermute | solution.py:321
  34.7 8.3 %collective-permute-start.13 = (bf16[128,512]{1,0:T(8,128)(2,1)S(1)}, bf16[128,512]{1,0:T(8,128)(2,1)S(1)}, u32[]{:S(2)}, u32[]{:S(2)}) collective-permute-start(bf16[128,512]{1,0:T(8,128)(2,1)S(1)} %get-tuple-element.46), channel_id=1, source_target_pairs={{0,6},{1,7},{2,0},{3,1},{4,2},{5,3},{6,4},{7,5},{8,14},{9,15},{10,... | collective-permute-start | bytes 393224 | tf_op jit(solution)/shard_map/ppermute | solution.py:321

commit v5 on v4

--- a/solution.py
+++ b/solution.py
@@ -48,7 +48,7 @@
     return lax.dot_general(a, b, (((1,), (1,)), ((), ())), preferred_element_type=F32)
 
 
-def load_kernel(parts, w_pos, w_qkv, w_out, rel_ref, qkv_ref, out_ref, wbuf, table, sems):
+def load_kernel(parts, w_pos, w_qkv, rel_ref, kv_ref, wbuf, table, sems):
     rows, cols = rel_ref.shape
     width = w_pos.shape[0]
     half = width // 2
@@ -59,9 +59,8 @@
         return pltpu.make_async_copy(w_pos.at[part], wbuf.at[part], sems.at[i])
 
     copies = [pos_copy(i) for i in range(parts)]
-    for c in (1, 2, 0):
-        copies.append(pltpu.make_async_copy(w_qkv.at[c], qkv_ref.at[c], sems.at[parts + c]))
-    copies.append(pltpu.make_async_copy(w_out, out_ref, sems.at[parts + 3]))
+    for c in range(2):
+        copies.append(pltpu.make_async_copy(w_qkv.at[c + 1], kv_ref.at[c], sems.at[parts + c]))
     for item in copies:
         item.start()
     fine = 16
@@ -88,26 +87,22 @@
         item.wait()
 
 
-def load(w_pos, w_qkv, w_out, rows):
+def load(w_pos, w_qkv, rows):
     width, cols = w_pos.shape
     parts = 8
     return call(
         functools.partial(load_kernel, parts),
-        (
-            pltpu.VMEM((rows, cols), BF16),
-            pltpu.VMEM(w_qkv.shape, BF16),
-            pltpu.VMEM(w_out.shape, BF16),
-        ),
-        [hbm_spec()] * 3,
+        (pltpu.VMEM((rows, cols), BF16), pltpu.VMEM((2, width, cols), BF16)),
+        [hbm_spec()] * 2,
         [
             pltpu.VMEM((width, cols), BF16),
             pltpu.VMEM((rows, width), BF16),
-            pltpu.SemaphoreType.DMA((parts + 4,)),
+            pltpu.SemaphoreType.DMA((parts + 2,)),
         ],
         rows * width,
         rows * width,
         "load",
-    )(in_hbm(w_pos), in_hbm(w_qkv), in_hbm(w_out))
+    )(in_hbm(w_pos), in_hbm(w_qkv))
 
 
 def here(back):
@@ -120,57 +115,77 @@
     return 2 * place + (core if i == 0 else 1 - core)
 
 
-def kv_kernel(first, last, back, mine_ref, other_ref, w_ref, *refs):
+def kv_kernel(sources, kinds, first, last, *refs):
     refs = list(refs)
+    x_refs = [refs.pop(0) for _ in sources]
+    w_ref = refs.pop(0)
     acc_ref = None if first else refs.pop(0)
-    doc_ref = refs.pop(0) if last else None
-    rows, depth = mine_ref.shape
-    core, place = here(back)
-    for c in range(2):
-        total = None if first else acc_ref[c]
-        for i, x_ref in enumerate((mine_ref, other_ref)):
+    doc_ref = refs.pop(0) if last == "keys" else None
+    (out_ref,) = refs
+    rows, depth = x_refs[0].shape
+    for kind in kinds:
+        total = None if first else acc_ref[kind - 1]
+        for (back, i), x_ref in zip(sources, x_refs):
+            core, place = here(back)
             start = pl.multiple_of(row_block(core, place, i) * depth, depth)
-            term = dot(x_ref[...], w_ref[c + 1, pl.ds(start, depth)])
+            term = dot(x_ref[...], w_ref[kind - 1, pl.ds(start, depth)])
             total = term if total is None else total + term
-        if last:
-            refs[c][:rows] = total.astype(BF16)
+        if last == "keys":
+            head_dim = out_ref.shape[1]
+            for h in range(total.shape[1] // head_dim):
+                part = total[:, h * head_dim : (h + 1) * head_dim]
+                out_ref[h * rows : (h + 1) * rows] = part.astype(BF16)
+            docs = jnp.broadcast_to(doc_ref[...], (16, rows)).astype(BF16)
+            out_ref[out_ref.shape[0] - 16 :] = docs
+        elif last == "values":
+            out_ref[...] = total.astype(BF16)
         else:
-            refs[0][c] = total
-    if last:
-        key_ref = refs[0]
-        key_ref[rows:] = jnp.zeros((16, key_ref.shape[1]), BF16)
-        key_ref[rows:, :rows] = jnp.broadcast_to(doc_ref[...], (16, rows)).astype(BF16)
-
-
-def kv_step(back, mine, other, w_qkv, acc, docs):
-    rows, depth = mine.shape
+            out_ref[kind - 1] = total
+
+
+def kv_step(chunks, w_qkv, acc, kinds=(1, 2), last=None, docs=None, heads=None):
+    sources = tuple(chunks)
+    rows, depth = chunks[sources[0]].shape
     cols = w_qkv.shape[2]
-    first, last = acc is None, docs is not None
-    args = [mine, other, w_qkv] + ([] if first else [acc]) + ([docs] if last else [])
+    args = [chunks[source] for source in sources] + [w_qkv]
+    args += ([] if acc is None else [acc]) + ([] if docs is None else [docs])
     out = pltpu.VMEM((2, rows, cols), F32)
-    if last:
-        out = (pltpu.VMEM((rows + 16, cols), BF16), pltpu.VMEM((rows, cols), BF16))
-    return call(
-        functools.partial(kv_kernel, first, last, back),
+    if last == "keys":
+        assert rows == cols // heads
+        out = pltpu.VMEM((heads * rows + 16, cols // heads), BF16)
+    elif last == "values":
+        out = pltpu.VMEM((rows, cols), BF16)
+    return call(
+        functools.partial(kv_kernel, sources, kinds, acc is None, last),
         out,
         [vmem_spec()] * len(args),
         [],
-        rows * depth,
-        rows * depth,
+        16 * rows * depth * cols,
+        0,
         "kv_step",
     )(*args)
 
 
 def q_kernel(count, heads, *refs):
     x_refs = refs[:count]
-    w_ref, cb_ref, pb_ref, key_ref, rel_ref, doc_ref, qc_ref, score_ref = refs[count:]
+    w_ref, w_out, cb_ref, pb_ref, key_ref, rel_ref, doc_ref = refs[count : count + 7]
+    qc_ref, score_ref, w_out_ref, wbuf, sems = refs[count + 7 :]
     rows, depth = x_refs[0].shape
     head_dim = qc_ref.shape[1] // heads
+
+    def copy(i):
+        core, place = here(i // 2)
+        start = pl.multiple_of(row_block(core, place, i % 2) * depth, depth)
+        return pltpu.make_async_copy(w_ref.at[0, pl.ds(start, depth)], wbuf.at[i], sems.at[i])
+
+    copies = [copy(i) for i in range(count)]
+    copies.append(pltpu.make_async_copy(w_out, w_out_ref, sems.at[count]))
+    for item in copies:
+        item.start()
     total = None
     for i in range(count):
-        core, place = here(i // 2)
-        start = pl.multiple_of(row_block(core, place, i % 2) * depth, depth)
-        term = dot(x_refs[i][...], w_ref[0, pl.ds(start, depth)])
+        copies[i].wait()
+        term = dot(x_refs[i][...], wbuf[i])
         total = term if total is None else total + term
     query_content = (total + cb_ref[...]).astype(BF16)
     query_pos = (total + pb_ref[...]).astype(BF16)
@@ -185,27 +200,33 @@
         pos = pltpu.roll(
             dot_nt(query_pos[:, part], rel_ref[:, part]), rows + 1, 1, stride=1, stride_axis=0
         )
-        content = dot_nt(query_content[:, part], key_ref[:rows, part])
+        content = dot_nt(query_content[:, part], key_ref[h * rows : (h + 1) * rows])
         score_ref[h, :, :rows] = pos[:, :rows]
         score_ref[h, :, rows:] = jnp.where(allowed, (content + pos[:, rows:]) * scale, -1e30)
-
-
-def queries(chunks, w_qkv, content_bias, position_bias, own_key, rel, docs):
+    copies[count].wait()
+
+
+def queries(chunks, w_qkv, w_out, content_bias, position_bias, own_key, rel, docs):
     count = len(chunks)
     rows, depth = chunks[0].shape
     cols = w_qkv.shape[2]
     heads = content_bias.shape[0]
     return call(
         functools.partial(q_kernel, count, heads),
-        (pltpu.VMEM((rows, cols), BF16), pltpu.VMEM((heads, rows, 2 * rows), F32)),
-        [vmem_spec()] * (count + 6),
-        [],
+        (
+            pltpu.VMEM((rows, cols), BF16),
+            pltpu.VMEM((heads, rows, 2 * rows), F32),
+            pltpu.VMEM(w_out.shape, BF16),
+        ),
+        [vmem_spec()] * count + [hbm_spec()] * 2 + [vmem_spec()] * 5,
+        [pltpu.VMEM((count, depth, cols), BF16), pltpu.SemaphoreType.DMA((count + 1,))],
         2 * count * rows * depth * cols,
         2 * count * depth * cols,
         "queries",
     )(
         *chunks,
-        w_qkv,
+        in_hbm(w_qkv),
+        in_hbm(w_out),
         content_bias.reshape(1, cols),
         position_bias.reshape(1, cols),
         own_key,
@@ -218,12 +239,13 @@
     heads, rows, _ = score_ref.shape
     head_dim = qc_ref.shape[1] // heads
     exists = jnp.minimum(lax.axis_index("seq"), 1).astype(F32)
-    mem_doc = jnp.broadcast_to(mem_ref[rows : rows + 1, :rows].astype(F32) * exists, (rows, rows))
+    mem_doc = mem_ref[heads * rows : heads * rows + 1].astype(F32) * exists
+    mem_doc = jnp.broadcast_to(mem_doc, (rows, rows))
     allowed = mem_doc == jnp.broadcast_to(doc_ref[...], (rows, rows)).T
     scale = 1.0 / (float(head_dim) ** 0.5)
     for h in range(heads):
         part = slice(h * head_dim, (h + 1) * head_dim)
-        content = dot_nt(qc_ref[:, part], mem_ref[:rows, part])
+        content = dot_nt(qc_ref[:, part], mem_ref[h * rows : (h + 1) * rows])
         mem = jnp.where(allowed, (content + score_ref[h, :, :rows]) * scale, -1e30)
         own = score_ref[h, :, rows:]
         top = jnp.maximum(
@@ -329,18 +351,24 @@
     mine = [tokens] + [across(tokens, k) for k in range(1, chips)]
     other = [swap(tokens)]
     docs = (doc_ids + 1).astype(F32).reshape(1, rows)
-    rel, w_qkv, w_out = load(w_pos, w_qkv, w_out, 2 * rows)
+    rel, w_kv = load(w_pos, w_qkv, 2 * rows)
     for k in range(1, chips):
         mine[k], rel = lax.optimization_barrier((mine[k], rel))
         other.append(swap(mine[k]))
+    last = chips - 1
     acc = None
-    for k in range(chips):
-        acc = kv_step(k, mine[k], other[k], w_qkv, acc, docs if k == chips - 1 else None)
-    own_key, own_val = acc
-    mem_key, mem_val = onward(own_key), onward(own_val)
-    query_content, score = queries(
+    for k in range(last):
+        acc = kv_step({(k, 0): mine[k], (k, 1): other[k]}, w_kv, acc)
+    part = {(last, 0): mine[last], (last, 1): other[last]}
+    own_key = kv_step(part, w_kv, acc, (1,), "keys", docs, content_bias.shape[0])
+    mem_key = onward(own_key)
+    own_val = kv_step(part, w_kv, acc, (2,), "values")
+    mem_val = onward(own_val)
+    own_val, rel = lax.optimization_barrier((own_val, rel))
+    query_content, score, w_out = queries(
         [chunk for pair in zip(mine, other) for chunk in pair],
         w_qkv,
+        w_out,
         content_bias,
         position_bias,
         own_key,
@@ -353,6 +381,7 @@
     head_out, away, keep = mix(first, weights, out, mem_val, w_out, width)
     total = {first[0]: keep[0] + swap(away)[0].astype(F32)}
     away, keep = rest(others, head_out, w_out, width)
+    away, total[first[0]] = lax.optimization_barrier((away, total[first[0]]))
     away = swap(away).astype(F32)
     for i, k in enumerate(others):
         total[k] = keep[i] + away[i]

time: 43.9 us -> 42.8 us (0.975)
  waiting for transfers between devices: 12.7 us -> 11.6 us
  starting transfers between devices: 17.4 us -> 16.9 us
    ppermute x2, waiting for transfers between devices: 4.26 us -> 1.04 us  [onward(): lax.ppermute(value, 'seq', [(i, (i + 1) % segments) for i in range(segmen...]
    ppermute x6, waiting for transfers between devices: 6.98 us -> 9.8 us  [across(): lax.ppermute(value, 'mp', [(i, (i + 2 * k) % count) for i in range(count)])]
    pallas_call x1, Pallas kernels: 1.05 us -> 3.56 us  [queries(): call(functools.partial(q_kernel, count, heads), (pltpu.VMEM((rows, cols),...]
    pallas_call x1, Pallas kernels: 7.16 us -> 4.76 us  [load(): call(functools.partial(load_kernel, parts), (pltpu.VMEM((rows, cols), BF1...]
    ppermute x6, starting transfers between devices: 1.65 us -> 0.89 us  [swap(): return lax.ppermute(value, 'mp', [(i, i ^ 1) for i in range(count)])]
    ppermute x6, waiting for transfers between devices: 1.41 us -> 0.73 us  [swap(): return lax.ppermute(value, 'mp', [(i, i ^ 1) for i in range(count)])]
    pallas_call x4 -> x5, Pallas kernels: 1.85 us -> 2 us  [kv_step(): call(functools.partial(kv_kernel, sources, kinds, acc is None, last), out...]
  transfers between devices with their start and end apart: 14 -> 14, of which waited for: 5 -> 7; matrix products, arithmetic and copies ran while one was open for 0% -> 0% of each run, Pallas kernels for 25% -> 28%
where the time goes in v5:
time: 42.8 us; the launch traced here: 42.4 us
  starting transfers between devices  16.9 us (39%)
  Pallas kernels  12.8 us (30%)
  waiting for transfers between devices  11.6 us (27%)
  other arithmetic  0.96 us (2%)
    ppermute x6, starting transfers between devices, across(): lax.ppermute(value, 'mp', [(i, (i + 2 * k) % count) for i in range(count)])  12.9 us
    ppermute x6, waiting for transfers between devices, across(): lax.ppermute(value, 'mp', [(i, (i + 2 * k) % count) for i in range(count)])  9.8 us
    pallas_call x1, Pallas kernels, load(): call(functools.partial(load_kernel, parts), (pltpu.VMEM((rows, cols), BF1...  4.76 us
    pallas_call x1, Pallas kernels, queries(): call(functools.partial(q_kernel, count, heads), (pltpu.VMEM((rows, cols),...  3.56 us
    ppermute x2, starting transfers between devices, onward(): lax.ppermute(value, 'seq', [(i, (i + 1) % segments) for i in range(segmen...  3.08 us
    pallas_call x5, Pallas kernels, kv_step(): call(functools.partial(kv_kernel, sources, kinds, acc is None, last), out...  2 us
    pallas_call x1, Pallas kernels, weigh(): call(weigh_kernel, (pltpu.VMEM((heads, rows, rows), BF16), pltpu.VMEM((ro...  1.46 us
    ppermute x2, waiting for transfers between devices, onward(): lax.ppermute(value, 'seq', [(i, (i + 1) % segments) for i in range(segmen...  1.04 us
  transfers between devices with their start and end apart: 14, of which 7 were waited for; matrix products, arithmetic and copies ran while one was open for 0% of the time, Pallas kernels for 28%

profile of v5, /device:TPU:0, one launch (start us, length us, event | category | flops | bytes accessed | tf_op | source)
XLA Modules:
  0.0 42.4 jit_solution(16644579413429122638)
XLA Ops:
  0.0 3.0 %collective-permute-start.1 = (bf16[128,512]{1,0:T(8,128)(2,1)}, bf16[128,512]{1,0:T(8,128)(2,1)S(1)}, u32[]{:S(2)}, u32[]{:S(2)}) collective-permute-start(bf16[128,512]{1,0:T(8,128)(2,1)} %refs_0_.3), channel_id=1, source_target_pairs={{0,2},{1,3},{2,4},{3,5},{4,6},{5,7},{6,0},{7,1},{8,10},{9,11},{10,... | collective-permute-start | bytes 393224 | tf_op jit(solution)/shard_map/ppermute | solution.py:343
  3.0 2.6 %collective-permute-start.3 = (bf16[128,512]{1,0:T(8,128)(2,1)}, bf16[128,512]{1,0:T(8,128)(2,1)S(1)}, u32[]{:S(2)}, u32[]{:S(2)}) collective-permute-start(bf16[128,512]{1,0:T(8,128)(2,1)} %refs_0_.3), channel_id=1, source_target_pairs={{0,4},{1,5},{2,6},{3,7},{4,0},{5,1},{6,2},{7,3},{8,12},{9,13},{10,... | collective-permute-start | bytes 393224 | tf_op jit(solution)/shard_map/ppermute | solution.py:343
  5.6 1.3 %collective-permute-start.5 = (bf16[128,512]{1,0:T(8,128)(2,1)}, bf16[128,512]{1,0:T(8,128)(2,1)S(1)}, u32[]{:S(2)}, u32[]{:S(2)}) collective-permute-start(bf16[128,512]{1,0:T(8,128)(2,1)} %refs_0_.3), channel_id=1, source_target_pairs={{0,6},{1,7},{2,0},{3,1},{4,2},{5,3},{6,4},{7,5},{8,14},{9,15},{10,... | collective-permute-start | bytes 393224 | tf_op jit(solution)/shard_map/ppermute | solution.py:343
  7.0 4.8 %load.1 = (bf16[256,512]{1,0:T(8,128)(2,1)S(1)}, bf16[2,4096,512]{2,1,0:T(8,128)(2,1)S(1)}) custom-call(bf16[4096,512]{1,0:T(8,128)(2,1)} %w_pos.1, bf16[3,4096,512]{2,1,0:T(8,128)(2,1)} %refs_8_.1), custom_call_target="tpu_custom_call" | custom-call | flops 1048576 | bytes 1048576 | tf_op jit(solution)/shard_map/load/pallas_call | solution.py:93
  12.0 2.5 %collective-permute-done.3.refs_0_.refs_4_ = bf16[128,512]{1,0:T(8,128)(2,1)S(1)} collective-permute-done((bf16[128,512]{1,0:T(8,128)(2,1)}, bf16[128,512]{1,0:T(8,128)(2,1)S(1)}, u32[]{:S(2)}, u32[]{:S(2)}) %collective-permute-start.3) | collective-permute-done | bytes 131104 | tf_op jit(solution)/shard_map/ppermute | solution.py:343
  15.2 0.4 %kv_step.5.refs_3_ = f32[2,128,512]{2,1,0:T(8,128)S(1)} custom-call(bf16[128,512]{1,0:T(8,128)(2,1)S(1)} %copy-done, bf16[128,512]{1,0:T(8,128)(2,1)S(1)} %collective-permute-done.refs_1_, bf16[2,4096,512]{2,1,0:T(8,128)(2,1)S(1)} %get-tuple-element.33.refs_2_), custom_call_target="tpu_custom_call" | custom-call | flops 536870912 | tf_op jit(solution)/shard_map/kv_step/pallas_call | solution.py:158
  15.6 0.5 %kv_step.6.refs_3_ = f32[2,128,512]{2,1,0:T(8,128)S(1)} custom-call(bf16[128,512]{1,0:T(8,128)(2,1)S(1)} %collective-permute-done.1.refs_0_.refs_2_, bf16[128,512]{1,0:T(8,128)(2,1)S(1)} %collective-permute-done.2.refs_1_.refs_3_, bf16[2,4096,512]{2,1,0:T(8,128)(2,1)S(1)} %get-tuple-element.33.refs_2_, f32[2,128,512]{2,1,0:T(8,128)S(1)} %kv_step.5.refs_3_), custom_call_target="tpu_custom_call" | custom-call | flops 536870912 | tf_op jit(solution)/shard_map/kv_step/pallas_call | solution.py:158
  16.1 0.5 %kv_step.7.refs_3_ = f32[2,128,512]{2,1,0:T(8,128)S(1)} custom-call(bf16[128,512]{1,0:T(8,128)(2,1)S(1)} %collective-permute-done.3.refs_0_.refs_4_, bf16[128,512]{1,0:T(8,128)(2,1)S(1)} %collective-permute-done.4.refs_1_.refs_5_, bf16[2,4096,512]{2,1,0:T(8,128)(2,1)S(1)} %get-tuple-element.33.refs_2_, f32[2,128,512]{2,1,0:T(8,128)S(1)} %kv_step.6.refs_3_), custom_call_target="tpu_custom_call" | custom-call | flops 536870912 | tf_op jit(solution)/shard_map/kv_step/pallas_call | solution.py:158
  16.6 0.3 kv_step.8.refs_12_
  17.0 1.5 %collective-permute-start.7 = (bf16[528,128]{1,0:T(8,128)(2,1)S(1)}, bf16[528,128]{1,0:T(8,128)(2,1)S(1)}, u32[]{:S(2)}, u32[]{:S(2)}) collective-permute-start(bf16[528,128]{1,0:T(8,128)(2,1)S(1)} %kv_step.8.refs_12_), channel_id=1, source_target_pairs={{0,8},{8,16},{16,24},{24,0},{1,9},{9,17},{17,25},{25,1},{2,10},{10... | collective-permute-start | bytes 405512 | tf_op jit(solution)/shard_map/ppermute | solution.py:349
  18.8 1.5 %collective-permute-start.8 = (bf16[128,512]{1,0:T(8,128)(2,1)S(1)}, bf16[128,512]{1,0:T(8,128)(2,1)S(1)}, u32[]{:S(2)}, u32[]{:S(2)}) collective-permute-start(bf16[128,512]{1,0:T(8,128)(2,1)S(1)} %kv_step.9.val_ref), channel_id=1, source_target_pairs={{0,8},{8,16},{16,24},{24,0},{1,9},{9,17},{17,25},{25,1},{2,10},{10... | collective-permute-start | bytes 393224 | tf_op jit(solution)/shard_map/ppermute | solution.py:349
  20.4 3.6 %queries.1 = (bf16[128,512]{1,0:T(8,128)(2,1)S(1)}, f32[4,128,256]{2,1,0:T(8,128)S(1)}, bf16[512,4096]{1,0:T(8,128)(2,1)S(1)}) custom-call(bf16[128,512]{1,0:T(8,128)(2,1)S(1)} %copy-done, bf16[128,512]{1,0:T(8,128)(2,1)S(1)} %collective-permute-done.refs_1_, bf16[128,512]{1,0:T(8,128)(2,1)S(1)} %collective-permute-done.1.refs_0_.refs_2_, ...), custom_call_target="tpu_custom_call" | custom-call | flops 536870912 | bytes 4194304 | tf_op jit(solution)/shard_map/queries/pallas_call | solution.py:214
  23.9 0.4 collective-permute-done.7.mem_ref
  24.3 1.5 %weigh.1 = (bf16[4,128,128]{2,1,0:T(8,128)(2,1)S(1)}, f32[128,512]{1,0:T(8,128)S(1)}) custom-call(bf16[128,512]{1,0:T(8,128)(2,1)S(1)} %get-tuple-element.36.qc_ref, f32[4,128,256]{2,1,0:T(8,128)S(1)} %get-tuple-element.37.score_ref, bf16[528,128]{1,0:T(8,128)(2,1)S(1)} %collective-permute-done.7.mem_ref, bf16[128,512]{1,0:T(8,128)(2,1)S(1)} %kv_step.9.val_ref, ...), custom_call_target="tpu_custom_call" | custom-call | flops 67108864 | bytes 524288 | tf_op jit(solution)/shard_map/weigh/pallas_call | solution.py:264
  25.8 0.6 %collective-permute-done.8.mem_ref = bf16[128,512]{1,0:T(8,128)(2,1)S(1)} collective-permute-done((bf16[128,512]{1,0:T(8,128)(2,1)S(1)}, bf16[128,512]{1,0:T(8,128)(2,1)S(1)}, u32[]{:S(2)}, u32[]{:S(2)}) %collective-permute-start.8) | collective-permute-done | bytes 131104 | tf_op jit(solution)/shard_map/ppermute | solution.py:349
  26.4 0.4 mix.1
  26.9 0.6 %rest.1 = (bf16[3,128,512]{2,1,0:T(8,128)(2,1)S(1)}, f32[3,128,512]{2,1,0:T(8,128)S(1)}) custom-call(bf16[128,512]{1,0:T(8,128)(2,1)S(1)} %get-tuple-element.42.head_ref, bf16[512,4096]{1,0:T(8,128)(2,1)S(1)} %get-tuple-element.41.w_ref), custom_call_target="tpu_custom_call" | custom-call | flops 402653184 | bytes 3145728 | tf_op jit(solution)/shard_map/rest/pallas_call | solution.py:324
  27.5 0.7 %collective-permute-done.9 = bf16[1,128,512]{2,1,0:T(8,128)(2,1)S(1)} collective-permute-done((bf16[1,128,512]{2,1,0:T(8,128)(2,1)S(1)}, bf16[1,128,512]{2,1,0:T(8,128)(2,1)S(1)}, u32[]{:S(2)}, u32[]{:S(2)}) %collective-permute-start.9) | collective-permute-done | bytes 131104 | tf_op jit(solution)/shard_map/ppermute | solution.py:346
  28.5 2.1 %collective-permute-start.11 = (bf16[128,512]{1,0:T(8,128)(2,1)S(1)}, bf16[128,512]{1,0:T(8,128)(2,1)S(1)}, u32[]{:S(2)}, u32[]{:S(2)}) collective-permute-start(bf16[128,512]{1,0:T(8,128)(2,1)S(1)} %add_bitcast_fusion), channel_id=1, source_target_pairs={{0,4},{1,5},{2,6},{3,7},{4,0},{5,1},{6,2},{7,3},{8,12},{9,13},{10,... | collective-permute-start | bytes 393224 | tf_op jit(solution)/shard_map/ppermute | solution.py:343
  30.8 2.6 %collective-permute-start.12 = (bf16[128,512]{1,0:T(8,128)(2,1)S(1)}, bf16[128,512]{1,0:T(8,128)(2,1)S(1)}, u32[]{:S(2)}, u32[]{:S(2)}) collective-permute-start(bf16[128,512]{1,0:T(8,128)(2,1)S(1)} %get-tuple-element.49), channel_id=1, source_target_pairs={{0,2},{1,3},{2,4},{3,5},{4,6},{5,7},{6,0},{7,1},{8,10},{9,11},{10,... | collective-permute-start | bytes 393224 | tf_op jit(solution)/shard_map/ppermute | solution.py:343
  33.4 1.3 %collective-permute-start.13 = (bf16[128,512]{1,0:T(8,128)(2,1)S(1)}, bf16[128,512]{1,0:T(8,128)(2,1)S(1)}, u32[]{:S(2)}, u32[]{:S(2)}) collective-permute-start(bf16[128,512]{1,0:T(8,128)(2,1)S(1)} %get-tuple-element.50), channel_id=1, source_target_pairs={{0,6},{1,7},{2,0},{3,1},{4,2},{5,3},{6,4},{7,5},{8,14},{9,15},{10,... | collective-permute-start | bytes 393224 | tf_op jit(solution)/shard_map/ppermute | solution.py:343
  34.7 6.3 %collective-permute-done.11 = bf16[128,512]{1,0:T(8,128)(2,1)S(1)} collective-permute-done((bf16[128,512]{1,0:T(8,128)(2,1)S(1)}, bf16[128,512]{1,0:T(8,128)(2,1)S(1)}, u32[]{:S(2)}, u32[]{:S(2)}) %collective-permute-start.11) | collective-permute-done | bytes 131104 | tf_op jit(solution)/shard_map/ppermute | solution.py:343
  41.0 0.6 %collective-permute-done.13 = bf16[128,512]{1,0:T(8,128)(2,1)S(1)} collective-permute-done((bf16[128,512]{1,0:T(8,128)(2,1)S(1)}, bf16[128,512]{1,0:T(8,128)(2,1)S(1)}, u32[]{:S(2)}, u32[]{:S(2)}) %collective-permute-start.13) | collective-permute-done | bytes 131104 | tf_op jit(solution)/shard_map/ppermute | solution.py:343
  41.7 0.7 %fusion.6 = bf16[128,512]{1,0:T(8,128)(2,1)} fusion(f32[3,128,512]{2,1,0:T(8,128)S(1)} %convert_element_type.39, bf16[128,512]{1,0:T(8,128)(2,1)S(1)} %collective-permute-done.13, bf16[128,512]{1,0:T(8,128)(2,1)S(1)} %collective-permute-done.12, bf16[128,512]{1,0:T(8,128)(2,1)S(1)} %collective-permute-done.11, f32[3,128,512]{2,1,0:T(8,128)S(1)} %get-tuple-element.43), kind=kLoop, calls=%fused_computation.9 | loop fusion | flops 524288 | bytes 1048576 | tf_op jit(solution)/shard_map/convert_element_type | solution.py:392
  (27 shorter events, 1.7 us)
Async XLA Ops:
  0.0 15.2 %copy-start = (bf16[128,512]{1,0:T(8,128)(2,1)S(1)}, bf16[128,512]{1,0:T(8,128)(2,1)}, u32[]{:S(2)}) copy-start(bf16[128,512]{1,0:T(8,128)(2,1)} %refs_0_.3) | copy-start | bytes 393220
  0.0 14.6 %copy-start.3 = (s32[128]{0:T(128)S(1)}, s32[128]{0:T(128)}, u32[]{:S(2)}) copy-start(s32[128]{0:T(128)} %param.13) | copy-start | bytes 1540
  0.0 11.7 %collective-permute-start.1 = (bf16[128,512]{1,0:T(8,128)(2,1)}, bf16[128,512]{1,0:T(8,128)(2,1)S(1)}, u32[]{:S(2)}, u32[]{:S(2)}) collective-permute-start(bf16[128,512]{1,0:T(8,128)(2,1)} %refs_0_.3), channel_id=1, source_target_pairs={{0,2},{1,3},{2,4},{3,5},{4,6},{5,7},{6,0},{7,1},{8,10},{9,11},{10,... | collective-permute-start | bytes 393224 | tf_op jit(solution)/shard_map/ppermute | solution.py:343
  3.0 11.6 %collective-permute-start.3 = (bf16[128,512]{1,0:T(8,128)(2,1)}, bf16[128,512]{1,0:T(8,128)(2,1)S(1)}, u32[]{:S(2)}, u32[]{:S(2)}) collective-permute-start(bf16[128,512]{1,0:T(8,128)(2,1)} %refs_0_.3), channel_id=1, source_target_pairs={{0,4},{1,5},{2,6},{3,7},{4,0},{5,1},{6,2},{7,3},{8,12},{9,13},{10,... | collective-permute-start | bytes 393224 | tf_op jit(solution)/shard_map/ppermute | solution.py:343
  5.6 9.6 %collective-permute-start = (bf16[128,512]{1,0:T(8,128)(2,1)}, bf16[128,512]{1,0:T(8,128)(2,1)S(1)}, u32[]{:S(2)}, u32[]{:S(2)}) collective-permute-start(bf16[128,512]{1,0:T(8,128)(2,1)} %refs_0_.3), channel_id=1, source_target_pairs={{0,1},{1,0},{2,3},{3,2},{4,5},{5,4},{6,7},{7,6},{8,9},{9,8},{10,11... | collective-permute-start | bytes 393224 | tf_op jit(solution)/shard_map/ppermute | solution.py:346
  5.6 9.2 %collective-permute-start.5 = (bf16[128,512]{1,0:T(8,128)(2,1)}, bf16[128,512]{1,0:T(8,128)(2,1)S(1)}, u32[]{:S(2)}, u32[]{:S(2)}) collective-permute-start(bf16[128,512]{1,0:T(8,128)(2,1)} %refs_0_.3), channel_id=1, source_target_pairs={{0,6},{1,7},{2,0},{3,1},{4,2},{5,3},{6,4},{7,5},{8,14},{9,15},{10,... | collective-permute-start | bytes 393224 | tf_op jit(solution)/shard_map/ppermute | solution.py:343
  11.7 3.9 %collective-permute-start.2 = (bf16[128,512]{1,0:T(8,128)(2,1)S(1)}, bf16[128,512]{1,0:T(8,128)(2,1)S(1)}, u32[]{:S(2)}, u32[]{:S(2)}) collective-permute-start(bf16[128,512]{1,0:T(8,128)(2,1)S(1)} %collective-permute-done.1.refs_0_.refs_2_), channel_id=1, source_target_pairs={{0,1},{1,0},{2,3},{3,2},{4,5},{5,4},{6,7},{7,6},{8,9},{9,8},{10,11... | collective-permute-start | bytes 393224 | tf_op jit(solution)/shard_map/ppermute | solution.py:346
  14.6 1.5 %collective-permute-start.4 = (bf16[128,512]{1,0:T(8,128)(2,1)S(1)}, bf16[128,512]{1,0:T(8,128)(2,1)S(1)}, u32[]{:S(2)}, u32[]{:S(2)}) collective-permute-start(bf16[128,512]{1,0:T(8,128)(2,1)S(1)} %collective-permute-done.3.refs_0_.refs_4_), channel_id=1, source_target_pairs={{0,1},{1,0},{2,3},{3,2},{4,5},{5,4},{6,7},{7,6},{8,9},{9,8},{10,11... | collective-permute-start | bytes 393224 | tf_op jit(solution)/shard_map/ppermute | solution.py:346
  14.9 1.7 %collective-permute-start.6 = (bf16[128,512]{1,0:T(8,128)(2,1)S(1)}, bf16[128,512]{1,0:T(8,128)(2,1)S(1)}, u32[]{:S(2)}, u32[]{:S(2)}) collective-permute-start(bf16[128,512]{1,0:T(8,128)(2,1)S(1)} %collective-permute-done.5.refs_0_.refs_6_), channel_id=1, source_target_pairs={{0,1},{1,0},{2,3},{3,2},{4,5},{5,4},{6,7},{7,6},{8,9},{9,8},{10,11... | collective-permute-start | bytes 393224 | tf_op jit(solution)/shard_map/ppermute | solution.py:346
  16.9 3.4 %copy-start.1 = (f32[4,128]{1,0:T(4,128)S(1)}, f32[4,128]{1,0:T(4,128)}, u32[]{:S(2)}) copy-start(f32[4,128]{1,0:T(4,128)} %param.11) | copy-start | bytes 6148
  16.9 3.4 %copy-start.2 = (f32[4,128]{1,0:T(4,128)S(1)}, f32[4,128]{1,0:T(4,128)}, u32[]{:S(2)}) copy-start(f32[4,128]{1,0:T(4,128)} %param.12) | copy-start | bytes 6148
  17.0 7.4 %collective-permute-start.7 = (bf16[528,128]{1,0:T(8,128)(2,1)S(1)}, bf16[528,128]{1,0:T(8,128)(2,1)S(1)}, u32[]{:S(2)}, u32[]{:S(2)}) collective-permute-start(bf16[528,128]{1,0:T(8,128)(2,1)S(1)} %kv_step.8.refs_12_), channel_id=1, source_target_pairs={{0,8},{8,16},{16,24},{24,0},{1,9},{9,17},{17,25},{25,1},{2,10},{10... | collective-permute-start | bytes 405512 | tf_op jit(solution)/shard_map/ppermute | solution.py:349
  18.8 7.6 %collective-permute-start.8 = (bf16[128,512]{1,0:T(8,128)(2,1)S(1)}, bf16[128,512]{1,0:T(8,128)(2,1)S(1)}, u32[]{:S(2)}, u32[]{:S(2)}) collective-permute-start(bf16[128,512]{1,0:T(8,128)(2,1)S(1)} %kv_step.9.val_ref), channel_id=1, source_target_pairs={{0,8},{8,16},{16,24},{24,0},{1,9},{9,17},{17,25},{25,1},{2,10},{10... | collective-permute-start | bytes 393224 | tf_op jit(solution)/shard_map/ppermute | solution.py:349
  26.8 1.4 %collective-permute-start.9 = (bf16[1,128,512]{2,1,0:T(8,128)(2,1)S(1)}, bf16[1,128,512]{2,1,0:T(8,128)(2,1)S(1)}, u32[]{:S(2)}, u32[]{:S(2)}) collective-permute-start(bf16[1,128,512]{2,1,0:T(8,128)(2,1)S(1)} %get-tuple-element.46), channel_id=1, source_target_pairs={{0,1},{1,0},{2,3},{3,2},{4,5},{5,4},{6,7},{7,6},{8,9},{9,8},{10,11... | collective-permute-start | bytes 393224 | tf_op jit(solution)/shard_map/ppermute | solution.py:346
  28.3 2.3 %collective-permute-start.10 = (bf16[3,128,512]{2,1,0:T(8,128)(2,1)S(1)}, bf16[3,128,512]{2,1,0:T(8,128)(2,1)S(1)}, u32[]{:S(2)}, u32[]{:S(2)}) collective-permute-start(bf16[3,128,512]{2,1,0:T(8,128)(2,1)S(1)} %get-tuple-element.47), channel_id=1, source_target_pairs={{0,1},{1,0},{2,3},{3,2},{4,5},{5,4},{6,7},{7,6},{8,9},{9,8},{10,11... | collective-permute-start | bytes 1179656 | tf_op jit(solution)/shard_map/ppermute | solution.py:346
  28.5 12.5 %collective-permute-start.11 = (bf16[128,512]{1,0:T(8,128)(2,1)S(1)}, bf16[128,512]{1,0:T(8,128)(2,1)S(1)}, u32[]{:S(2)}, u32[]{:S(2)}) collective-permute-start(bf16[128,512]{1,0:T(8,128)(2,1)S(1)} %add_bitcast_fusion), channel_id=1, source_target_pairs={{0,4},{1,5},{2,6},{3,7},{4,0},{5,1},{6,2},{7,3},{8,12},{9,13},{10,... | collective-permute-start | bytes 393224 | tf_op jit(solution)/shard_map/ppermute | solution.py:343
  30.8 10.2 %collective-permute-start.12 = (bf16[128,512]{1,0:T(8,128)(2,1)S(1)}, bf16[128,512]{1,0:T(8,128)(2,1)S(1)}, u32[]{:S(2)}, u32[]{:S(2)}) collective-permute-start(bf16[128,512]{1,0:T(8,128)(2,1)S(1)} %get-tuple-element.49), channel_id=1, source_target_pairs={{0,2},{1,3},{2,4},{3,5},{4,6},{5,7},{6,0},{7,1},{8,10},{9,11},{10,... | collective-permute-start | bytes 393224 | tf_op jit(solution)/shard_map/ppermute | solution.py:343
  33.4 8.3 %collective-permute-start.13 = (bf16[128,512]{1,0:T(8,128)(2,1)S(1)}, bf16[128,512]{1,0:T(8,128)(2,1)S(1)}, u32[]{:S(2)}, u32[]{:S(2)}) collective-permute-start(bf16[128,512]{1,0:T(8,128)(2,1)S(1)} %get-tuple-element.50), channel_id=1, source_target_pairs={{0,6},{1,7},{2,0},{3,1},{4,2},{5,3},{6,4},{7,5},{8,14},{9,15},{10,... | collective-permute-start | bytes 393224 | tf_op jit(solution)/shard_map/ppermute | solution.py:343

commit v6 on v5

--- a/solution.py
+++ b/solution.py
@@ -272,62 +272,56 @@
     )(query_content, score, mem_key, own_val, docs)
 
 
-def blocks_out(offsets, head_out, w_ref, away_ref, keep_ref):
-    width = away_ref.shape[2]
+def blocks_out(away, offsets, head_out, w_ref, out_ref):
+    width = out_ref.shape[2]
     core, chip = here(0)
     chips = lax.axis_size("mp") // 2
-    for away in (True, False):
-        for i, k in enumerate(offsets):
-            block = 2 * lax.rem(chip + k, chips) + (1 - core if away else core)
-            start = pl.multiple_of(block * width, width)
-            term = dot(head_out, w_ref[:, pl.ds(start, width)])
-            if away:
-                away_ref[i] = term.astype(BF16)
-            else:
-                keep_ref[i] = term
-
-
-def mix_kernel(offsets, weight_ref, out_ref, mem_ref, w_ref, head_ref, away_ref, keep_ref):
+    for i, k in enumerate(offsets):
+        block = 2 * lax.rem(chip + k, chips) + (1 - core if away else core)
+        start = pl.multiple_of(block * width, width)
+        out_ref[i] = dot(head_out, w_ref[:, pl.ds(start, width)]).astype(out_ref.dtype)
+
+
+def mix_kernel(first, weight_ref, out_ref, mem_ref, w_ref, head_ref, away_ref):
     heads, rows, _ = weight_ref.shape
     head_dim = out_ref.shape[1] // heads
     for h in range(heads):
         part = slice(h * head_dim, (h + 1) * head_dim)
         out = out_ref[:, part] + dot(weight_ref[h], mem_ref[:, part])
         head_ref[:, part] = out.astype(BF16)
-    blocks_out(offsets, head_ref[...], w_ref, away_ref, keep_ref)
-
-
-def rest_kernel(offsets, head_ref, w_ref, away_ref, keep_ref):
-    blocks_out(offsets, head_ref[...], w_ref, away_ref, keep_ref)
-
-
-def block_shapes(offsets, rows, width):
-    count = len(offsets)
-    return (pltpu.VMEM((count, rows, width), BF16), pltpu.VMEM((count, rows, width), F32))
-
-
-def mix(offsets, weights, out, mem_val, w_out, width):
+    blocks_out(True, [first], head_ref[...], w_ref, away_ref)
+
+
+def mix(first, weights, out, mem_val, w_out, width):
     rows, cols = out.shape
     return call(
-        functools.partial(mix_kernel, offsets),
-        (pltpu.VMEM((rows, cols), BF16),) + block_shapes(offsets, rows, width),
+        functools.partial(mix_kernel, first),
+        (pltpu.VMEM((rows, cols), BF16), pltpu.VMEM((1, rows, width), BF16)),
         [vmem_spec()] * 4,
         [],
-        4 * rows * cols * width * len(offsets),
-        4 * cols * width * len(offsets),
+        2 * rows * cols * width,
+        2 * cols * width,
         "mix",
     )(weights, out, mem_val, w_out)
 
 
-def rest(offsets, head_out, w_out, width):
+def rest_kernel(others, kept, head_ref, w_ref, away_ref, keep_ref):
+    blocks_out(True, others, head_ref[...], w_ref, away_ref)
+    blocks_out(False, kept, head_ref[...], w_ref, keep_ref)
+
+
+def rest(others, kept, head_out, w_out, width):
     rows, cols = head_out.shape
     return call(
-        functools.partial(rest_kernel, offsets),
-        block_shapes(offsets, rows, width),
+        functools.partial(rest_kernel, others, kept),
+        (
+            pltpu.VMEM((len(others), rows, width), BF16),
+            pltpu.VMEM((len(kept), rows, width), F32),
+        ),
         [vmem_spec()] * 2,
         [],
-        4 * rows * cols * width * len(offsets),
-        4 * cols * width * len(offsets),
+        4 * rows * cols * width * len(kept),
+        4 * cols * width * len(kept),
         "rest",
     )(head_out, w_out)
 
@@ -376,17 +370,18 @@
         docs,
     )
     weights, out = weigh(query_content, score, mem_key, own_val, docs)
-    first = [chips // 2]
-    others = [k for k in range(chips) if k not in first]
-    head_out, away, keep = mix(first, weights, out, mem_val, w_out, width)
-    total = {first[0]: keep[0] + swap(away)[0].astype(F32)}
-    away, keep = rest(others, head_out, w_out, width)
-    away, total[first[0]] = lax.optimization_barrier((away, total[first[0]]))
-    away = swap(away).astype(F32)
+    first = chips // 2
+    others = [k for k in range(chips) if k != first]
+    head_out, away = mix(first, weights, out, mem_val, w_out, width)
+    swapped = swap(away)
+    away, keep = rest(others, [first] + others, head_out, w_out, width)
+    total = {first: keep[0] + swapped[0].astype(F32)}
+    away, total[first] = lax.optimization_barrier((away, total[first]))
+    away = swap(away)
     for i, k in enumerate(others):
-        total[k] = keep[i] + away[i]
+        total[k] = keep[i + 1] + away[i].astype(F32)
     result = total[0]
-    for k in first + others:
+    for k in [first] + others:
         if k > 0:
             result = result + across(total[k].astype(BF16), k).astype(F32)
     return result.astype(BF16)

time: 42.8 us -> 42.7 us (level)
  transfers between devices with their start and end apart: 14 -> 14, of which waited for: 7 -> 7; matrix products, arithmetic and copies ran while one was open for 0% -> 0% of each run, Pallas kernels for 28% -> 29%
where the time goes in v6:
time: 42.7 us; the launch traced here: 42.2 us
  starting transfers between devices  16.9 us (40%)
  Pallas kernels  12.8 us (30%)
  waiting for transfers between devices  11.5 us (27%)
  other arithmetic  0.84 us (2%)
    ppermute x6, starting transfers between devices, across(): lax.ppermute(value, 'mp', [(i, (i + 2 * k) % count) for i in range(count)])  12.9 us
    ppermute x6, waiting for transfers between devices, across(): lax.ppermute(value, 'mp', [(i, (i + 2 * k) % count) for i in range(count)])  9.8 us
    pallas_call x1, Pallas kernels, load(): call(functools.partial(load_kernel, parts), (pltpu.VMEM((rows, cols), BF1...  4.76 us
    pallas_call x1, Pallas kernels, queries(): call(functools.partial(q_kernel, count, heads), (pltpu.VMEM((rows, cols),...  3.56 us
    ppermute x2, starting transfers between devices, onward(): lax.ppermute(value, 'seq', [(i, (i + 1) % segments) for i in range(segmen...  3.08 us
    pallas_call x5, Pallas kernels, kv_step(): call(functools.partial(kv_kernel, sources, kinds, acc is None, last), out...  2 us
    pallas_call x1, Pallas kernels, weigh(): call(weigh_kernel, (pltpu.VMEM((heads, rows, rows), BF16), pltpu.VMEM((ro...  1.46 us
    ppermute x2, waiting for transfers between devices, onward(): lax.ppermute(value, 'seq', [(i, (i + 1) % segments) for i in range(segmen...  1.04 us
  transfers between devices with their start and end apart: 14, of which 7 were waited for; matrix products, arithmetic and copies ran while one was open for 0% of the time, Pallas kernels for 29%

profile of v6, /device:TPU:0, one launch (start us, length us, event | category | flops | bytes accessed | tf_op | source)
XLA Modules:
  0.0 42.2 jit_solution(16809617798915401012)
XLA Ops:
  0.0 3.0 %collective-permute-start.1 = (bf16[128,512]{1,0:T(8,128)(2,1)}, bf16[128,512]{1,0:T(8,128)(2,1)S(1)}, u32[]{:S(2)}, u32[]{:S(2)}) collective-permute-start(bf16[128,512]{1,0:T(8,128)(2,1)} %refs_0_.3), channel_id=1, source_target_pairs={{0,2},{1,3},{2,4},{3,5},{4,6},{5,7},{6,0},{7,1},{8,10},{9,11},{10,... | collective-permute-start | bytes 393224 | tf_op jit(solution)/shard_map/ppermute | solution.py:337
  3.0 2.6 %collective-permute-start.3 = (bf16[128,512]{1,0:T(8,128)(2,1)}, bf16[128,512]{1,0:T(8,128)(2,1)S(1)}, u32[]{:S(2)}, u32[]{:S(2)}) collective-permute-start(bf16[128,512]{1,0:T(8,128)(2,1)} %refs_0_.3), channel_id=1, source_target_pairs={{0,4},{1,5},{2,6},{3,7},{4,0},{5,1},{6,2},{7,3},{8,12},{9,13},{10,... | collective-permute-start | bytes 393224 | tf_op jit(solution)/shard_map/ppermute | solution.py:337
  5.6 1.3 %collective-permute-start.5 = (bf16[128,512]{1,0:T(8,128)(2,1)}, bf16[128,512]{1,0:T(8,128)(2,1)S(1)}, u32[]{:S(2)}, u32[]{:S(2)}) collective-permute-start(bf16[128,512]{1,0:T(8,128)(2,1)} %refs_0_.3), channel_id=1, source_target_pairs={{0,6},{1,7},{2,0},{3,1},{4,2},{5,3},{6,4},{7,5},{8,14},{9,15},{10,... | collective-permute-start | bytes 393224 | tf_op jit(solution)/shard_map/ppermute | solution.py:337
  7.0 4.8 %load.1 = (bf16[256,512]{1,0:T(8,128)(2,1)S(1)}, bf16[2,4096,512]{2,1,0:T(8,128)(2,1)S(1)}) custom-call(bf16[4096,512]{1,0:T(8,128)(2,1)} %w_pos.1, bf16[3,4096,512]{2,1,0:T(8,128)(2,1)} %refs_8_.1), custom_call_target="tpu_custom_call" | custom-call | flops 1048576 | bytes 1048576 | tf_op jit(solution)/shard_map/load/pallas_call | solution.py:93
  12.0 2.5 %collective-permute-done.3.refs_0_.refs_4_ = bf16[128,512]{1,0:T(8,128)(2,1)S(1)} collective-permute-done((bf16[128,512]{1,0:T(8,128)(2,1)}, bf16[128,512]{1,0:T(8,128)(2,1)S(1)}, u32[]{:S(2)}, u32[]{:S(2)}) %collective-permute-start.3) | collective-permute-done | bytes 131104 | tf_op jit(solution)/shard_map/ppermute | solution.py:337
  15.2 0.4 %kv_step.5.refs_3_ = f32[2,128,512]{2,1,0:T(8,128)S(1)} custom-call(bf16[128,512]{1,0:T(8,128)(2,1)S(1)} %copy-done, bf16[128,512]{1,0:T(8,128)(2,1)S(1)} %collective-permute-done.refs_1_, bf16[2,4096,512]{2,1,0:T(8,128)(2,1)S(1)} %get-tuple-element.32.refs_2_), custom_call_target="tpu_custom_call" | custom-call | flops 536870912 | tf_op jit(solution)/shard_map/kv_step/pallas_call | solution.py:158
  15.6 0.5 %kv_step.6.refs_3_ = f32[2,128,512]{2,1,0:T(8,128)S(1)} custom-call(bf16[128,512]{1,0:T(8,128)(2,1)S(1)} %collective-permute-done.1.refs_0_.refs_2_, bf16[128,512]{1,0:T(8,128)(2,1)S(1)} %collective-permute-done.2.refs_1_.refs_3_, bf16[2,4096,512]{2,1,0:T(8,128)(2,1)S(1)} %get-tuple-element.32.refs_2_, f32[2,128,512]{2,1,0:T(8,128)S(1)} %kv_step.5.refs_3_), custom_call_target="tpu_custom_call" | custom-call | flops 536870912 | tf_op jit(solution)/shard_map/kv_step/pallas_call | solution.py:158
  16.1 0.5 %kv_step.7.refs_3_ = f32[2,128,512]{2,1,0:T(8,128)S(1)} custom-call(bf16[128,512]{1,0:T(8,128)(2,1)S(1)} %collective-permute-done.3.refs_0_.refs_4_, bf16[128,512]{1,0:T(8,128)(2,1)S(1)} %collective-permute-done.4.refs_1_.refs_5_, bf16[2,4096,512]{2,1,0:T(8,128)(2,1)S(1)} %get-tuple-element.32.refs_2_, f32[2,128,512]{2,1,0:T(8,128)S(1)} %kv_step.6.refs_3_), custom_call_target="tpu_custom_call" | custom-call | flops 536870912 | tf_op jit(solution)/shard_map/kv_step/pallas_call | solution.py:158
  16.6 0.3 kv_step.8.refs_12_
  17.0 1.5 %collective-permute-start.7 = (bf16[528,128]{1,0:T(8,128)(2,1)S(1)}, bf16[528,128]{1,0:T(8,128)(2,1)S(1)}, u32[]{:S(2)}, u32[]{:S(2)}) collective-permute-start(bf16[528,128]{1,0:T(8,128)(2,1)S(1)} %kv_step.8.refs_12_), channel_id=1, source_target_pairs={{0,8},{8,16},{16,24},{24,0},{1,9},{9,17},{17,25},{25,1},{2,10},{10... | collective-permute-start | bytes 405512 | tf_op jit(solution)/shard_map/ppermute | solution.py:343
  18.8 1.5 %collective-permute-start.8 = (bf16[128,512]{1,0:T(8,128)(2,1)S(1)}, bf16[128,512]{1,0:T(8,128)(2,1)S(1)}, u32[]{:S(2)}, u32[]{:S(2)}) collective-permute-start(bf16[128,512]{1,0:T(8,128)(2,1)S(1)} %kv_step.9.val_ref), channel_id=1, source_target_pairs={{0,8},{8,16},{16,24},{24,0},{1,9},{9,17},{17,25},{25,1},{2,10},{10... | collective-permute-start | bytes 393224 | tf_op jit(solution)/shard_map/ppermute | solution.py:343
  20.4 3.6 %queries.1 = (bf16[128,512]{1,0:T(8,128)(2,1)S(1)}, f32[4,128,256]{2,1,0:T(8,128)S(1)}, bf16[512,4096]{1,0:T(8,128)(2,1)S(1)}) custom-call(bf16[128,512]{1,0:T(8,128)(2,1)S(1)} %copy-done, bf16[128,512]{1,0:T(8,128)(2,1)S(1)} %collective-permute-done.refs_1_, bf16[128,512]{1,0:T(8,128)(2,1)S(1)} %collective-permute-done.1.refs_0_.refs_2_, ...), custom_call_target="tpu_custom_call" | custom-call | flops 536870912 | bytes 4194304 | tf_op jit(solution)/shard_map/queries/pallas_call | solution.py:214
  23.9 0.4 collective-permute-done.7.mem_ref
  24.3 1.5 %weigh.1 = (bf16[4,128,128]{2,1,0:T(8,128)(2,1)S(1)}, f32[128,512]{1,0:T(8,128)S(1)}) custom-call(bf16[128,512]{1,0:T(8,128)(2,1)S(1)} %get-tuple-element.35.qc_ref, f32[4,128,256]{2,1,0:T(8,128)S(1)} %get-tuple-element.36.score_ref, bf16[528,128]{1,0:T(8,128)(2,1)S(1)} %collective-permute-done.7.mem_ref, bf16[128,512]{1,0:T(8,128)(2,1)S(1)} %kv_step.9.val_ref, ...), custom_call_target="tpu_custom_call" | custom-call | flops 67108864 | bytes 524288 | tf_op jit(solution)/shard_map/weigh/pallas_call | solution.py:264
  25.8 0.6 %collective-permute-done.8.mem_ref = bf16[128,512]{1,0:T(8,128)(2,1)S(1)} collective-permute-done((bf16[128,512]{1,0:T(8,128)(2,1)S(1)}, bf16[128,512]{1,0:T(8,128)(2,1)S(1)}, u32[]{:S(2)}, u32[]{:S(2)}) %collective-permute-start.8) | collective-permute-done | bytes 131104 | tf_op jit(solution)/shard_map/ppermute | solution.py:343
  26.4 0.3 mix.1
  26.9 0.7 %rest.1 = (bf16[3,128,512]{2,1,0:T(8,128)(2,1)S(1)}, f32[4,128,512]{2,1,0:T(8,128)S(1)}) custom-call(bf16[128,512]{1,0:T(8,128)(2,1)S(1)} %get-tuple-element.41.head_ref, bf16[512,4096]{1,0:T(8,128)(2,1)S(1)} %get-tuple-element.40.w_ref), custom_call_target="tpu_custom_call" | custom-call | flops 536870912 | bytes 4194304 | tf_op jit(solution)/shard_map/rest/pallas_call | solution.py:315
  27.5 0.7 %collective-permute-done.9 = bf16[1,128,512]{2,1,0:T(8,128)(2,1)S(1)} collective-permute-done((bf16[1,128,512]{2,1,0:T(8,128)(2,1)S(1)}, bf16[1,128,512]{2,1,0:T(8,128)(2,1)S(1)}, u32[]{:S(2)}, u32[]{:S(2)}) %collective-permute-start.9) | collective-permute-done | bytes 131104 | tf_op jit(solution)/shard_map/ppermute | solution.py:340
  28.4 2.1 %collective-permute-start.11 = (bf16[128,512]{1,0:T(8,128)(2,1)S(1)}, bf16[128,512]{1,0:T(8,128)(2,1)S(1)}, u32[]{:S(2)}, u32[]{:S(2)}) collective-permute-start(bf16[128,512]{1,0:T(8,128)(2,1)S(1)} %add_bitcast_fusion), channel_id=1, source_target_pairs={{0,4},{1,5},{2,6},{3,7},{4,0},{5,1},{6,2},{7,3},{8,12},{9,13},{10,... | collective-permute-start | bytes 393224 | tf_op jit(solution)/shard_map/ppermute | solution.py:337
  30.6 2.6 %collective-permute-start.12 = (bf16[128,512]{1,0:T(8,128)(2,1)S(1)}, bf16[128,512]{1,0:T(8,128)(2,1)S(1)}, u32[]{:S(2)}, u32[]{:S(2)}) collective-permute-start(bf16[128,512]{1,0:T(8,128)(2,1)S(1)} %get-tuple-element.47), channel_id=1, source_target_pairs={{0,2},{1,3},{2,4},{3,5},{4,6},{5,7},{6,0},{7,1},{8,10},{9,11},{10,... | collective-permute-start | bytes 393224 | tf_op jit(solution)/shard_map/ppermute | solution.py:337
  33.2 1.3 %collective-permute-start.13 = (bf16[128,512]{1,0:T(8,128)(2,1)S(1)}, bf16[128,512]{1,0:T(8,128)(2,1)S(1)}, u32[]{:S(2)}, u32[]{:S(2)}) collective-permute-start(bf16[128,512]{1,0:T(8,128)(2,1)S(1)} %get-tuple-element.48), channel_id=1, source_target_pairs={{0,6},{1,7},{2,0},{3,1},{4,2},{5,3},{6,4},{7,5},{8,14},{9,15},{10,... | collective-permute-start | bytes 393224 | tf_op jit(solution)/shard_map/ppermute | solution.py:337
  34.5 6.5 %collective-permute-done.11 = bf16[128,512]{1,0:T(8,128)(2,1)S(1)} collective-permute-done((bf16[128,512]{1,0:T(8,128)(2,1)S(1)}, bf16[128,512]{1,0:T(8,128)(2,1)S(1)}, u32[]{:S(2)}, u32[]{:S(2)}) %collective-permute-start.11) | collective-permute-done | bytes 131104 | tf_op jit(solution)/shard_map/ppermute | solution.py:337
  41.0 0.5 %collective-permute-done.13 = bf16[128,512]{1,0:T(8,128)(2,1)S(1)} collective-permute-done((bf16[128,512]{1,0:T(8,128)(2,1)S(1)}, bf16[128,512]{1,0:T(8,128)(2,1)S(1)}, u32[]{:S(2)}, u32[]{:S(2)}) %collective-permute-start.13) | collective-permute-done | bytes 131104 | tf_op jit(solution)/shard_map/ppermute | solution.py:337
  41.5 0.7 %fusion.2 = bf16[128,512]{1,0:T(8,128)(2,1)} fusion(bf16[128,512]{1,0:T(8,128)(2,1)S(1)} %collective-permute-done.13, bf16[128,512]{1,0:T(8,128)(2,1)S(1)} %collective-permute-done.12, bf16[128,512]{1,0:T(8,128)(2,1)S(1)} %collective-permute-done.11, f32[4,128,512]{2,1,0:T(8,128)S(1)} %get-tuple-element.42, bf16[3,128,512]{2,1,0:T(8,128)(2,1)S(1)} %collective-permute-done.10), kind=kLoop, calls=%fused_computation.3 | loop fusion | flops 589824 | bytes 917504 | tf_op jit(solution)/shard_map/convert_element_type | solution.py:387
  (26 shorter events, 1.6 us)
Async XLA Ops:
  0.0 15.2 %copy-start = (bf16[128,512]{1,0:T(8,128)(2,1)S(1)}, bf16[128,512]{1,0:T(8,128)(2,1)}, u32[]{:S(2)}) copy-start(bf16[128,512]{1,0:T(8,128)(2,1)} %refs_0_.3) | copy-start | bytes 393220
  0.0 14.6 %copy-start.3 = (s32[128]{0:T(128)S(1)}, s32[128]{0:T(128)}, u32[]{:S(2)}) copy-start(s32[128]{0:T(128)} %param.13) | copy-start | bytes 1540
  0.0 11.7 %collective-permute-start.1 = (bf16[128,512]{1,0:T(8,128)(2,1)}, bf16[128,512]{1,0:T(8,128)(2,1)S(1)}, u32[]{:S(2)}, u32[]{:S(2)}) collective-permute-start(bf16[128,512]{1,0:T(8,128)(2,1)} %refs_0_.3), channel_id=1, source_target_pairs={{0,2},{1,3},{2,4},{3,5},{4,6},{5,7},{6,0},{7,1},{8,10},{9,11},{10,... | collective-permute-start | bytes 393224 | tf_op jit(solution)/shard_map/ppermute | solution.py:337
  3.0 11.6 %collective-permute-start.3 = (bf16[128,512]{1,0:T(8,128)(2,1)}, bf16[128,512]{1,0:T(8,128)(2,1)S(1)}, u32[]{:S(2)}, u32[]{:S(2)}) collective-permute-start(bf16[128,512]{1,0:T(8,128)(2,1)} %refs_0_.3), channel_id=1, source_target_pairs={{0,4},{1,5},{2,6},{3,7},{4,0},{5,1},{6,2},{7,3},{8,12},{9,13},{10,... | collective-permute-start | bytes 393224 | tf_op jit(solution)/shard_map/ppermute | solution.py:337
  5.6 9.6 %collective-permute-start = (bf16[128,512]{1,0:T(8,128)(2,1)}, bf16[128,512]{1,0:T(8,128)(2,1)S(1)}, u32[]{:S(2)}, u32[]{:S(2)}) collective-permute-start(bf16[128,512]{1,0:T(8,128)(2,1)} %refs_0_.3), channel_id=1, source_target_pairs={{0,1},{1,0},{2,3},{3,2},{4,5},{5,4},{6,7},{7,6},{8,9},{9,8},{10,11... | collective-permute-start | bytes 393224 | tf_op jit(solution)/shard_map/ppermute | solution.py:340
  5.6 9.2 %collective-permute-start.5 = (bf16[128,512]{1,0:T(8,128)(2,1)}, bf16[128,512]{1,0:T(8,128)(2,1)S(1)}, u32[]{:S(2)}, u32[]{:S(2)}) collective-permute-start(bf16[128,512]{1,0:T(8,128)(2,1)} %refs_0_.3), channel_id=1, source_target_pairs={{0,6},{1,7},{2,0},{3,1},{4,2},{5,3},{6,4},{7,5},{8,14},{9,15},{10,... | collective-permute-start | bytes 393224 | tf_op jit(solution)/shard_map/ppermute | solution.py:337
  11.7 3.9 %collective-permute-start.2 = (bf16[128,512]{1,0:T(8,128)(2,1)S(1)}, bf16[128,512]{1,0:T(8,128)(2,1)S(1)}, u32[]{:S(2)}, u32[]{:S(2)}) collective-permute-start(bf16[128,512]{1,0:T(8,128)(2,1)S(1)} %collective-permute-done.1.refs_0_.refs_2_), channel_id=1, source_target_pairs={{0,1},{1,0},{2,3},{3,2},{4,5},{5,4},{6,7},{7,6},{8,9},{9,8},{10,11... | collective-permute-start | bytes 393224 | tf_op jit(solution)/shard_map/ppermute | solution.py:340
  14.6 1.5 %collective-permute-start.4 = (bf16[128,512]{1,0:T(8,128)(2,1)S(1)}, bf16[128,512]{1,0:T(8,128)(2,1)S(1)}, u32[]{:S(2)}, u32[]{:S(2)}) collective-permute-start(bf16[128,512]{1,0:T(8,128)(2,1)S(1)} %collective-permute-done.3.refs_0_.refs_4_), channel_id=1, source_target_pairs={{0,1},{1,0},{2,3},{3,2},{4,5},{5,4},{6,7},{7,6},{8,9},{9,8},{10,11... | collective-permute-start | bytes 393224 | tf_op jit(solution)/shard_map/ppermute | solution.py:340
  14.9 1.7 %collective-permute-start.6 = (bf16[128,512]{1,0:T(8,128)(2,1)S(1)}, bf16[128,512]{1,0:T(8,128)(2,1)S(1)}, u32[]{:S(2)}, u32[]{:S(2)}) collective-permute-start(bf16[128,512]{1,0:T(8,128)(2,1)S(1)} %collective-permute-done.5.refs_0_.refs_6_), channel_id=1, source_target_pairs={{0,1},{1,0},{2,3},{3,2},{4,5},{5,4},{6,7},{7,6},{8,9},{9,8},{10,11... | collective-permute-start | bytes 393224 | tf_op jit(solution)/shard_map/ppermute | solution.py:340
  16.9 3.4 %copy-start.1 = (f32[4,128]{1,0:T(4,128)S(1)}, f32[4,128]{1,0:T(4,128)}, u32[]{:S(2)}) copy-start(f32[4,128]{1,0:T(4,128)} %param.11) | copy-start | bytes 6148
  16.9 3.4 %copy-start.2 = (f32[4,128]{1,0:T(4,128)S(1)}, f32[4,128]{1,0:T(4,128)}, u32[]{:S(2)}) copy-start(f32[4,128]{1,0:T(4,128)} %param.12) | copy-start | bytes 6148
  17.0 7.4 %collective-permute-start.7 = (bf16[528,128]{1,0:T(8,128)(2,1)S(1)}, bf16[528,128]{1,0:T(8,128)(2,1)S(1)}, u32[]{:S(2)}, u32[]{:S(2)}) collective-permute-start(bf16[528,128]{1,0:T(8,128)(2,1)S(1)} %kv_step.8.refs_12_), channel_id=1, source_target_pairs={{0,8},{8,16},{16,24},{24,0},{1,9},{9,17},{17,25},{25,1},{2,10},{10... | collective-permute-start | bytes 405512 | tf_op jit(solution)/shard_map/ppermute | solution.py:343
  18.8 7.6 %collective-permute-start.8 = (bf16[128,512]{1,0:T(8,128)(2,1)S(1)}, bf16[128,512]{1,0:T(8,128)(2,1)S(1)}, u32[]{:S(2)}, u32[]{:S(2)}) collective-permute-start(bf16[128,512]{1,0:T(8,128)(2,1)S(1)} %kv_step.9.val_ref), channel_id=1, source_target_pairs={{0,8},{8,16},{16,24},{24,0},{1,9},{9,17},{17,25},{25,1},{2,10},{10... | collective-permute-start | bytes 393224 | tf_op jit(solution)/shard_map/ppermute | solution.py:343
  26.8 1.4 %collective-permute-start.9 = (bf16[1,128,512]{2,1,0:T(8,128)(2,1)S(1)}, bf16[1,128,512]{2,1,0:T(8,128)(2,1)S(1)}, u32[]{:S(2)}, u32[]{:S(2)}) collective-permute-start(bf16[1,128,512]{2,1,0:T(8,128)(2,1)S(1)} %get-tuple-element.44), channel_id=1, source_target_pairs={{0,1},{1,0},{2,3},{3,2},{4,5},{5,4},{6,7},{7,6},{8,9},{9,8},{10,11... | collective-permute-start | bytes 393224 | tf_op jit(solution)/shard_map/ppermute | solution.py:340
  28.2 2.3 %collective-permute-start.10 = (bf16[3,128,512]{2,1,0:T(8,128)(2,1)S(1)}, bf16[3,128,512]{2,1,0:T(8,128)(2,1)S(1)}, u32[]{:S(2)}, u32[]{:S(2)}) collective-permute-start(bf16[3,128,512]{2,1,0:T(8,128)(2,1)S(1)} %get-tuple-element.45), channel_id=1, source_target_pairs={{0,1},{1,0},{2,3},{3,2},{4,5},{5,4},{6,7},{7,6},{8,9},{9,8},{10,11... | collective-permute-start | bytes 1179656 | tf_op jit(solution)/shard_map/ppermute | solution.py:340
  28.4 12.5 %collective-permute-start.11 = (bf16[128,512]{1,0:T(8,128)(2,1)S(1)}, bf16[128,512]{1,0:T(8,128)(2,1)S(1)}, u32[]{:S(2)}, u32[]{:S(2)}) collective-permute-start(bf16[128,512]{1,0:T(8,128)(2,1)S(1)} %add_bitcast_fusion), channel_id=1, source_target_pairs={{0,4},{1,5},{2,6},{3,7},{4,0},{5,1},{6,2},{7,3},{8,12},{9,13},{10,... | collective-permute-start | bytes 393224 | tf_op jit(solution)/shard_map/ppermute | solution.py:337
  30.6 10.4 %collective-permute-start.12 = (bf16[128,512]{1,0:T(8,128)(2,1)S(1)}, bf16[128,512]{1,0:T(8,128)(2,1)S(1)}, u32[]{:S(2)}, u32[]{:S(2)}) collective-permute-start(bf16[128,512]{1,0:T(8,128)(2,1)S(1)} %get-tuple-element.47), channel_id=1, source_target_pairs={{0,2},{1,3},{2,4},{3,5},{4,6},{5,7},{6,0},{7,1},{8,10},{9,11},{10,... | collective-permute-start | bytes 393224 | tf_op jit(solution)/shard_map/ppermute | solution.py:337
  33.2 8.3 %collective-permute-start.13 = (bf16[128,512]{1,0:T(8,128)(2,1)S(1)}, bf16[128,512]{1,0:T(8,128)(2,1)S(1)}, u32[]{:S(2)}, u32[]{:S(2)}) collective-permute-start(bf16[128,512]{1,0:T(8,128)(2,1)S(1)} %get-tuple-element.48), channel_id=1, source_target_pairs={{0,6},{1,7},{2,0},{3,1},{4,2},{5,3},{6,4},{7,5},{8,14},{9,15},{10,... | collective-permute-start | bytes 393224 | tf_op jit(solution)/shard_map/ppermute | solution.py:337

commit v7 on v6

--- a/solution.py
+++ b/solution.py
@@ -239,7 +239,7 @@
     heads, rows, _ = score_ref.shape
     head_dim = qc_ref.shape[1] // heads
     exists = jnp.minimum(lax.axis_index("seq"), 1).astype(F32)
-    mem_doc = mem_ref[heads * rows : heads * rows + 1].astype(F32) * exists
+    mem_doc = mem_ref[heads * rows : heads * rows + 16].astype(F32)[:1] * exists
     mem_doc = jnp.broadcast_to(mem_doc, (rows, rows))
     allowed = mem_doc == jnp.broadcast_to(doc_ref[...], (rows, rows)).T
     scale = 1.0 / (float(head_dim) ** 0.5)

time: 42.7 us -> 42.7 us (level)
  no operation moved by 1% of the time
where the time goes in v7:
time: 42.7 us; the launch traced here: 42.2 us
  starting transfers between devices  16.9 us (40%)
  Pallas kernels  12.8 us (30%)
  waiting for transfers between devices  11.5 us (27%)
  other arithmetic  0.84 us (2%)
    ppermute x6, starting transfers between devices, across(): lax.ppermute(value, 'mp', [(i, (i + 2 * k) % count) for i in range(count)])  12.9 us
    ppermute x6, waiting for transfers between devices, across(): lax.ppermute(value, 'mp', [(i, (i + 2 * k) % count) for i in range(count)])  9.8 us
    pallas_call x1, Pallas kernels, load(): call(functools.partial(load_kernel, parts), (pltpu.VMEM((rows, cols), BF1...  4.76 us
    pallas_call x1, Pallas kernels, queries(): call(functools.partial(q_kernel, count, heads), (pltpu.VMEM((rows, cols),...  3.56 us
    ppermute x2, starting transfers between devices, onward(): lax.ppermute(value, 'seq', [(i, (i + 1) % segments) for i in range(segmen...  3.08 us
    pallas_call x5, Pallas kernels, kv_step(): call(functools.partial(kv_kernel, sources, kinds, acc is None, last), out...  2 us
    pallas_call x1, Pallas kernels, weigh(): call(weigh_kernel, (pltpu.VMEM((heads, rows, rows), BF16), pltpu.VMEM((ro...  1.46 us
    ppermute x2, waiting for transfers between devices, onward(): lax.ppermute(value, 'seq', [(i, (i + 1) % segments) for i in range(segmen...  1.04 us
  transfers between devices with their start and end apart: 14, of which 7 were waited for; matrix products, arithmetic and copies ran while one was open for 0% of the time, Pallas kernels for 29%

profile of v7, /device:TPU:0, one launch (start us, length us, event | category | flops | bytes accessed | tf_op | source)
XLA Modules:
  0.0 42.2 jit_solution(8011704050688282106)
XLA Ops:
  0.0 3.0 %collective-permute-start.1 = (bf16[128,512]{1,0:T(8,128)(2,1)}, bf16[128,512]{1,0:T(8,128)(2,1)S(1)}, u32[]{:S(2)}, u32[]{:S(2)}) collective-permute-start(bf16[128,512]{1,0:T(8,128)(2,1)} %refs_0_.3), channel_id=1, source_target_pairs={{0,2},{1,3},{2,4},{3,5},{4,6},{5,7},{6,0},{7,1},{8,10},{9,11},{10,... | collective-permute-start | bytes 393224 | tf_op jit(solution)/shard_map/ppermute | solution.py:337
  3.0 2.6 %collective-permute-start.3 = (bf16[128,512]{1,0:T(8,128)(2,1)}, bf16[128,512]{1,0:T(8,128)(2,1)S(1)}, u32[]{:S(2)}, u32[]{:S(2)}) collective-permute-start(bf16[128,512]{1,0:T(8,128)(2,1)} %refs_0_.3), channel_id=1, source_target_pairs={{0,4},{1,5},{2,6},{3,7},{4,0},{5,1},{6,2},{7,3},{8,12},{9,13},{10,... | collective-permute-start | bytes 393224 | tf_op jit(solution)/shard_map/ppermute | solution.py:337
  5.6 1.3 %collective-permute-start.5 = (bf16[128,512]{1,0:T(8,128)(2,1)}, bf16[128,512]{1,0:T(8,128)(2,1)S(1)}, u32[]{:S(2)}, u32[]{:S(2)}) collective-permute-start(bf16[128,512]{1,0:T(8,128)(2,1)} %refs_0_.3), channel_id=1, source_target_pairs={{0,6},{1,7},{2,0},{3,1},{4,2},{5,3},{6,4},{7,5},{8,14},{9,15},{10,... | collective-permute-start | bytes 393224 | tf_op jit(solution)/shard_map/ppermute | solution.py:337
  7.0 4.8 %load.1 = (bf16[256,512]{1,0:T(8,128)(2,1)S(1)}, bf16[2,4096,512]{2,1,0:T(8,128)(2,1)S(1)}) custom-call(bf16[4096,512]{1,0:T(8,128)(2,1)} %w_pos.1, bf16[3,4096,512]{2,1,0:T(8,128)(2,1)} %refs_8_.1), custom_call_target="tpu_custom_call" | custom-call | flops 1048576 | bytes 1048576 | tf_op jit(solution)/shard_map/load/pallas_call | solution.py:93
  12.0 2.5 %collective-permute-done.3.refs_0_.refs_4_ = bf16[128,512]{1,0:T(8,128)(2,1)S(1)} collective-permute-done((bf16[128,512]{1,0:T(8,128)(2,1)}, bf16[128,512]{1,0:T(8,128)(2,1)S(1)}, u32[]{:S(2)}, u32[]{:S(2)}) %collective-permute-start.3) | collective-permute-done | bytes 131104 | tf_op jit(solution)/shard_map/ppermute | solution.py:337
  15.2 0.4 %kv_step.5.refs_3_ = f32[2,128,512]{2,1,0:T(8,128)S(1)} custom-call(bf16[128,512]{1,0:T(8,128)(2,1)S(1)} %copy-done, bf16[128,512]{1,0:T(8,128)(2,1)S(1)} %collective-permute-done.refs_1_, bf16[2,4096,512]{2,1,0:T(8,128)(2,1)S(1)} %get-tuple-element.32.refs_2_), custom_call_target="tpu_custom_call" | custom-call | flops 536870912 | tf_op jit(solution)/shard_map/kv_step/pallas_call | solution.py:158
  15.6 0.5 %kv_step.6.refs_3_ = f32[2,128,512]{2,1,0:T(8,128)S(1)} custom-call(bf16[128,512]{1,0:T(8,128)(2,1)S(1)} %collective-permute-done.1.refs_0_.refs_2_, bf16[128,512]{1,0:T(8,128)(2,1)S(1)} %collective-permute-done.2.refs_1_.refs_3_, bf16[2,4096,512]{2,1,0:T(8,128)(2,1)S(1)} %get-tuple-element.32.refs_2_, f32[2,128,512]{2,1,0:T(8,128)S(1)} %kv_step.5.refs_3_), custom_call_target="tpu_custom_call" | custom-call | flops 536870912 | tf_op jit(solution)/shard_map/kv_step/pallas_call | solution.py:158
  16.1 0.5 %kv_step.7.refs_3_ = f32[2,128,512]{2,1,0:T(8,128)S(1)} custom-call(bf16[128,512]{1,0:T(8,128)(2,1)S(1)} %collective-permute-done.3.refs_0_.refs_4_, bf16[128,512]{1,0:T(8,128)(2,1)S(1)} %collective-permute-done.4.refs_1_.refs_5_, bf16[2,4096,512]{2,1,0:T(8,128)(2,1)S(1)} %get-tuple-element.32.refs_2_, f32[2,128,512]{2,1,0:T(8,128)S(1)} %kv_step.6.refs_3_), custom_call_target="tpu_custom_call" | custom-call | flops 536870912 | tf_op jit(solution)/shard_map/kv_step/pallas_call | solution.py:158
  16.6 0.3 kv_step.8.refs_12_
  17.0 1.5 %collective-permute-start.7 = (bf16[528,128]{1,0:T(8,128)(2,1)S(1)}, bf16[528,128]{1,0:T(8,128)(2,1)S(1)}, u32[]{:S(2)}, u32[]{:S(2)}) collective-permute-start(bf16[528,128]{1,0:T(8,128)(2,1)S(1)} %kv_step.8.refs_12_), channel_id=1, source_target_pairs={{0,8},{8,16},{16,24},{24,0},{1,9},{9,17},{17,25},{25,1},{2,10},{10... | collective-permute-start | bytes 405512 | tf_op jit(solution)/shard_map/ppermute | solution.py:343
  18.8 1.5 %collective-permute-start.8 = (bf16[128,512]{1,0:T(8,128)(2,1)S(1)}, bf16[128,512]{1,0:T(8,128)(2,1)S(1)}, u32[]{:S(2)}, u32[]{:S(2)}) collective-permute-start(bf16[128,512]{1,0:T(8,128)(2,1)S(1)} %kv_step.9.val_ref), channel_id=1, source_target_pairs={{0,8},{8,16},{16,24},{24,0},{1,9},{9,17},{17,25},{25,1},{2,10},{10... | collective-permute-start | bytes 393224 | tf_op jit(solution)/shard_map/ppermute | solution.py:343
  20.4 3.6 %queries.1 = (bf16[128,512]{1,0:T(8,128)(2,1)S(1)}, f32[4,128,256]{2,1,0:T(8,128)S(1)}, bf16[512,4096]{1,0:T(8,128)(2,1)S(1)}) custom-call(bf16[128,512]{1,0:T(8,128)(2,1)S(1)} %copy-done, bf16[128,512]{1,0:T(8,128)(2,1)S(1)} %collective-permute-done.refs_1_, bf16[128,512]{1,0:T(8,128)(2,1)S(1)} %collective-permute-done.1.refs_0_.refs_2_, ...), custom_call_target="tpu_custom_call" | custom-call | flops 536870912 | bytes 4194304 | tf_op jit(solution)/shard_map/queries/pallas_call | solution.py:214
  23.9 0.4 collective-permute-done.7.mem_ref
  24.3 1.5 %weigh.1 = (bf16[4,128,128]{2,1,0:T(8,128)(2,1)S(1)}, f32[128,512]{1,0:T(8,128)S(1)}) custom-call(bf16[128,512]{1,0:T(8,128)(2,1)S(1)} %get-tuple-element.35.qc_ref, f32[4,128,256]{2,1,0:T(8,128)S(1)} %get-tuple-element.36.score_ref, bf16[528,128]{1,0:T(8,128)(2,1)S(1)} %collective-permute-done.7.mem_ref, bf16[128,512]{1,0:T(8,128)(2,1)S(1)} %kv_step.9.val_ref, ...), custom_call_target="tpu_custom_call" | custom-call | flops 67108864 | bytes 524288 | tf_op jit(solution)/shard_map/weigh/pallas_call | solution.py:264
  25.8 0.6 %collective-permute-done.8.mem_ref = bf16[128,512]{1,0:T(8,128)(2,1)S(1)} collective-permute-done((bf16[128,512]{1,0:T(8,128)(2,1)S(1)}, bf16[128,512]{1,0:T(8,128)(2,1)S(1)}, u32[]{:S(2)}, u32[]{:S(2)}) %collective-permute-start.8) | collective-permute-done | bytes 131104 | tf_op jit(solution)/shard_map/ppermute | solution.py:343
  26.4 0.3 mix.1
  26.9 0.7 %rest.1 = (bf16[3,128,512]{2,1,0:T(8,128)(2,1)S(1)}, f32[4,128,512]{2,1,0:T(8,128)S(1)}) custom-call(bf16[128,512]{1,0:T(8,128)(2,1)S(1)} %get-tuple-element.41.head_ref, bf16[512,4096]{1,0:T(8,128)(2,1)S(1)} %get-tuple-element.40.w_ref), custom_call_target="tpu_custom_call" | custom-call | flops 536870912 | bytes 4194304 | tf_op jit(solution)/shard_map/rest/pallas_call | solution.py:315
  27.5 0.7 %collective-permute-done.9 = bf16[1,128,512]{2,1,0:T(8,128)(2,1)S(1)} collective-permute-done((bf16[1,128,512]{2,1,0:T(8,128)(2,1)S(1)}, bf16[1,128,512]{2,1,0:T(8,128)(2,1)S(1)}, u32[]{:S(2)}, u32[]{:S(2)}) %collective-permute-start.9) | collective-permute-done | bytes 131104 | tf_op jit(solution)/shard_map/ppermute | solution.py:340
  28.4 2.1 %collective-permute-start.11 = (bf16[128,512]{1,0:T(8,128)(2,1)S(1)}, bf16[128,512]{1,0:T(8,128)(2,1)S(1)}, u32[]{:S(2)}, u32[]{:S(2)}) collective-permute-start(bf16[128,512]{1,0:T(8,128)(2,1)S(1)} %add_bitcast_fusion), channel_id=1, source_target_pairs={{0,4},{1,5},{2,6},{3,7},{4,0},{5,1},{6,2},{7,3},{8,12},{9,13},{10,... | collective-permute-start | bytes 393224 | tf_op jit(solution)/shard_map/ppermute | solution.py:337
  30.6 2.6 %collective-permute-start.12 = (bf16[128,512]{1,0:T(8,128)(2,1)S(1)}, bf16[128,512]{1,0:T(8,128)(2,1)S(1)}, u32[]{:S(2)}, u32[]{:S(2)}) collective-permute-start(bf16[128,512]{1,0:T(8,128)(2,1)S(1)} %get-tuple-element.47), channel_id=1, source_target_pairs={{0,2},{1,3},{2,4},{3,5},{4,6},{5,7},{6,0},{7,1},{8,10},{9,11},{10,... | collective-permute-start | bytes 393224 | tf_op jit(solution)/shard_map/ppermute | solution.py:337
  33.2 1.3 %collective-permute-start.13 = (bf16[128,512]{1,0:T(8,128)(2,1)S(1)}, bf16[128,512]{1,0:T(8,128)(2,1)S(1)}, u32[]{:S(2)}, u32[]{:S(2)}) collective-permute-start(bf16[128,512]{1,0:T(8,128)(2,1)S(1)} %get-tuple-element.48), channel_id=1, source_target_pairs={{0,6},{1,7},{2,0},{3,1},{4,2},{5,3},{6,4},{7,5},{8,14},{9,15},{10,... | collective-permute-start | bytes 393224 | tf_op jit(solution)/shard_map/ppermute | solution.py:337
  34.5 6.5 %collective-permute-done.11 = bf16[128,512]{1,0:T(8,128)(2,1)S(1)} collective-permute-done((bf16[128,512]{1,0:T(8,128)(2,1)S(1)}, bf16[128,512]{1,0:T(8,128)(2,1)S(1)}, u32[]{:S(2)}, u32[]{:S(2)}) %collective-permute-start.11) | collective-permute-done | bytes 131104 | tf_op jit(solution)/shard_map/ppermute | solution.py:337
  41.0 0.5 %collective-permute-done.13 = bf16[128,512]{1,0:T(8,128)(2,1)S(1)} collective-permute-done((bf16[128,512]{1,0:T(8,128)(2,1)S(1)}, bf16[128,512]{1,0:T(8,128)(2,1)S(1)}, u32[]{:S(2)}, u32[]{:S(2)}) %collective-permute-start.13) | collective-permute-done | bytes 131104 | tf_op jit(solution)/shard_map/ppermute | solution.py:337
  41.5 0.7 %fusion.2 = bf16[128,512]{1,0:T(8,128)(2,1)} fusion(bf16[128,512]{1,0:T(8,128)(2,1)S(1)} %collective-permute-done.13, bf16[128,512]{1,0:T(8,128)(2,1)S(1)} %collective-permute-done.12, bf16[128,512]{1,0:T(8,128)(2,1)S(1)} %collective-permute-done.11, f32[4,128,512]{2,1,0:T(8,128)S(1)} %get-tuple-element.42, bf16[3,128,512]{2,1,0:T(8,128)(2,1)S(1)} %collective-permute-done.10), kind=kLoop, calls=%fused_computation.3 | loop fusion | flops 589824 | bytes 917504 | tf_op jit(solution)/shard_map/convert_element_type | solution.py:387
  (26 shorter events, 1.6 us)
Async XLA Ops:
  0.0 15.2 %copy-start = (bf16[128,512]{1,0:T(8,128)(2,1)S(1)}, bf16[128,512]{1,0:T(8,128)(2,1)}, u32[]{:S(2)}) copy-start(bf16[128,512]{1,0:T(8,128)(2,1)} %refs_0_.3) | copy-start | bytes 393220
  0.0 14.6 %copy-start.3 = (s32[128]{0:T(128)S(1)}, s32[128]{0:T(128)}, u32[]{:S(2)}) copy-start(s32[128]{0:T(128)} %param.13) | copy-start | bytes 1540
  0.0 11.7 %collective-permute-start.1 = (bf16[128,512]{1,0:T(8,128)(2,1)}, bf16[128,512]{1,0:T(8,128)(2,1)S(1)}, u32[]{:S(2)}, u32[]{:S(2)}) collective-permute-start(bf16[128,512]{1,0:T(8,128)(2,1)} %refs_0_.3), channel_id=1, source_target_pairs={{0,2},{1,3},{2,4},{3,5},{4,6},{5,7},{6,0},{7,1},{8,10},{9,11},{10,... | collective-permute-start | bytes 393224 | tf_op jit(solution)/shard_map/ppermute | solution.py:337
  3.0 11.6 %collective-permute-start.3 = (bf16[128,512]{1,0:T(8,128)(2,1)}, bf16[128,512]{1,0:T(8,128)(2,1)S(1)}, u32[]{:S(2)}, u32[]{:S(2)}) collective-permute-start(bf16[128,512]{1,0:T(8,128)(2,1)} %refs_0_.3), channel_id=1, source_target_pairs={{0,4},{1,5},{2,6},{3,7},{4,0},{5,1},{6,2},{7,3},{8,12},{9,13},{10,... | collective-permute-start | bytes 393224 | tf_op jit(solution)/shard_map/ppermute | solution.py:337
  5.6 9.6 %collective-permute-start = (bf16[128,512]{1,0:T(8,128)(2,1)}, bf16[128,512]{1,0:T(8,128)(2,1)S(1)}, u32[]{:S(2)}, u32[]{:S(2)}) collective-permute-start(bf16[128,512]{1,0:T(8,128)(2,1)} %refs_0_.3), channel_id=1, source_target_pairs={{0,1},{1,0},{2,3},{3,2},{4,5},{5,4},{6,7},{7,6},{8,9},{9,8},{10,11... | collective-permute-start | bytes 393224 | tf_op jit(solution)/shard_map/ppermute | solution.py:340
  5.6 9.2 %collective-permute-start.5 = (bf16[128,512]{1,0:T(8,128)(2,1)}, bf16[128,512]{1,0:T(8,128)(2,1)S(1)}, u32[]{:S(2)}, u32[]{:S(2)}) collective-permute-start(bf16[128,512]{1,0:T(8,128)(2,1)} %refs_0_.3), channel_id=1, source_target_pairs={{0,6},{1,7},{2,0},{3,1},{4,2},{5,3},{6,4},{7,5},{8,14},{9,15},{10,... | collective-permute-start | bytes 393224 | tf_op jit(solution)/shard_map/ppermute | solution.py:337
  11.7 3.9 %collective-permute-start.2 = (bf16[128,512]{1,0:T(8,128)(2,1)S(1)}, bf16[128,512]{1,0:T(8,128)(2,1)S(1)}, u32[]{:S(2)}, u32[]{:S(2)}) collective-permute-start(bf16[128,512]{1,0:T(8,128)(2,1)S(1)} %collective-permute-done.1.refs_0_.refs_2_), channel_id=1, source_target_pairs={{0,1},{1,0},{2,3},{3,2},{4,5},{5,4},{6,7},{7,6},{8,9},{9,8},{10,11... | collective-permute-start | bytes 393224 | tf_op jit(solution)/shard_map/ppermute | solution.py:340
  14.6 1.5 %collective-permute-start.4 = (bf16[128,512]{1,0:T(8,128)(2,1)S(1)}, bf16[128,512]{1,0:T(8,128)(2,1)S(1)}, u32[]{:S(2)}, u32[]{:S(2)}) collective-permute-start(bf16[128,512]{1,0:T(8,128)(2,1)S(1)} %collective-permute-done.3.refs_0_.refs_4_), channel_id=1, source_target_pairs={{0,1},{1,0},{2,3},{3,2},{4,5},{5,4},{6,7},{7,6},{8,9},{9,8},{10,11... | collective-permute-start | bytes 393224 | tf_op jit(solution)/shard_map/ppermute | solution.py:340
  14.9 1.7 %collective-permute-start.6 = (bf16[128,512]{1,0:T(8,128)(2,1)S(1)}, bf16[128,512]{1,0:T(8,128)(2,1)S(1)}, u32[]{:S(2)}, u32[]{:S(2)}) collective-permute-start(bf16[128,512]{1,0:T(8,128)(2,1)S(1)} %collective-permute-done.5.refs_0_.refs_6_), channel_id=1, source_target_pairs={{0,1},{1,0},{2,3},{3,2},{4,5},{5,4},{6,7},{7,6},{8,9},{9,8},{10,11... | collective-permute-start | bytes 393224 | tf_op jit(solution)/shard_map/ppermute | solution.py:340
  16.9 3.4 %copy-start.1 = (f32[4,128]{1,0:T(4,128)S(1)}, f32[4,128]{1,0:T(4,128)}, u32[]{:S(2)}) copy-start(f32[4,128]{1,0:T(4,128)} %param.11) | copy-start | bytes 6148
  16.9 3.4 %copy-start.2 = (f32[4,128]{1,0:T(4,128)S(1)}, f32[4,128]{1,0:T(4,128)}, u32[]{:S(2)}) copy-start(f32[4,128]{1,0:T(4,128)} %param.12) | copy-start | bytes 6148
  17.0 7.4 %collective-permute-start.7 = (bf16[528,128]{1,0:T(8,128)(2,1)S(1)}, bf16[528,128]{1,0:T(8,128)(2,1)S(1)}, u32[]{:S(2)}, u32[]{:S(2)}) collective-permute-start(bf16[528,128]{1,0:T(8,128)(2,1)S(1)} %kv_step.8.refs_12_), channel_id=1, source_target_pairs={{0,8},{8,16},{16,24},{24,0},{1,9},{9,17},{17,25},{25,1},{2,10},{10... | collective-permute-start | bytes 405512 | tf_op jit(solution)/shard_map/ppermute | solution.py:343
  18.8 7.6 %collective-permute-start.8 = (bf16[128,512]{1,0:T(8,128)(2,1)S(1)}, bf16[128,512]{1,0:T(8,128)(2,1)S(1)}, u32[]{:S(2)}, u32[]{:S(2)}) collective-permute-start(bf16[128,512]{1,0:T(8,128)(2,1)S(1)} %kv_step.9.val_ref), channel_id=1, source_target_pairs={{0,8},{8,16},{16,24},{24,0},{1,9},{9,17},{17,25},{25,1},{2,10},{10... | collective-permute-start | bytes 393224 | tf_op jit(solution)/shard_map/ppermute | solution.py:343
  26.8 1.4 %collective-permute-start.9 = (bf16[1,128,512]{2,1,0:T(8,128)(2,1)S(1)}, bf16[1,128,512]{2,1,0:T(8,128)(2,1)S(1)}, u32[]{:S(2)}, u32[]{:S(2)}) collective-permute-start(bf16[1,128,512]{2,1,0:T(8,128)(2,1)S(1)} %get-tuple-element.44), channel_id=1, source_target_pairs={{0,1},{1,0},{2,3},{3,2},{4,5},{5,4},{6,7},{7,6},{8,9},{9,8},{10,11... | collective-permute-start | bytes 393224 | tf_op jit(solution)/shard_map/ppermute | solution.py:340
  28.2 2.3 %collective-permute-start.10 = (bf16[3,128,512]{2,1,0:T(8,128)(2,1)S(1)}, bf16[3,128,512]{2,1,0:T(8,128)(2,1)S(1)}, u32[]{:S(2)}, u32[]{:S(2)}) collective-permute-start(bf16[3,128,512]{2,1,0:T(8,128)(2,1)S(1)} %get-tuple-element.45), channel_id=1, source_target_pairs={{0,1},{1,0},{2,3},{3,2},{4,5},{5,4},{6,7},{7,6},{8,9},{9,8},{10,11... | collective-permute-start | bytes 1179656 | tf_op jit(solution)/shard_map/ppermute | solution.py:340
  28.4 12.5 %collective-permute-start.11 = (bf16[128,512]{1,0:T(8,128)(2,1)S(1)}, bf16[128,512]{1,0:T(8,128)(2,1)S(1)}, u32[]{:S(2)}, u32[]{:S(2)}) collective-permute-start(bf16[128,512]{1,0:T(8,128)(2,1)S(1)} %add_bitcast_fusion), channel_id=1, source_target_pairs={{0,4},{1,5},{2,6},{3,7},{4,0},{5,1},{6,2},{7,3},{8,12},{9,13},{10,... | collective-permute-start | bytes 393224 | tf_op jit(solution)/shard_map/ppermute | solution.py:337
  30.6 10.4 %collective-permute-start.12 = (bf16[128,512]{1,0:T(8,128)(2,1)S(1)}, bf16[128,512]{1,0:T(8,128)(2,1)S(1)}, u32[]{:S(2)}, u32[]{:S(2)}) collective-permute-start(bf16[128,512]{1,0:T(8,128)(2,1)S(1)} %get-tuple-element.47), channel_id=1, source_target_pairs={{0,2},{1,3},{2,4},{3,5},{4,6},{5,7},{6,0},{7,1},{8,10},{9,11},{10,... | collective-permute-start | bytes 393224 | tf_op jit(solution)/shard_map/ppermute | solution.py:337
  33.2 8.3 %collective-permute-start.13 = (bf16[128,512]{1,0:T(8,128)(2,1)S(1)}, bf16[128,512]{1,0:T(8,128)(2,1)S(1)}, u32[]{:S(2)}, u32[]{:S(2)}) collective-permute-start(bf16[128,512]{1,0:T(8,128)(2,1)S(1)} %get-tuple-element.48), channel_id=1, source_target_pairs={{0,6},{1,7},{2,0},{3,1},{4,2},{5,3},{6,4},{7,5},{8,14},{9,15},{10,... | collective-permute-start | bytes 393224 | tf_op jit(solution)/shard_map/ppermute | solution.py:337

commit v8 on v7

--- a/solution.py
+++ b/solution.py
@@ -9,7 +9,7 @@
 
 BF16 = jnp.bfloat16
 F32 = jnp.float32
-VMEM_LIMIT = 24 * 1024 * 1024
+VMEM_LIMIT = 16 * 1024 * 1024
 
 
 def vmem_spec():
@@ -326,6 +326,29 @@
     )(head_out, w_out)
 
 
+def total_kernel(own_ref, *refs):
+    out_ref, buf, sem = refs[-3:]
+    total = own_ref[...]
+    for term in refs[:-3]:
+        total = total + term[...].astype(F32)
+    buf[...] = total.astype(BF16)
+    copy = pltpu.make_async_copy(buf, out_ref, sem)
+    copy.start()
+    copy.wait()
+
+
+def total_sum(own, terms):
+    return pl.pallas_call(
+        total_kernel,
+        out_shape=jax.ShapeDtypeStruct(own.shape, BF16),
+        in_specs=[vmem_spec()] * (1 + len(terms)),
+        out_specs=hbm_spec(),
+        scratch_shapes=[pltpu.VMEM(own.shape, BF16), pltpu.SemaphoreType.DMA],
+        compiler_params=pltpu.CompilerParams(vmem_limit_bytes=VMEM_LIMIT),
+        name="total",
+    )(own, *terms)
+
+
 def shards(tokens, w_qkv, w_pos, w_out, content_bias, position_bias, doc_ids):
     rows = tokens.shape[0]
     count = lax.axis_size("mp")
@@ -352,8 +375,11 @@
     last = chips - 1
     acc = None
     for k in range(last):
-        acc = kv_step({(k, 0): mine[k], (k, 1): other[k]}, w_kv, acc)
-    part = {(last, 0): mine[last], (last, 1): other[last]}
+        part = {(k, 0): mine[k], (k, 1): other[k]}
+        if k == last - 1:
+            part[last, 0] = mine[last]
+        acc = kv_step(part, w_kv, acc)
+    part = {(last, 1): other[last]}
     own_key = kv_step(part, w_kv, acc, (1,), "keys", docs, content_bias.shape[0])
     mem_key = onward(own_key)
     own_val = kv_step(part, w_kv, acc, (2,), "values")
@@ -380,11 +406,8 @@
     away = swap(away)
     for i, k in enumerate(others):
         total[k] = keep[i + 1] + away[i].astype(F32)
-    result = total[0]
-    for k in [first] + others:
-        if k > 0:
-            result = result + across(total[k].astype(BF16), k).astype(F32)
-    return result.astype(BF16)
+    terms = [across(total[k].astype(BF16), k) for k in [first] + others if k > 0]
+    return total_sum(total[0], terms)
 
 
 def solution(mesh):

time: 42.7 us -> 42.8 us (level)
  other arithmetic: 0.84 us -> 0.14 us
  Pallas kernels: 12.8 us -> 13.5 us
    pallas_call x0 -> x1, Pallas kernels: none -> 0.72 us  [total_sum(): pl.pallas_call(total_kernel, out_shape=jax.ShapeDtypeStruct(own.shape, BF...]
    convert_element_type x2 -> x1, other arithmetic: 0.8 us -> 0.11 us  [shards(): total[k].astype(BF16)]
where the time goes in v8:
time: 42.8 us; the launch traced here: 42.3 us
  starting transfers between devices  16.9 us (39%)
  Pallas kernels  13.5 us (32%)
  waiting for transfers between devices  11.6 us (27%)
    ppermute x6, starting transfers between devices, across(): lax.ppermute(value, 'mp', [(i, (i + 2 * k) % count) for i in range(count)])  12.9 us
    ppermute x6, waiting for transfers between devices, across(): lax.ppermute(value, 'mp', [(i, (i + 2 * k) % count) for i in range(count)])  9.8 us
    pallas_call x1, Pallas kernels, load(): call(functools.partial(load_kernel, parts), (pltpu.VMEM((rows, cols), BF1...  4.76 us
    pallas_call x1, Pallas kernels, queries(): call(functools.partial(q_kernel, count, heads), (pltpu.VMEM((rows, cols),...  3.56 us
    ppermute x2, starting transfers between devices, onward(): lax.ppermute(value, 'seq', [(i, (i + 1) % segments) for i in range(segmen...  3.09 us
    pallas_call x5, Pallas kernels, kv_step(): call(functools.partial(kv_kernel, sources, kinds, acc is None, last), out...  1.98 us
    pallas_call x1, Pallas kernels, weigh(): call(weigh_kernel, (pltpu.VMEM((heads, rows, rows), BF16), pltpu.VMEM((ro...  1.46 us
    ppermute x2, waiting for transfers between devices, onward(): lax.ppermute(value, 'seq', [(i, (i + 1) % segments) for i in range(segmen...  1.1 us
  transfers between devices with their start and end apart: 14, of which 7 were waited for; matrix products, arithmetic and copies ran while one was open for 0% of the time, Pallas kernels for 29%

profile of v8, /device:TPU:0, one launch (start us, length us, event | category | flops | bytes accessed | tf_op | source)
XLA Modules:
  0.0 42.3 jit_solution(12241715606003563867)
XLA Ops:
  0.0 3.0 %collective-permute-start.1 = (bf16[128,512]{1,0:T(8,128)(2,1)}, bf16[128,512]{1,0:T(8,128)(2,1)S(1)}, u32[]{:S(2)}, u32[]{:S(2)}) collective-permute-start(bf16[128,512]{1,0:T(8,128)(2,1)} %refs_0_.3), channel_id=1, source_target_pairs={{0,2},{1,3},{2,4},{3,5},{4,6},{5,7},{6,0},{7,1},{8,10},{9,11},{10,... | collective-permute-start | bytes 393224 | tf_op jit(solution)/shard_map/ppermute | solution.py:360
  3.0 2.6 %collective-permute-start.3 = (bf16[128,512]{1,0:T(8,128)(2,1)}, bf16[128,512]{1,0:T(8,128)(2,1)S(1)}, u32[]{:S(2)}, u32[]{:S(2)}) collective-permute-start(bf16[128,512]{1,0:T(8,128)(2,1)} %refs_0_.3), channel_id=1, source_target_pairs={{0,4},{1,5},{2,6},{3,7},{4,0},{5,1},{6,2},{7,3},{8,12},{9,13},{10,... | collective-permute-start | bytes 393224 | tf_op jit(solution)/shard_map/ppermute | solution.py:360
  5.6 1.3 %collective-permute-start.5 = (bf16[128,512]{1,0:T(8,128)(2,1)}, bf16[128,512]{1,0:T(8,128)(2,1)S(1)}, u32[]{:S(2)}, u32[]{:S(2)}) collective-permute-start(bf16[128,512]{1,0:T(8,128)(2,1)} %refs_0_.3), channel_id=1, source_target_pairs={{0,6},{1,7},{2,0},{3,1},{4,2},{5,3},{6,4},{7,5},{8,14},{9,15},{10,... | collective-permute-start | bytes 393224 | tf_op jit(solution)/shard_map/ppermute | solution.py:360
  7.0 4.8 %load.1 = (bf16[256,512]{1,0:T(8,128)(2,1)S(1)}, bf16[2,4096,512]{2,1,0:T(8,128)(2,1)S(1)}) custom-call(bf16[4096,512]{1,0:T(8,128)(2,1)} %w_pos.1, bf16[3,4096,512]{2,1,0:T(8,128)(2,1)} %refs_8_.1), custom_call_target="tpu_custom_call" | custom-call | flops 1048576 | bytes 1048576 | tf_op jit(solution)/shard_map/load/pallas_call | solution.py:93
  12.0 2.5 %collective-permute-done.3.refs_0_.refs_4_ = bf16[128,512]{1,0:T(8,128)(2,1)S(1)} collective-permute-done((bf16[128,512]{1,0:T(8,128)(2,1)}, bf16[128,512]{1,0:T(8,128)(2,1)S(1)}, u32[]{:S(2)}, u32[]{:S(2)}) %collective-permute-start.3) | collective-permute-done | bytes 131104 | tf_op jit(solution)/shard_map/ppermute | solution.py:360
  14.9 0.3 collective-permute-start.6
  15.2 0.4 %kv_step.5.refs_3_ = f32[2,128,512]{2,1,0:T(8,128)S(1)} custom-call(bf16[128,512]{1,0:T(8,128)(2,1)S(1)} %copy-done, bf16[128,512]{1,0:T(8,128)(2,1)S(1)} %collective-permute-done.refs_1_, bf16[2,4096,512]{2,1,0:T(8,128)(2,1)S(1)} %get-tuple-element.32.refs_2_.refs_3_.refs_1_), custom_call_target="tpu_custom_call" | custom-call | flops 536870912 | tf_op jit(solution)/shard_map/kv_step/pallas_call | solution.py:158
  15.6 0.5 %kv_step.6.refs_4_ = f32[2,128,512]{2,1,0:T(8,128)S(1)} custom-call(bf16[128,512]{1,0:T(8,128)(2,1)S(1)} %collective-permute-done.1.refs_0_.refs_2_, bf16[128,512]{1,0:T(8,128)(2,1)S(1)} %collective-permute-done.2.refs_1_.refs_3_, bf16[2,4096,512]{2,1,0:T(8,128)(2,1)S(1)} %get-tuple-element.32.refs_2_.refs_3_.refs_1_, f32[2,128,512]{2,1,0:T(8,128)S(1)} %kv_step.5.refs_3_), custom_call_target="tpu_custom_call" | custom-call | flops 536870912 | tf_op jit(solution)/shard_map/kv_step/pallas_call | solution.py:158
  16.1 0.6 %kv_step.7.refs_2_ = f32[2,128,512]{2,1,0:T(8,128)S(1)} custom-call(bf16[128,512]{1,0:T(8,128)(2,1)S(1)} %collective-permute-done.3.refs_0_.refs_4_, bf16[128,512]{1,0:T(8,128)(2,1)S(1)} %collective-permute-done.4.refs_1_.refs_5_, bf16[128,512]{1,0:T(8,128)(2,1)S(1)} %collective-permute-done.5.refs_2_.refs_6_, ...), custom_call_target="tpu_custom_call" | custom-call | flops 536870912 | tf_op jit(solution)/shard_map/kv_step/pallas_call | solution.py:158
  17.0 1.5 %collective-permute-start.7 = (bf16[528,128]{1,0:T(8,128)(2,1)S(1)}, bf16[528,128]{1,0:T(8,128)(2,1)S(1)}, u32[]{:S(2)}, u32[]{:S(2)}) collective-permute-start(bf16[528,128]{1,0:T(8,128)(2,1)S(1)} %kv_step.8.refs_12_), channel_id=1, source_target_pairs={{0,8},{8,16},{16,24},{24,0},{1,9},{9,17},{17,25},{25,1},{2,10},{10... | collective-permute-start | bytes 405512 | tf_op jit(solution)/shard_map/ppermute | solution.py:366
  18.8 1.5 %collective-permute-start.8 = (bf16[128,512]{1,0:T(8,128)(2,1)S(1)}, bf16[128,512]{1,0:T(8,128)(2,1)S(1)}, u32[]{:S(2)}, u32[]{:S(2)}) collective-permute-start(bf16[128,512]{1,0:T(8,128)(2,1)S(1)} %kv_step.9.val_ref), channel_id=1, source_target_pairs={{0,8},{8,16},{16,24},{24,0},{1,9},{9,17},{17,25},{25,1},{2,10},{10... | collective-permute-start | bytes 393224 | tf_op jit(solution)/shard_map/ppermute | solution.py:366
  20.3 3.6 %queries.1 = (bf16[128,512]{1,0:T(8,128)(2,1)S(1)}, f32[4,128,256]{2,1,0:T(8,128)S(1)}, bf16[512,4096]{1,0:T(8,128)(2,1)S(1)}) custom-call(bf16[128,512]{1,0:T(8,128)(2,1)S(1)} %copy-done, bf16[128,512]{1,0:T(8,128)(2,1)S(1)} %collective-permute-done.refs_1_, bf16[128,512]{1,0:T(8,128)(2,1)S(1)} %collective-permute-done.1.refs_0_.refs_2_, ...), custom_call_target="tpu_custom_call" | custom-call | flops 536870912 | bytes 4194304 | tf_op jit(solution)/shard_map/queries/pallas_call | solution.py:214
  23.9 0.5 %collective-permute-done.7.mem_ref = bf16[528,128]{1,0:T(8,128)(2,1)S(1)} collective-permute-done((bf16[528,128]{1,0:T(8,128)(2,1)S(1)}, bf16[528,128]{1,0:T(8,128)(2,1)S(1)}, u32[]{:S(2)}, u32[]{:S(2)}) %collective-permute-start.7) | collective-permute-done | bytes 135200 | tf_op jit(solution)/shard_map/ppermute | solution.py:366
  24.4 1.5 %weigh.1 = (bf16[4,128,128]{2,1,0:T(8,128)(2,1)S(1)}, f32[128,512]{1,0:T(8,128)S(1)}) custom-call(bf16[128,512]{1,0:T(8,128)(2,1)S(1)} %get-tuple-element.35.qc_ref, f32[4,128,256]{2,1,0:T(8,128)S(1)} %get-tuple-element.36.score_ref, bf16[528,128]{1,0:T(8,128)(2,1)S(1)} %collective-permute-done.7.mem_ref, bf16[128,512]{1,0:T(8,128)(2,1)S(1)} %kv_step.9.val_ref, ...), custom_call_target="tpu_custom_call" | custom-call | flops 67108864 | bytes 524288 | tf_op jit(solution)/shard_map/weigh/pallas_call | solution.py:264
  25.8 0.6 %collective-permute-done.8.mem_ref = bf16[128,512]{1,0:T(8,128)(2,1)S(1)} collective-permute-done((bf16[128,512]{1,0:T(8,128)(2,1)S(1)}, bf16[128,512]{1,0:T(8,128)(2,1)S(1)}, u32[]{:S(2)}, u32[]{:S(2)}) %collective-permute-start.8) | collective-permute-done | bytes 131104 | tf_op jit(solution)/shard_map/ppermute | solution.py:366
  26.5 0.3 mix.1
  26.9 0.7 %rest.1 = (bf16[3,128,512]{2,1,0:T(8,128)(2,1)S(1)}, f32[4,128,512]{2,1,0:T(8,128)S(1)}) custom-call(bf16[128,512]{1,0:T(8,128)(2,1)S(1)} %get-tuple-element.41.head_ref, bf16[512,4096]{1,0:T(8,128)(2,1)S(1)} %get-tuple-element.40.w_ref), custom_call_target="tpu_custom_call" | custom-call | flops 536870912 | bytes 4194304 | tf_op jit(solution)/shard_map/rest/pallas_call | solution.py:315
  27.6 0.7 %collective-permute-done.9 = bf16[1,128,512]{2,1,0:T(8,128)(2,1)S(1)} collective-permute-done((bf16[1,128,512]{2,1,0:T(8,128)(2,1)S(1)}, bf16[1,128,512]{2,1,0:T(8,128)(2,1)S(1)}, u32[]{:S(2)}, u32[]{:S(2)}) %collective-permute-start.9) | collective-permute-done | bytes 131104 | tf_op jit(solution)/shard_map/ppermute | solution.py:363
  28.5 2.1 %collective-permute-start.11 = (bf16[128,512]{1,0:T(8,128)(2,1)S(1)}, bf16[128,512]{1,0:T(8,128)(2,1)S(1)}, u32[]{:S(2)}, u32[]{:S(2)}) collective-permute-start(bf16[128,512]{1,0:T(8,128)(2,1)S(1)} %add_bitcast_fusion.1), channel_id=1, source_target_pairs={{0,4},{1,5},{2,6},{3,7},{4,0},{5,1},{6,2},{7,3},{8,12},{9,13},{10,... | collective-permute-start | bytes 393224 | tf_op jit(solution)/shard_map/ppermute | solution.py:360
  30.7 2.6 %collective-permute-start.12 = (bf16[128,512]{1,0:T(8,128)(2,1)S(1)}, bf16[128,512]{1,0:T(8,128)(2,1)S(1)}, u32[]{:S(2)}, u32[]{:S(2)}) collective-permute-start(bf16[128,512]{1,0:T(8,128)(2,1)S(1)} %get-tuple-element.48), channel_id=1, source_target_pairs={{0,2},{1,3},{2,4},{3,5},{4,6},{5,7},{6,0},{7,1},{8,10},{9,11},{10,... | collective-permute-start | bytes 393224 | tf_op jit(solution)/shard_map/ppermute | solution.py:360
  33.3 1.3 %collective-permute-start.13 = (bf16[128,512]{1,0:T(8,128)(2,1)S(1)}, bf16[128,512]{1,0:T(8,128)(2,1)S(1)}, u32[]{:S(2)}, u32[]{:S(2)}) collective-permute-start(bf16[128,512]{1,0:T(8,128)(2,1)S(1)} %get-tuple-element.47), channel_id=1, source_target_pairs={{0,6},{1,7},{2,0},{3,1},{4,2},{5,3},{6,4},{7,5},{8,14},{9,15},{10,... | collective-permute-start | bytes 393224 | tf_op jit(solution)/shard_map/ppermute | solution.py:360
  34.6 6.4 %collective-permute-done.11.refs_0_ = bf16[128,512]{1,0:T(8,128)(2,1)S(1)} collective-permute-done((bf16[128,512]{1,0:T(8,128)(2,1)S(1)}, bf16[128,512]{1,0:T(8,128)(2,1)S(1)}, u32[]{:S(2)}, u32[]{:S(2)}) %collective-permute-start.11) | collective-permute-done | bytes 131104 | tf_op jit(solution)/shard_map/ppermute | solution.py:360
  41.0 0.6 %collective-permute-done.13.refs_2_ = bf16[128,512]{1,0:T(8,128)(2,1)S(1)} collective-permute-done((bf16[128,512]{1,0:T(8,128)(2,1)S(1)}, bf16[128,512]{1,0:T(8,128)(2,1)S(1)}, u32[]{:S(2)}, u32[]{:S(2)}) %collective-permute-start.13) | collective-permute-done | bytes 131104 | tf_op jit(solution)/shard_map/ppermute | solution.py:360
  41.6 0.7 %total.1 = bf16[128,512]{1,0:T(8,128)(2,1)} custom-call(f32[128,512]{1,0:T(8,128)S(1)} %get-tuple-element.49.own_ref, bf16[128,512]{1,0:T(8,128)(2,1)S(1)} %collective-permute-done.11.refs_0_, bf16[128,512]{1,0:T(8,128)(2,1)S(1)} %collective-permute-done.12.refs_1_, bf16[128,512]{1,0:T(8,128)(2,1)S(1)} %collective-permute-done.13.refs_2_), custom_call_target="tpu_custom_call" | custom-call | tf_op jit(solution)/shard_map/total/pallas_call | solution.py:341
  (26 shorter events, 1.5 us)
Async XLA Ops:
  0.0 15.2 %copy-start = (bf16[128,512]{1,0:T(8,128)(2,1)S(1)}, bf16[128,512]{1,0:T(8,128)(2,1)}, u32[]{:S(2)}) copy-start(bf16[128,512]{1,0:T(8,128)(2,1)} %refs_0_.3) | copy-start | bytes 393220
  0.0 14.6 %copy-start.3 = (s32[128]{0:T(128)S(1)}, s32[128]{0:T(128)}, u32[]{:S(2)}) copy-start(s32[128]{0:T(128)} %param.13) | copy-start | bytes 1540
  0.0 11.7 %collective-permute-start.1 = (bf16[128,512]{1,0:T(8,128)(2,1)}, bf16[128,512]{1,0:T(8,128)(2,1)S(1)}, u32[]{:S(2)}, u32[]{:S(2)}) collective-permute-start(bf16[128,512]{1,0:T(8,128)(2,1)} %refs_0_.3), channel_id=1, source_target_pairs={{0,2},{1,3},{2,4},{3,5},{4,6},{5,7},{6,0},{7,1},{8,10},{9,11},{10,... | collective-permute-start | bytes 393224 | tf_op jit(solution)/shard_map/ppermute | solution.py:360
  3.0 11.6 %collective-permute-start.3 = (bf16[128,512]{1,0:T(8,128)(2,1)}, bf16[128,512]{1,0:T(8,128)(2,1)S(1)}, u32[]{:S(2)}, u32[]{:S(2)}) collective-permute-start(bf16[128,512]{1,0:T(8,128)(2,1)} %refs_0_.3), channel_id=1, source_target_pairs={{0,4},{1,5},{2,6},{3,7},{4,0},{5,1},{6,2},{7,3},{8,12},{9,13},{10,... | collective-permute-start | bytes 393224 | tf_op jit(solution)/shard_map/ppermute | solution.py:360
  5.6 9.6 %collective-permute-start = (bf16[128,512]{1,0:T(8,128)(2,1)}, bf16[128,512]{1,0:T(8,128)(2,1)S(1)}, u32[]{:S(2)}, u32[]{:S(2)}) collective-permute-start(bf16[128,512]{1,0:T(8,128)(2,1)} %refs_0_.3), channel_id=1, source_target_pairs={{0,1},{1,0},{2,3},{3,2},{4,5},{5,4},{6,7},{7,6},{8,9},{9,8},{10,11... | collective-permute-start | bytes 393224 | tf_op jit(solution)/shard_map/ppermute | solution.py:363
  5.6 9.2 %collective-permute-start.5 = (bf16[128,512]{1,0:T(8,128)(2,1)}, bf16[128,512]{1,0:T(8,128)(2,1)S(1)}, u32[]{:S(2)}, u32[]{:S(2)}) collective-permute-start(bf16[128,512]{1,0:T(8,128)(2,1)} %refs_0_.3), channel_id=1, source_target_pairs={{0,6},{1,7},{2,0},{3,1},{4,2},{5,3},{6,4},{7,5},{8,14},{9,15},{10,... | collective-permute-start | bytes 393224 | tf_op jit(solution)/shard_map/ppermute | solution.py:360
  11.7 3.9 %collective-permute-start.2 = (bf16[128,512]{1,0:T(8,128)(2,1)S(1)}, bf16[128,512]{1,0:T(8,128)(2,1)S(1)}, u32[]{:S(2)}, u32[]{:S(2)}) collective-permute-start(bf16[128,512]{1,0:T(8,128)(2,1)S(1)} %collective-permute-done.1.refs_0_.refs_2_), channel_id=1, source_target_pairs={{0,1},{1,0},{2,3},{3,2},{4,5},{5,4},{6,7},{7,6},{8,9},{9,8},{10,11... | collective-permute-start | bytes 393224 | tf_op jit(solution)/shard_map/ppermute | solution.py:363
  14.6 1.5 %collective-permute-start.4 = (bf16[128,512]{1,0:T(8,128)(2,1)S(1)}, bf16[128,512]{1,0:T(8,128)(2,1)S(1)}, u32[]{:S(2)}, u32[]{:S(2)}) collective-permute-start(bf16[128,512]{1,0:T(8,128)(2,1)S(1)} %collective-permute-done.3.refs_0_.refs_4_), channel_id=1, source_target_pairs={{0,1},{1,0},{2,3},{3,2},{4,5},{5,4},{6,7},{7,6},{8,9},{9,8},{10,11... | collective-permute-start | bytes 393224 | tf_op jit(solution)/shard_map/ppermute | solution.py:363
  14.9 1.9 %collective-permute-start.6 = (bf16[128,512]{1,0:T(8,128)(2,1)S(1)}, bf16[128,512]{1,0:T(8,128)(2,1)S(1)}, u32[]{:S(2)}, u32[]{:S(2)}) collective-permute-start(bf16[128,512]{1,0:T(8,128)(2,1)S(1)} %collective-permute-done.5.refs_2_.refs_6_), channel_id=1, source_target_pairs={{0,1},{1,0},{2,3},{3,2},{4,5},{5,4},{6,7},{7,6},{8,9},{9,8},{10,11... | collective-permute-start | bytes 393224 | tf_op jit(solution)/shard_map/ppermute | solution.py:363
  17.0 3.4 %copy-start.1 = (f32[4,128]{1,0:T(4,128)S(1)}, f32[4,128]{1,0:T(4,128)}, u32[]{:S(2)}) copy-start(f32[4,128]{1,0:T(4,128)} %param.11) | copy-start | bytes 6148
  17.0 3.3 %copy-start.2 = (f32[4,128]{1,0:T(4,128)S(1)}, f32[4,128]{1,0:T(4,128)}, u32[]{:S(2)}) copy-start(f32[4,128]{1,0:T(4,128)} %param.12) | copy-start | bytes 6148
  17.0 7.4 %collective-permute-start.7 = (bf16[528,128]{1,0:T(8,128)(2,1)S(1)}, bf16[528,128]{1,0:T(8,128)(2,1)S(1)}, u32[]{:S(2)}, u32[]{:S(2)}) collective-permute-start(bf16[528,128]{1,0:T(8,128)(2,1)S(1)} %kv_step.8.refs_12_), channel_id=1, source_target_pairs={{0,8},{8,16},{16,24},{24,0},{1,9},{9,17},{17,25},{25,1},{2,10},{10... | collective-permute-start | bytes 405512 | tf_op jit(solution)/shard_map/ppermute | solution.py:366
  18.8 7.7 %collective-permute-start.8 = (bf16[128,512]{1,0:T(8,128)(2,1)S(1)}, bf16[128,512]{1,0:T(8,128)(2,1)S(1)}, u32[]{:S(2)}, u32[]{:S(2)}) collective-permute-start(bf16[128,512]{1,0:T(8,128)(2,1)S(1)} %kv_step.9.val_ref), channel_id=1, source_target_pairs={{0,8},{8,16},{16,24},{24,0},{1,9},{9,17},{17,25},{25,1},{2,10},{10... | collective-permute-start | bytes 393224 | tf_op jit(solution)/shard_map/ppermute | solution.py:366
  26.8 1.4 %collective-permute-start.9 = (bf16[1,128,512]{2,1,0:T(8,128)(2,1)S(1)}, bf16[1,128,512]{2,1,0:T(8,128)(2,1)S(1)}, u32[]{:S(2)}, u32[]{:S(2)}) collective-permute-start(bf16[1,128,512]{2,1,0:T(8,128)(2,1)S(1)} %get-tuple-element.44), channel_id=1, source_target_pairs={{0,1},{1,0},{2,3},{3,2},{4,5},{5,4},{6,7},{7,6},{8,9},{9,8},{10,11... | collective-permute-start | bytes 393224 | tf_op jit(solution)/shard_map/ppermute | solution.py:363
  28.3 2.3 %collective-permute-start.10 = (bf16[3,128,512]{2,1,0:T(8,128)(2,1)S(1)}, bf16[3,128,512]{2,1,0:T(8,128)(2,1)S(1)}, u32[]{:S(2)}, u32[]{:S(2)}) collective-permute-start(bf16[3,128,512]{2,1,0:T(8,128)(2,1)S(1)} %get-tuple-element.45), channel_id=1, source_target_pairs={{0,1},{1,0},{2,3},{3,2},{4,5},{5,4},{6,7},{7,6},{8,9},{9,8},{10,11... | collective-permute-start | bytes 1179656 | tf_op jit(solution)/shard_map/ppermute | solution.py:363
  28.5 12.5 %collective-permute-start.11 = (bf16[128,512]{1,0:T(8,128)(2,1)S(1)}, bf16[128,512]{1,0:T(8,128)(2,1)S(1)}, u32[]{:S(2)}, u32[]{:S(2)}) collective-permute-start(bf16[128,512]{1,0:T(8,128)(2,1)S(1)} %add_bitcast_fusion.1), channel_id=1, source_target_pairs={{0,4},{1,5},{2,6},{3,7},{4,0},{5,1},{6,2},{7,3},{8,12},{9,13},{10,... | collective-permute-start | bytes 393224 | tf_op jit(solution)/shard_map/ppermute | solution.py:360
  30.7 10.3 %collective-permute-start.12 = (bf16[128,512]{1,0:T(8,128)(2,1)S(1)}, bf16[128,512]{1,0:T(8,128)(2,1)S(1)}, u32[]{:S(2)}, u32[]{:S(2)}) collective-permute-start(bf16[128,512]{1,0:T(8,128)(2,1)S(1)} %get-tuple-element.48), channel_id=1, source_target_pairs={{0,2},{1,3},{2,4},{3,5},{4,6},{5,7},{6,0},{7,1},{8,10},{9,11},{10,... | collective-permute-start | bytes 393224 | tf_op jit(solution)/shard_map/ppermute | solution.py:360
  33.3 8.3 %collective-permute-start.13 = (bf16[128,512]{1,0:T(8,128)(2,1)S(1)}, bf16[128,512]{1,0:T(8,128)(2,1)S(1)}, u32[]{:S(2)}, u32[]{:S(2)}) collective-permute-start(bf16[128,512]{1,0:T(8,128)(2,1)S(1)} %get-tuple-element.47), channel_id=1, source_target_pairs={{0,6},{1,7},{2,0},{3,1},{4,2},{5,3},{6,4},{7,5},{8,14},{9,15},{10,... | collective-permute-start | bytes 393224 | tf_op jit(solution)/shard_map/ppermute | solution.py:360

commit v9 on v7

--- a/solution.py
+++ b/solution.py
@@ -9,7 +9,7 @@
 
 BF16 = jnp.bfloat16
 F32 = jnp.float32
-VMEM_LIMIT = 24 * 1024 * 1024
+VMEM_LIMIT = 16 * 1024 * 1024
 
 
 def vmem_spec():

time: 42.7 us -> 42.7 us (level)
  no operation moved by 1% of the time
where the time goes in v9:
time: 42.7 us; the launch traced here: 42.2 us
  starting transfers between devices  16.9 us (40%)
  Pallas kernels  12.8 us (30%)
  waiting for transfers between devices  11.5 us (27%)
  other arithmetic  0.84 us (2%)
    ppermute x6, starting transfers between devices, across(): lax.ppermute(value, 'mp', [(i, (i + 2 * k) % count) for i in range(count)])  12.9 us
    ppermute x6, waiting for transfers between devices, across(): lax.ppermute(value, 'mp', [(i, (i + 2 * k) % count) for i in range(count)])  9.8 us
    pallas_call x1, Pallas kernels, load(): call(functools.partial(load_kernel, parts), (pltpu.VMEM((rows, cols), BF1...  4.76 us
    pallas_call x1, Pallas kernels, queries(): call(functools.partial(q_kernel, count, heads), (pltpu.VMEM((rows, cols),...  3.56 us
    ppermute x2, starting transfers between devices, onward(): lax.ppermute(value, 'seq', [(i, (i + 1) % segments) for i in range(segmen...  3.08 us
    pallas_call x5, Pallas kernels, kv_step(): call(functools.partial(kv_kernel, sources, kinds, acc is None, last), out...  2 us
    pallas_call x1, Pallas kernels, weigh(): call(weigh_kernel, (pltpu.VMEM((heads, rows, rows), BF16), pltpu.VMEM((ro...  1.46 us
    ppermute x2, waiting for transfers between devices, onward(): lax.ppermute(value, 'seq', [(i, (i + 1) % segments) for i in range(segmen...  1.04 us
  transfers between devices with their start and end apart: 14, of which 7 were waited for; matrix products, arithmetic and copies ran while one was open for 0% of the time, Pallas kernels for 29%

profile of v9, /device:TPU:0, one launch (start us, length us, event | category | flops | bytes accessed | tf_op | source)
XLA Modules:
  0.0 42.2 jit_solution(8246039380916137373)
XLA Ops:
  0.0 3.0 %collective-permute-start.1 = (bf16[128,512]{1,0:T(8,128)(2,1)}, bf16[128,512]{1,0:T(8,128)(2,1)S(1)}, u32[]{:S(2)}, u32[]{:S(2)}) collective-permute-start(bf16[128,512]{1,0:T(8,128)(2,1)} %refs_0_.3), channel_id=1, source_target_pairs={{0,2},{1,3},{2,4},{3,5},{4,6},{5,7},{6,0},{7,1},{8,10},{9,11},{10,... | collective-permute-start | bytes 393224 | tf_op jit(solution)/shard_map/ppermute | solution.py:337
  3.0 2.6 %collective-permute-start.3 = (bf16[128,512]{1,0:T(8,128)(2,1)}, bf16[128,512]{1,0:T(8,128)(2,1)S(1)}, u32[]{:S(2)}, u32[]{:S(2)}) collective-permute-start(bf16[128,512]{1,0:T(8,128)(2,1)} %refs_0_.3), channel_id=1, source_target_pairs={{0,4},{1,5},{2,6},{3,7},{4,0},{5,1},{6,2},{7,3},{8,12},{9,13},{10,... | collective-permute-start | bytes 393224 | tf_op jit(solution)/shard_map/ppermute | solution.py:337
  5.6 1.3 %collective-permute-start.5 = (bf16[128,512]{1,0:T(8,128)(2,1)}, bf16[128,512]{1,0:T(8,128)(2,1)S(1)}, u32[]{:S(2)}, u32[]{:S(2)}) collective-permute-start(bf16[128,512]{1,0:T(8,128)(2,1)} %refs_0_.3), channel_id=1, source_target_pairs={{0,6},{1,7},{2,0},{3,1},{4,2},{5,3},{6,4},{7,5},{8,14},{9,15},{10,... | collective-permute-start | bytes 393224 | tf_op jit(solution)/shard_map/ppermute | solution.py:337
  7.0 4.8 %load.1 = (bf16[256,512]{1,0:T(8,128)(2,1)S(1)}, bf16[2,4096,512]{2,1,0:T(8,128)(2,1)S(1)}) custom-call(bf16[4096,512]{1,0:T(8,128)(2,1)} %w_pos.1, bf16[3,4096,512]{2,1,0:T(8,128)(2,1)} %refs_8_.1), custom_call_target="tpu_custom_call" | custom-call | flops 1048576 | bytes 1048576 | tf_op jit(solution)/shard_map/load/pallas_call | solution.py:93
  12.0 2.5 %collective-permute-done.3.refs_0_.refs_4_ = bf16[128,512]{1,0:T(8,128)(2,1)S(1)} collective-permute-done((bf16[128,512]{1,0:T(8,128)(2,1)}, bf16[128,512]{1,0:T(8,128)(2,1)S(1)}, u32[]{:S(2)}, u32[]{:S(2)}) %collective-permute-start.3) | collective-permute-done | bytes 131104 | tf_op jit(solution)/shard_map/ppermute | solution.py:337
  15.2 0.4 %kv_step.5.refs_3_ = f32[2,128,512]{2,1,0:T(8,128)S(1)} custom-call(bf16[128,512]{1,0:T(8,128)(2,1)S(1)} %copy-done, bf16[128,512]{1,0:T(8,128)(2,1)S(1)} %collective-permute-done.refs_1_, bf16[2,4096,512]{2,1,0:T(8,128)(2,1)S(1)} %get-tuple-element.32.refs_2_), custom_call_target="tpu_custom_call" | custom-call | flops 536870912 | tf_op jit(solution)/shard_map/kv_step/pallas_call | solution.py:158
  15.6 0.5 %kv_step.6.refs_3_ = f32[2,128,512]{2,1,0:T(8,128)S(1)} custom-call(bf16[128,512]{1,0:T(8,128)(2,1)S(1)} %collective-permute-done.1.refs_0_.refs_2_, bf16[128,512]{1,0:T(8,128)(2,1)S(1)} %collective-permute-done.2.refs_1_.refs_3_, bf16[2,4096,512]{2,1,0:T(8,128)(2,1)S(1)} %get-tuple-element.32.refs_2_, f32[2,128,512]{2,1,0:T(8,128)S(1)} %kv_step.5.refs_3_), custom_call_target="tpu_custom_call" | custom-call | flops 536870912 | tf_op jit(solution)/shard_map/kv_step/pallas_call | solution.py:158
  16.1 0.5 %kv_step.7.refs_3_ = f32[2,128,512]{2,1,0:T(8,128)S(1)} custom-call(bf16[128,512]{1,0:T(8,128)(2,1)S(1)} %collective-permute-done.3.refs_0_.refs_4_, bf16[128,512]{1,0:T(8,128)(2,1)S(1)} %collective-permute-done.4.refs_1_.refs_5_, bf16[2,4096,512]{2,1,0:T(8,128)(2,1)S(1)} %get-tuple-element.32.refs_2_, f32[2,128,512]{2,1,0:T(8,128)S(1)} %kv_step.6.refs_3_), custom_call_target="tpu_custom_call" | custom-call | flops 536870912 | tf_op jit(solution)/shard_map/kv_step/pallas_call | solution.py:158
  16.6 0.3 kv_step.8.refs_12_
  17.0 1.5 %collective-permute-start.7 = (bf16[528,128]{1,0:T(8,128)(2,1)S(1)}, bf16[528,128]{1,0:T(8,128)(2,1)S(1)}, u32[]{:S(2)}, u32[]{:S(2)}) collective-permute-start(bf16[528,128]{1,0:T(8,128)(2,1)S(1)} %kv_step.8.refs_12_), channel_id=1, source_target_pairs={{0,8},{8,16},{16,24},{24,0},{1,9},{9,17},{17,25},{25,1},{2,10},{10... | collective-permute-start | bytes 405512 | tf_op jit(solution)/shard_map/ppermute | solution.py:343
  18.8 1.5 %collective-permute-start.8 = (bf16[128,512]{1,0:T(8,128)(2,1)S(1)}, bf16[128,512]{1,0:T(8,128)(2,1)S(1)}, u32[]{:S(2)}, u32[]{:S(2)}) collective-permute-start(bf16[128,512]{1,0:T(8,128)(2,1)S(1)} %kv_step.9.val_ref), channel_id=1, source_target_pairs={{0,8},{8,16},{16,24},{24,0},{1,9},{9,17},{17,25},{25,1},{2,10},{10... | collective-permute-start | bytes 393224 | tf_op jit(solution)/shard_map/ppermute | solution.py:343
  20.4 3.6 %queries.1 = (bf16[128,512]{1,0:T(8,128)(2,1)S(1)}, f32[4,128,256]{2,1,0:T(8,128)S(1)}, bf16[512,4096]{1,0:T(8,128)(2,1)S(1)}) custom-call(bf16[128,512]{1,0:T(8,128)(2,1)S(1)} %copy-done, bf16[128,512]{1,0:T(8,128)(2,1)S(1)} %collective-permute-done.refs_1_, bf16[128,512]{1,0:T(8,128)(2,1)S(1)} %collective-permute-done.1.refs_0_.refs_2_, ...), custom_call_target="tpu_custom_call" | custom-call | flops 536870912 | bytes 4194304 | tf_op jit(solution)/shard_map/queries/pallas_call | solution.py:214
  23.9 0.4 collective-permute-done.7.mem_ref
  24.3 1.5 %weigh.1 = (bf16[4,128,128]{2,1,0:T(8,128)(2,1)S(1)}, f32[128,512]{1,0:T(8,128)S(1)}) custom-call(bf16[128,512]{1,0:T(8,128)(2,1)S(1)} %get-tuple-element.35.qc_ref, f32[4,128,256]{2,1,0:T(8,128)S(1)} %get-tuple-element.36.score_ref, bf16[528,128]{1,0:T(8,128)(2,1)S(1)} %collective-permute-done.7.mem_ref, bf16[128,512]{1,0:T(8,128)(2,1)S(1)} %kv_step.9.val_ref, ...), custom_call_target="tpu_custom_call" | custom-call | flops 67108864 | bytes 524288 | tf_op jit(solution)/shard_map/weigh/pallas_call | solution.py:264
  25.8 0.6 %collective-permute-done.8.mem_ref = bf16[128,512]{1,0:T(8,128)(2,1)S(1)} collective-permute-done((bf16[128,512]{1,0:T(8,128)(2,1)S(1)}, bf16[128,512]{1,0:T(8,128)(2,1)S(1)}, u32[]{:S(2)}, u32[]{:S(2)}) %collective-permute-start.8) | collective-permute-done | bytes 131104 | tf_op jit(solution)/shard_map/ppermute | solution.py:343
  26.4 0.3 mix.1
  26.9 0.7 %rest.1 = (bf16[3,128,512]{2,1,0:T(8,128)(2,1)S(1)}, f32[4,128,512]{2,1,0:T(8,128)S(1)}) custom-call(bf16[128,512]{1,0:T(8,128)(2,1)S(1)} %get-tuple-element.41.head_ref, bf16[512,4096]{1,0:T(8,128)(2,1)S(1)} %get-tuple-element.40.w_ref), custom_call_target="tpu_custom_call" | custom-call | flops 536870912 | bytes 4194304 | tf_op jit(solution)/shard_map/rest/pallas_call | solution.py:315
  27.5 0.7 %collective-permute-done.9 = bf16[1,128,512]{2,1,0:T(8,128)(2,1)S(1)} collective-permute-done((bf16[1,128,512]{2,1,0:T(8,128)(2,1)S(1)}, bf16[1,128,512]{2,1,0:T(8,128)(2,1)S(1)}, u32[]{:S(2)}, u32[]{:S(2)}) %collective-permute-start.9) | collective-permute-done | bytes 131104 | tf_op jit(solution)/shard_map/ppermute | solution.py:340
  28.4 2.1 %collective-permute-start.11 = (bf16[128,512]{1,0:T(8,128)(2,1)S(1)}, bf16[128,512]{1,0:T(8,128)(2,1)S(1)}, u32[]{:S(2)}, u32[]{:S(2)}) collective-permute-start(bf16[128,512]{1,0:T(8,128)(2,1)S(1)} %add_bitcast_fusion), channel_id=1, source_target_pairs={{0,4},{1,5},{2,6},{3,7},{4,0},{5,1},{6,2},{7,3},{8,12},{9,13},{10,... | collective-permute-start | bytes 393224 | tf_op jit(solution)/shard_map/ppermute | solution.py:337
  30.6 2.6 %collective-permute-start.12 = (bf16[128,512]{1,0:T(8,128)(2,1)S(1)}, bf16[128,512]{1,0:T(8,128)(2,1)S(1)}, u32[]{:S(2)}, u32[]{:S(2)}) collective-permute-start(bf16[128,512]{1,0:T(8,128)(2,1)S(1)} %get-tuple-element.47), channel_id=1, source_target_pairs={{0,2},{1,3},{2,4},{3,5},{4,6},{5,7},{6,0},{7,1},{8,10},{9,11},{10,... | collective-permute-start | bytes 393224 | tf_op jit(solution)/shard_map/ppermute | solution.py:337
  33.2 1.3 %collective-permute-start.13 = (bf16[128,512]{1,0:T(8,128)(2,1)S(1)}, bf16[128,512]{1,0:T(8,128)(2,1)S(1)}, u32[]{:S(2)}, u32[]{:S(2)}) collective-permute-start(bf16[128,512]{1,0:T(8,128)(2,1)S(1)} %get-tuple-element.48), channel_id=1, source_target_pairs={{0,6},{1,7},{2,0},{3,1},{4,2},{5,3},{6,4},{7,5},{8,14},{9,15},{10,... | collective-permute-start | bytes 393224 | tf_op jit(solution)/shard_map/ppermute | solution.py:337
  34.5 6.5 %collective-permute-done.11 = bf16[128,512]{1,0:T(8,128)(2,1)S(1)} collective-permute-done((bf16[128,512]{1,0:T(8,128)(2,1)S(1)}, bf16[128,512]{1,0:T(8,128)(2,1)S(1)}, u32[]{:S(2)}, u32[]{:S(2)}) %collective-permute-start.11) | collective-permute-done | bytes 131104 | tf_op jit(solution)/shard_map/ppermute | solution.py:337
  41.0 0.5 %collective-permute-done.13 = bf16[128,512]{1,0:T(8,128)(2,1)S(1)} collective-permute-done((bf16[128,512]{1,0:T(8,128)(2,1)S(1)}, bf16[128,512]{1,0:T(8,128)(2,1)S(1)}, u32[]{:S(2)}, u32[]{:S(2)}) %collective-permute-start.13) | collective-permute-done | bytes 131104 | tf_op jit(solution)/shard_map/ppermute | solution.py:337
  41.5 0.7 %fusion.2 = bf16[128,512]{1,0:T(8,128)(2,1)} fusion(bf16[128,512]{1,0:T(8,128)(2,1)S(1)} %collective-permute-done.13, bf16[128,512]{1,0:T(8,128)(2,1)S(1)} %collective-permute-done.12, bf16[128,512]{1,0:T(8,128)(2,1)S(1)} %collective-permute-done.11, f32[4,128,512]{2,1,0:T(8,128)S(1)} %get-tuple-element.42, bf16[3,128,512]{2,1,0:T(8,128)(2,1)S(1)} %collective-permute-done.10), kind=kLoop, calls=%fused_computation.3 | loop fusion | flops 589824 | bytes 917504 | tf_op jit(solution)/shard_map/convert_element_type | solution.py:387
  (26 shorter events, 1.6 us)
Async XLA Ops:
  0.0 15.2 %copy-start = (bf16[128,512]{1,0:T(8,128)(2,1)S(1)}, bf16[128,512]{1,0:T(8,128)(2,1)}, u32[]{:S(2)}) copy-start(bf16[128,512]{1,0:T(8,128)(2,1)} %refs_0_.3) | copy-start | bytes 393220
  0.0 14.6 %copy-start.3 = (s32[128]{0:T(128)S(1)}, s32[128]{0:T(128)}, u32[]{:S(2)}) copy-start(s32[128]{0:T(128)} %param.13) | copy-start | bytes 1540
  0.0 11.7 %collective-permute-start.1 = (bf16[128,512]{1,0:T(8,128)(2,1)}, bf16[128,512]{1,0:T(8,128)(2,1)S(1)}, u32[]{:S(2)}, u32[]{:S(2)}) collective-permute-start(bf16[128,512]{1,0:T(8,128)(2,1)} %refs_0_.3), channel_id=1, source_target_pairs={{0,2},{1,3},{2,4},{3,5},{4,6},{5,7},{6,0},{7,1},{8,10},{9,11},{10,... | collective-permute-start | bytes 393224 | tf_op jit(solution)/shard_map/ppermute | solution.py:337
  3.0 11.6 %collective-permute-start.3 = (bf16[128,512]{1,0:T(8,128)(2,1)}, bf16[128,512]{1,0:T(8,128)(2,1)S(1)}, u32[]{:S(2)}, u32[]{:S(2)}) collective-permute-start(bf16[128,512]{1,0:T(8,128)(2,1)} %refs_0_.3), channel_id=1, source_target_pairs={{0,4},{1,5},{2,6},{3,7},{4,0},{5,1},{6,2},{7,3},{8,12},{9,13},{10,... | collective-permute-start | bytes 393224 | tf_op jit(solution)/shard_map/ppermute | solution.py:337
  5.6 9.6 %collective-permute-start = (bf16[128,512]{1,0:T(8,128)(2,1)}, bf16[128,512]{1,0:T(8,128)(2,1)S(1)}, u32[]{:S(2)}, u32[]{:S(2)}) collective-permute-start(bf16[128,512]{1,0:T(8,128)(2,1)} %refs_0_.3), channel_id=1, source_target_pairs={{0,1},{1,0},{2,3},{3,2},{4,5},{5,4},{6,7},{7,6},{8,9},{9,8},{10,11... | collective-permute-start | bytes 393224 | tf_op jit(solution)/shard_map/ppermute | solution.py:340
  5.6 9.2 %collective-permute-start.5 = (bf16[128,512]{1,0:T(8,128)(2,1)}, bf16[128,512]{1,0:T(8,128)(2,1)S(1)}, u32[]{:S(2)}, u32[]{:S(2)}) collective-permute-start(bf16[128,512]{1,0:T(8,128)(2,1)} %refs_0_.3), channel_id=1, source_target_pairs={{0,6},{1,7},{2,0},{3,1},{4,2},{5,3},{6,4},{7,5},{8,14},{9,15},{10,... | collective-permute-start | bytes 393224 | tf_op jit(solution)/shard_map/ppermute | solution.py:337
  11.7 3.9 %collective-permute-start.2 = (bf16[128,512]{1,0:T(8,128)(2,1)S(1)}, bf16[128,512]{1,0:T(8,128)(2,1)S(1)}, u32[]{:S(2)}, u32[]{:S(2)}) collective-permute-start(bf16[128,512]{1,0:T(8,128)(2,1)S(1)} %collective-permute-done.1.refs_0_.refs_2_), channel_id=1, source_target_pairs={{0,1},{1,0},{2,3},{3,2},{4,5},{5,4},{6,7},{7,6},{8,9},{9,8},{10,11... | collective-permute-start | bytes 393224 | tf_op jit(solution)/shard_map/ppermute | solution.py:340
  14.6 1.5 %collective-permute-start.4 = (bf16[128,512]{1,0:T(8,128)(2,1)S(1)}, bf16[128,512]{1,0:T(8,128)(2,1)S(1)}, u32[]{:S(2)}, u32[]{:S(2)}) collective-permute-start(bf16[128,512]{1,0:T(8,128)(2,1)S(1)} %collective-permute-done.3.refs_0_.refs_4_), channel_id=1, source_target_pairs={{0,1},{1,0},{2,3},{3,2},{4,5},{5,4},{6,7},{7,6},{8,9},{9,8},{10,11... | collective-permute-start | bytes 393224 | tf_op jit(solution)/shard_map/ppermute | solution.py:340
  14.9 1.7 %collective-permute-start.6 = (bf16[128,512]{1,0:T(8,128)(2,1)S(1)}, bf16[128,512]{1,0:T(8,128)(2,1)S(1)}, u32[]{:S(2)}, u32[]{:S(2)}) collective-permute-start(bf16[128,512]{1,0:T(8,128)(2,1)S(1)} %collective-permute-done.5.refs_0_.refs_6_), channel_id=1, source_target_pairs={{0,1},{1,0},{2,3},{3,2},{4,5},{5,4},{6,7},{7,6},{8,9},{9,8},{10,11... | collective-permute-start | bytes 393224 | tf_op jit(solution)/shard_map/ppermute | solution.py:340
  16.9 3.4 %copy-start.1 = (f32[4,128]{1,0:T(4,128)S(1)}, f32[4,128]{1,0:T(4,128)}, u32[]{:S(2)}) copy-start(f32[4,128]{1,0:T(4,128)} %param.11) | copy-start | bytes 6148
  16.9 3.4 %copy-start.2 = (f32[4,128]{1,0:T(4,128)S(1)}, f32[4,128]{1,0:T(4,128)}, u32[]{:S(2)}) copy-start(f32[4,128]{1,0:T(4,128)} %param.12) | copy-start | bytes 6148
  17.0 7.4 %collective-permute-start.7 = (bf16[528,128]{1,0:T(8,128)(2,1)S(1)}, bf16[528,128]{1,0:T(8,128)(2,1)S(1)}, u32[]{:S(2)}, u32[]{:S(2)}) collective-permute-start(bf16[528,128]{1,0:T(8,128)(2,1)S(1)} %kv_step.8.refs_12_), channel_id=1, source_target_pairs={{0,8},{8,16},{16,24},{24,0},{1,9},{9,17},{17,25},{25,1},{2,10},{10... | collective-permute-start | bytes 405512 | tf_op jit(solution)/shard_map/ppermute | solution.py:343
  18.8 7.6 %collective-permute-start.8 = (bf16[128,512]{1,0:T(8,128)(2,1)S(1)}, bf16[128,512]{1,0:T(8,128)(2,1)S(1)}, u32[]{:S(2)}, u32[]{:S(2)}) collective-permute-start(bf16[128,512]{1,0:T(8,128)(2,1)S(1)} %kv_step.9.val_ref), channel_id=1, source_target_pairs={{0,8},{8,16},{16,24},{24,0},{1,9},{9,17},{17,25},{25,1},{2,10},{10... | collective-permute-start | bytes 393224 | tf_op jit(solution)/shard_map/ppermute | solution.py:343
  26.8 1.4 %collective-permute-start.9 = (bf16[1,128,512]{2,1,0:T(8,128)(2,1)S(1)}, bf16[1,128,512]{2,1,0:T(8,128)(2,1)S(1)}, u32[]{:S(2)}, u32[]{:S(2)}) collective-permute-start(bf16[1,128,512]{2,1,0:T(8,128)(2,1)S(1)} %get-tuple-element.44), channel_id=1, source_target_pairs={{0,1},{1,0},{2,3},{3,2},{4,5},{5,4},{6,7},{7,6},{8,9},{9,8},{10,11... | collective-permute-start | bytes 393224 | tf_op jit(solution)/shard_map/ppermute | solution.py:340
  28.2 2.3 %collective-permute-start.10 = (bf16[3,128,512]{2,1,0:T(8,128)(2,1)S(1)}, bf16[3,128,512]{2,1,0:T(8,128)(2,1)S(1)}, u32[]{:S(2)}, u32[]{:S(2)}) collective-permute-start(bf16[3,128,512]{2,1,0:T(8,128)(2,1)S(1)} %get-tuple-element.45), channel_id=1, source_target_pairs={{0,1},{1,0},{2,3},{3,2},{4,5},{5,4},{6,7},{7,6},{8,9},{9,8},{10,11... | collective-permute-start | bytes 1179656 | tf_op jit(solution)/shard_map/ppermute | solution.py:340
  28.4 12.5 %collective-permute-start.11 = (bf16[128,512]{1,0:T(8,128)(2,1)S(1)}, bf16[128,512]{1,0:T(8,128)(2,1)S(1)}, u32[]{:S(2)}, u32[]{:S(2)}) collective-permute-start(bf16[128,512]{1,0:T(8,128)(2,1)S(1)} %add_bitcast_fusion), channel_id=1, source_target_pairs={{0,4},{1,5},{2,6},{3,7},{4,0},{5,1},{6,2},{7,3},{8,12},{9,13},{10,... | collective-permute-start | bytes 393224 | tf_op jit(solution)/shard_map/ppermute | solution.py:337
  30.6 10.4 %collective-permute-start.12 = (bf16[128,512]{1,0:T(8,128)(2,1)S(1)}, bf16[128,512]{1,0:T(8,128)(2,1)S(1)}, u32[]{:S(2)}, u32[]{:S(2)}) collective-permute-start(bf16[128,512]{1,0:T(8,128)(2,1)S(1)} %get-tuple-element.47), channel_id=1, source_target_pairs={{0,2},{1,3},{2,4},{3,5},{4,6},{5,7},{6,0},{7,1},{8,10},{9,11},{10,... | collective-permute-start | bytes 393224 | tf_op jit(solution)/shard_map/ppermute | solution.py:337
  33.2 8.3 %collective-permute-start.13 = (bf16[128,512]{1,0:T(8,128)(2,1)S(1)}, bf16[128,512]{1,0:T(8,128)(2,1)S(1)}, u32[]{:S(2)}, u32[]{:S(2)}) collective-permute-start(bf16[128,512]{1,0:T(8,128)(2,1)S(1)} %get-tuple-element.48), channel_id=1, source_target_pairs={{0,6},{1,7},{2,0},{3,1},{4,2},{5,3},{6,4},{7,5},{8,14},{9,15},{10,... | collective-permute-start | bytes 393224 | tf_op jit(solution)/shard_map/ppermute | solution.py:337

commit v10 on v8

--- a/solution.py
+++ b/solution.py
@@ -121,7 +121,7 @@
     w_ref = refs.pop(0)
     acc_ref = None if first else refs.pop(0)
     doc_ref = refs.pop(0) if last == "keys" else None
-    (out_ref,) = refs
+    out_ref = refs[0]
     rows, depth = x_refs[0].shape
     for kind in kinds:
         total = None if first else acc_ref[kind - 1]
@@ -130,15 +130,15 @@
             start = pl.multiple_of(row_block(core, place, i) * depth, depth)
             term = dot(x_ref[...], w_ref[kind - 1, pl.ds(start, depth)])
             total = term if total is None else total + term
-        if last == "keys":
+        if last == "keys" and kind == 2:
+            refs[1][...] = total.astype(BF16)
+        elif last == "keys":
             head_dim = out_ref.shape[1]
             for h in range(total.shape[1] // head_dim):
                 part = total[:, h * head_dim : (h + 1) * head_dim]
                 out_ref[h * rows : (h + 1) * rows] = part.astype(BF16)
             docs = jnp.broadcast_to(doc_ref[...], (16, rows)).astype(BF16)
             out_ref[out_ref.shape[0] - 16 :] = docs
-        elif last == "values":
-            out_ref[...] = total.astype(BF16)
         else:
             out_ref[kind - 1] = total
 
@@ -152,9 +152,10 @@
     out = pltpu.VMEM((2, rows, cols), F32)
     if last == "keys":
         assert rows == cols // heads
-        out = pltpu.VMEM((heads * rows + 16, cols // heads), BF16)
-    elif last == "values":
-        out = pltpu.VMEM((rows, cols), BF16)
+        out = (
+            pltpu.VMEM((heads * rows + 16, cols // heads), BF16),
+            pltpu.VMEM((rows, cols), BF16),
+        )
     return call(
         functools.partial(kv_kernel, sources, kinds, acc is None, last),
         out,
@@ -380,9 +381,10 @@
             part[last, 0] = mine[last]
         acc = kv_step(part, w_kv, acc)
     part = {(last, 1): other[last]}
-    own_key = kv_step(part, w_kv, acc, (1,), "keys", docs, content_bias.shape[0])
+    own_key, own_val = kv_step(
+        part, w_kv, acc, (1, 2), "keys", docs, content_bias.shape[0]
+    )
     mem_key = onward(own_key)
-    own_val = kv_step(part, w_kv, acc, (2,), "values")
     mem_val = onward(own_val)
     own_val, rel = lax.optimization_barrier((own_val, rel))
     query_content, score, w_out = queries(

time: 42.8 us -> 42.8 us (level)
    pallas_call x5 -> x4, Pallas kernels: 1.98 us -> 1.82 us  [kv_step(): call(functools.partial(kv_kernel, sources, kinds, acc is None, last), out...]
  transfers between devices with their start and end apart: 14 -> 14, of which waited for: 7 -> 7; matrix products, arithmetic and copies ran while one was open for 0% -> 0% of each run, Pallas kernels for 29% -> 28%
where the time goes in v10:
time: 42.8 us; the launch traced here: 42.4 us
  starting transfers between devices  16.9 us (39%)
  Pallas kernels  13.4 us (31%)
  waiting for transfers between devices  11.8 us (28%)
    ppermute x6, starting transfers between devices, across(): lax.ppermute(value, 'mp', [(i, (i + 2 * k) % count) for i in range(count)])  13 us
    ppermute x6, waiting for transfers between devices, across(): lax.ppermute(value, 'mp', [(i, (i + 2 * k) % count) for i in range(count)])  9.8 us
    pallas_call x1, Pallas kernels, load(): call(functools.partial(load_kernel, parts), (pltpu.VMEM((rows, cols), BF1...  4.76 us
    pallas_call x1, Pallas kernels, queries(): call(functools.partial(q_kernel, count, heads), (pltpu.VMEM((rows, cols),...  3.56 us
    ppermute x2, starting transfers between devices, onward(): lax.ppermute(value, 'seq', [(i, (i + 1) % segments) for i in range(segmen...  3.03 us
    pallas_call x4, Pallas kernels, kv_step(): call(functools.partial(kv_kernel, sources, kinds, acc is None, last), out...  1.82 us
    pallas_call x1, Pallas kernels, weigh(): call(weigh_kernel, (pltpu.VMEM((heads, rows, rows), BF16), pltpu.VMEM((ro...  1.46 us
    ppermute x2, waiting for transfers between devices, onward(): lax.ppermute(value, 'seq', [(i, (i + 1) % segments) for i in range(segmen...  1.39 us
  transfers between devices with their start and end apart: 14, of which 7 were waited for; matrix products, arithmetic and copies ran while one was open for 0% of the time, Pallas kernels for 28%

profile of v10, /device:TPU:0, one launch (start us, length us, event | category | flops | bytes accessed | tf_op | source)
XLA Modules:
  0.0 42.4 jit_solution(12281002849576444005)
XLA Ops:
  0.0 3.0 %collective-permute-start.1 = (bf16[128,512]{1,0:T(8,128)(2,1)}, bf16[128,512]{1,0:T(8,128)(2,1)S(1)}, u32[]{:S(2)}, u32[]{:S(2)}) collective-permute-start(bf16[128,512]{1,0:T(8,128)(2,1)} %refs_0_.3), channel_id=1, source_target_pairs={{0,2},{1,3},{2,4},{3,5},{4,6},{5,7},{6,0},{7,1},{8,10},{9,11},{10,... | collective-permute-start | bytes 393224 | tf_op jit(solution)/shard_map/ppermute | solution.py:361
  3.0 2.6 %collective-permute-start.3 = (bf16[128,512]{1,0:T(8,128)(2,1)}, bf16[128,512]{1,0:T(8,128)(2,1)S(1)}, u32[]{:S(2)}, u32[]{:S(2)}) collective-permute-start(bf16[128,512]{1,0:T(8,128)(2,1)} %refs_0_.3), channel_id=1, source_target_pairs={{0,4},{1,5},{2,6},{3,7},{4,0},{5,1},{6,2},{7,3},{8,12},{9,13},{10,... | collective-permute-start | bytes 393224 | tf_op jit(solution)/shard_map/ppermute | solution.py:361
  5.6 1.3 %collective-permute-start.5 = (bf16[128,512]{1,0:T(8,128)(2,1)}, bf16[128,512]{1,0:T(8,128)(2,1)S(1)}, u32[]{:S(2)}, u32[]{:S(2)}) collective-permute-start(bf16[128,512]{1,0:T(8,128)(2,1)} %refs_0_.3), channel_id=1, source_target_pairs={{0,6},{1,7},{2,0},{3,1},{4,2},{5,3},{6,4},{7,5},{8,14},{9,15},{10,... | collective-permute-start | bytes 393224 | tf_op jit(solution)/shard_map/ppermute | solution.py:361
  7.0 4.8 %load.1 = (bf16[256,512]{1,0:T(8,128)(2,1)S(1)}, bf16[2,4096,512]{2,1,0:T(8,128)(2,1)S(1)}) custom-call(bf16[4096,512]{1,0:T(8,128)(2,1)} %w_pos.1, bf16[3,4096,512]{2,1,0:T(8,128)(2,1)} %refs_8_.1), custom_call_target="tpu_custom_call" | custom-call | flops 1048576 | bytes 1048576 | tf_op jit(solution)/shard_map/load/pallas_call | solution.py:93
  12.0 2.5 %collective-permute-done.3.refs_0_.refs_4_ = bf16[128,512]{1,0:T(8,128)(2,1)S(1)} collective-permute-done((bf16[128,512]{1,0:T(8,128)(2,1)}, bf16[128,512]{1,0:T(8,128)(2,1)S(1)}, u32[]{:S(2)}, u32[]{:S(2)}) %collective-permute-start.3) | collective-permute-done | bytes 131104 | tf_op jit(solution)/shard_map/ppermute | solution.py:361
  15.2 0.4 %kv_step.4.refs_3_ = f32[2,128,512]{2,1,0:T(8,128)S(1)} custom-call(bf16[128,512]{1,0:T(8,128)(2,1)S(1)} %copy-done, bf16[128,512]{1,0:T(8,128)(2,1)S(1)} %collective-permute-done.refs_1_, bf16[2,4096,512]{2,1,0:T(8,128)(2,1)S(1)} %get-tuple-element.34.refs_2_.refs_3_.refs_1_), custom_call_target="tpu_custom_call" | custom-call | flops 536870912 | tf_op jit(solution)/shard_map/kv_step/pallas_call | solution.py:159
  15.6 0.5 %kv_step.5.refs_4_ = f32[2,128,512]{2,1,0:T(8,128)S(1)} custom-call(bf16[128,512]{1,0:T(8,128)(2,1)S(1)} %collective-permute-done.1.refs_0_.refs_2_, bf16[128,512]{1,0:T(8,128)(2,1)S(1)} %collective-permute-done.2.refs_1_.refs_3_, bf16[2,4096,512]{2,1,0:T(8,128)(2,1)S(1)} %get-tuple-element.34.refs_2_.refs_3_.refs_1_, f32[2,128,512]{2,1,0:T(8,128)S(1)} %kv_step.4.refs_3_), custom_call_target="tpu_custom_call" | custom-call | flops 536870912 | tf_op jit(solution)/shard_map/kv_step/pallas_call | solution.py:159
  16.1 0.6 %kv_step.6.refs_2_ = f32[2,128,512]{2,1,0:T(8,128)S(1)} custom-call(bf16[128,512]{1,0:T(8,128)(2,1)S(1)} %collective-permute-done.3.refs_0_.refs_4_, bf16[128,512]{1,0:T(8,128)(2,1)S(1)} %collective-permute-done.4.refs_1_.refs_5_, bf16[128,512]{1,0:T(8,128)(2,1)S(1)} %collective-permute-done.5.refs_2_.refs_6_, ...), custom_call_target="tpu_custom_call" | custom-call | flops 536870912 | tf_op jit(solution)/shard_map/kv_step/pallas_call | solution.py:159
  16.8 0.3 kv_step.7
  17.1 1.6 %collective-permute-start.7 = (bf16[528,128]{1,0:T(8,128)(2,1)S(1)}, bf16[528,128]{1,0:T(8,128)(2,1)S(1)}, u32[]{:S(2)}, u32[]{:S(2)}) collective-permute-start(bf16[528,128]{1,0:T(8,128)(2,1)S(1)} %get-tuple-element.35.refs_12_), channel_id=1, source_target_pairs={{0,8},{8,16},{16,24},{24,0},{1,9},{9,17},{17,25},{25,1},{2,10},{10... | collective-permute-start | bytes 405512 | tf_op jit(solution)/shard_map/ppermute | solution.py:367
  18.6 1.5 %collective-permute-start.8 = (bf16[128,512]{1,0:T(8,128)(2,1)S(1)}, bf16[128,512]{1,0:T(8,128)(2,1)S(1)}, u32[]{:S(2)}, u32[]{:S(2)}) collective-permute-start(bf16[128,512]{1,0:T(8,128)(2,1)S(1)} %get-tuple-element.41.val_ref), channel_id=1, source_target_pairs={{0,8},{8,16},{16,24},{24,0},{1,9},{9,17},{17,25},{25,1},{2,10},{10... | collective-permute-start | bytes 393224 | tf_op jit(solution)/shard_map/ppermute | solution.py:367
  20.1 3.6 %queries.1 = (bf16[128,512]{1,0:T(8,128)(2,1)S(1)}, f32[4,128,256]{2,1,0:T(8,128)S(1)}, bf16[512,4096]{1,0:T(8,128)(2,1)S(1)}) custom-call(bf16[128,512]{1,0:T(8,128)(2,1)S(1)} %copy-done, bf16[128,512]{1,0:T(8,128)(2,1)S(1)} %collective-permute-done.refs_1_, bf16[128,512]{1,0:T(8,128)(2,1)S(1)} %collective-permute-done.1.refs_0_.refs_2_, ...), custom_call_target="tpu_custom_call" | custom-call | flops 536870912 | bytes 4194304 | tf_op jit(solution)/shard_map/queries/pallas_call | solution.py:215
  23.7 0.8 %collective-permute-done.7.mem_ref = bf16[528,128]{1,0:T(8,128)(2,1)S(1)} collective-permute-done((bf16[528,128]{1,0:T(8,128)(2,1)S(1)}, bf16[528,128]{1,0:T(8,128)(2,1)S(1)}, u32[]{:S(2)}, u32[]{:S(2)}) %collective-permute-start.7) | collective-permute-done | bytes 135200 | tf_op jit(solution)/shard_map/ppermute | solution.py:367
  24.5 1.5 %weigh.1 = (bf16[4,128,128]{2,1,0:T(8,128)(2,1)S(1)}, f32[128,512]{1,0:T(8,128)S(1)}) custom-call(bf16[128,512]{1,0:T(8,128)(2,1)S(1)} %get-tuple-element.39.qc_ref, f32[4,128,256]{2,1,0:T(8,128)S(1)} %get-tuple-element.40.score_ref, bf16[528,128]{1,0:T(8,128)(2,1)S(1)} %collective-permute-done.7.mem_ref, bf16[128,512]{1,0:T(8,128)(2,1)S(1)} %get-tuple-element.41.val_ref, ...), custom_call_target="tpu_custom_call" | custom-call | flops 67108864 | bytes 524288 | tf_op jit(solution)/shard_map/weigh/pallas_call | solution.py:265
  25.9 0.6 %collective-permute-done.8.mem_ref = bf16[128,512]{1,0:T(8,128)(2,1)S(1)} collective-permute-done((bf16[128,512]{1,0:T(8,128)(2,1)S(1)}, bf16[128,512]{1,0:T(8,128)(2,1)S(1)}, u32[]{:S(2)}, u32[]{:S(2)}) %collective-permute-start.8) | collective-permute-done | bytes 131104 | tf_op jit(solution)/shard_map/ppermute | solution.py:367
  26.5 0.3 mix.1
  27.0 0.7 %rest.1 = (bf16[3,128,512]{2,1,0:T(8,128)(2,1)S(1)}, f32[4,128,512]{2,1,0:T(8,128)S(1)}) custom-call(bf16[128,512]{1,0:T(8,128)(2,1)S(1)} %get-tuple-element.45.head_ref, bf16[512,4096]{1,0:T(8,128)(2,1)S(1)} %get-tuple-element.44.w_ref), custom_call_target="tpu_custom_call" | custom-call | flops 536870912 | bytes 4194304 | tf_op jit(solution)/shard_map/rest/pallas_call | solution.py:316
  27.7 0.6 %collective-permute-done.9 = bf16[1,128,512]{2,1,0:T(8,128)(2,1)S(1)} collective-permute-done((bf16[1,128,512]{2,1,0:T(8,128)(2,1)S(1)}, bf16[1,128,512]{2,1,0:T(8,128)(2,1)S(1)}, u32[]{:S(2)}, u32[]{:S(2)}) %collective-permute-start.9) | collective-permute-done | bytes 131104 | tf_op jit(solution)/shard_map/ppermute | solution.py:364
  28.5 2.1 %collective-permute-start.11 = (bf16[128,512]{1,0:T(8,128)(2,1)S(1)}, bf16[128,512]{1,0:T(8,128)(2,1)S(1)}, u32[]{:S(2)}, u32[]{:S(2)}) collective-permute-start(bf16[128,512]{1,0:T(8,128)(2,1)S(1)} %add_bitcast_fusion.1), channel_id=1, source_target_pairs={{0,4},{1,5},{2,6},{3,7},{4,0},{5,1},{6,2},{7,3},{8,12},{9,13},{10,... | collective-permute-start | bytes 393224 | tf_op jit(solution)/shard_map/ppermute | solution.py:361
  30.8 2.6 %collective-permute-start.12 = (bf16[128,512]{1,0:T(8,128)(2,1)S(1)}, bf16[128,512]{1,0:T(8,128)(2,1)S(1)}, u32[]{:S(2)}, u32[]{:S(2)}) collective-permute-start(bf16[128,512]{1,0:T(8,128)(2,1)S(1)} %get-tuple-element.52), channel_id=1, source_target_pairs={{0,2},{1,3},{2,4},{3,5},{4,6},{5,7},{6,0},{7,1},{8,10},{9,11},{10,... | collective-permute-start | bytes 393224 | tf_op jit(solution)/shard_map/ppermute | solution.py:361
  33.4 1.3 %collective-permute-start.13 = (bf16[128,512]{1,0:T(8,128)(2,1)S(1)}, bf16[128,512]{1,0:T(8,128)(2,1)S(1)}, u32[]{:S(2)}, u32[]{:S(2)}) collective-permute-start(bf16[128,512]{1,0:T(8,128)(2,1)S(1)} %get-tuple-element.51), channel_id=1, source_target_pairs={{0,6},{1,7},{2,0},{3,1},{4,2},{5,3},{6,4},{7,5},{8,14},{9,15},{10,... | collective-permute-start | bytes 393224 | tf_op jit(solution)/shard_map/ppermute | solution.py:361
  34.7 6.4 %collective-permute-done.11.refs_0_ = bf16[128,512]{1,0:T(8,128)(2,1)S(1)} collective-permute-done((bf16[128,512]{1,0:T(8,128)(2,1)S(1)}, bf16[128,512]{1,0:T(8,128)(2,1)S(1)}, u32[]{:S(2)}, u32[]{:S(2)}) %collective-permute-start.11) | collective-permute-done | bytes 131104 | tf_op jit(solution)/shard_map/ppermute | solution.py:361
  41.1 0.6 %collective-permute-done.13.refs_2_ = bf16[128,512]{1,0:T(8,128)(2,1)S(1)} collective-permute-done((bf16[128,512]{1,0:T(8,128)(2,1)S(1)}, bf16[128,512]{1,0:T(8,128)(2,1)S(1)}, u32[]{:S(2)}, u32[]{:S(2)}) %collective-permute-start.13) | collective-permute-done | bytes 131104 | tf_op jit(solution)/shard_map/ppermute | solution.py:361
  41.6 0.7 %total.1 = bf16[128,512]{1,0:T(8,128)(2,1)} custom-call(f32[128,512]{1,0:T(8,128)S(1)} %get-tuple-element.53.own_ref, bf16[128,512]{1,0:T(8,128)(2,1)S(1)} %collective-permute-done.11.refs_0_, bf16[128,512]{1,0:T(8,128)(2,1)S(1)} %collective-permute-done.12.refs_1_, bf16[128,512]{1,0:T(8,128)(2,1)S(1)} %collective-permute-done.13.refs_2_), custom_call_target="tpu_custom_call" | custom-call | tf_op jit(solution)/shard_map/total/pallas_call | solution.py:342
  (25 shorter events, 1.4 us)
Async XLA Ops:
  0.0 15.2 %copy-start = (bf16[128,512]{1,0:T(8,128)(2,1)S(1)}, bf16[128,512]{1,0:T(8,128)(2,1)}, u32[]{:S(2)}) copy-start(bf16[128,512]{1,0:T(8,128)(2,1)} %refs_0_.3) | copy-start | bytes 393220
  0.0 14.6 %copy-start.3 = (s32[128]{0:T(128)S(1)}, s32[128]{0:T(128)}, u32[]{:S(2)}) copy-start(s32[128]{0:T(128)} %param.13) | copy-start | bytes 1540
  0.0 11.7 %collective-permute-start.1 = (bf16[128,512]{1,0:T(8,128)(2,1)}, bf16[128,512]{1,0:T(8,128)(2,1)S(1)}, u32[]{:S(2)}, u32[]{:S(2)}) collective-permute-start(bf16[128,512]{1,0:T(8,128)(2,1)} %refs_0_.3), channel_id=1, source_target_pairs={{0,2},{1,3},{2,4},{3,5},{4,6},{5,7},{6,0},{7,1},{8,10},{9,11},{10,... | collective-permute-start | bytes 393224 | tf_op jit(solution)/shard_map/ppermute | solution.py:361
  3.0 11.6 %collective-permute-start.3 = (bf16[128,512]{1,0:T(8,128)(2,1)}, bf16[128,512]{1,0:T(8,128)(2,1)S(1)}, u32[]{:S(2)}, u32[]{:S(2)}) collective-permute-start(bf16[128,512]{1,0:T(8,128)(2,1)} %refs_0_.3), channel_id=1, source_target_pairs={{0,4},{1,5},{2,6},{3,7},{4,0},{5,1},{6,2},{7,3},{8,12},{9,13},{10,... | collective-permute-start | bytes 393224 | tf_op jit(solution)/shard_map/ppermute | solution.py:361
  5.6 9.6 %collective-permute-start = (bf16[128,512]{1,0:T(8,128)(2,1)}, bf16[128,512]{1,0:T(8,128)(2,1)S(1)}, u32[]{:S(2)}, u32[]{:S(2)}) collective-permute-start(bf16[128,512]{1,0:T(8,128)(2,1)} %refs_0_.3), channel_id=1, source_target_pairs={{0,1},{1,0},{2,3},{3,2},{4,5},{5,4},{6,7},{7,6},{8,9},{9,8},{10,11... | collective-permute-start | bytes 393224 | tf_op jit(solution)/shard_map/ppermute | solution.py:364
  5.6 9.2 %collective-permute-start.5 = (bf16[128,512]{1,0:T(8,128)(2,1)}, bf16[128,512]{1,0:T(8,128)(2,1)S(1)}, u32[]{:S(2)}, u32[]{:S(2)}) collective-permute-start(bf16[128,512]{1,0:T(8,128)(2,1)} %refs_0_.3), channel_id=1, source_target_pairs={{0,6},{1,7},{2,0},{3,1},{4,2},{5,3},{6,4},{7,5},{8,14},{9,15},{10,... | collective-permute-start | bytes 393224 | tf_op jit(solution)/shard_map/ppermute | solution.py:361
  11.7 3.9 %collective-permute-start.2 = (bf16[128,512]{1,0:T(8,128)(2,1)S(1)}, bf16[128,512]{1,0:T(8,128)(2,1)S(1)}, u32[]{:S(2)}, u32[]{:S(2)}) collective-permute-start(bf16[128,512]{1,0:T(8,128)(2,1)S(1)} %collective-permute-done.1.refs_0_.refs_2_), channel_id=1, source_target_pairs={{0,1},{1,0},{2,3},{3,2},{4,5},{5,4},{6,7},{7,6},{8,9},{9,8},{10,11... | collective-permute-start | bytes 393224 | tf_op jit(solution)/shard_map/ppermute | solution.py:364
  14.6 1.5 %collective-permute-start.4 = (bf16[128,512]{1,0:T(8,128)(2,1)S(1)}, bf16[128,512]{1,0:T(8,128)(2,1)S(1)}, u32[]{:S(2)}, u32[]{:S(2)}) collective-permute-start(bf16[128,512]{1,0:T(8,128)(2,1)S(1)} %collective-permute-done.3.refs_0_.refs_4_), channel_id=1, source_target_pairs={{0,1},{1,0},{2,3},{3,2},{4,5},{5,4},{6,7},{7,6},{8,9},{9,8},{10,11... | collective-permute-start | bytes 393224 | tf_op jit(solution)/shard_map/ppermute | solution.py:364
  14.9 1.9 %collective-permute-start.6 = (bf16[128,512]{1,0:T(8,128)(2,1)S(1)}, bf16[128,512]{1,0:T(8,128)(2,1)S(1)}, u32[]{:S(2)}, u32[]{:S(2)}) collective-permute-start(bf16[128,512]{1,0:T(8,128)(2,1)S(1)} %collective-permute-done.5.refs_2_.refs_6_), channel_id=1, source_target_pairs={{0,1},{1,0},{2,3},{3,2},{4,5},{5,4},{6,7},{7,6},{8,9},{9,8},{10,11... | collective-permute-start | bytes 393224 | tf_op jit(solution)/shard_map/ppermute | solution.py:364
  16.7 3.4 %copy-start.1 = (f32[4,128]{1,0:T(4,128)S(1)}, f32[4,128]{1,0:T(4,128)}, u32[]{:S(2)}) copy-start(f32[4,128]{1,0:T(4,128)} %param.11) | copy-start | bytes 6148
  16.7 3.4 %copy-start.2 = (f32[4,128]{1,0:T(4,128)S(1)}, f32[4,128]{1,0:T(4,128)}, u32[]{:S(2)}) copy-start(f32[4,128]{1,0:T(4,128)} %param.12) | copy-start | bytes 6148
  17.1 7.4 %collective-permute-start.7 = (bf16[528,128]{1,0:T(8,128)(2,1)S(1)}, bf16[528,128]{1,0:T(8,128)(2,1)S(1)}, u32[]{:S(2)}, u32[]{:S(2)}) collective-permute-start(bf16[528,128]{1,0:T(8,128)(2,1)S(1)} %get-tuple-element.35.refs_12_), channel_id=1, source_target_pairs={{0,8},{8,16},{16,24},{24,0},{1,9},{9,17},{17,25},{25,1},{2,10},{10... | collective-permute-start | bytes 405512 | tf_op jit(solution)/shard_map/ppermute | solution.py:367
  18.6 7.9 %collective-permute-start.8 = (bf16[128,512]{1,0:T(8,128)(2,1)S(1)}, bf16[128,512]{1,0:T(8,128)(2,1)S(1)}, u32[]{:S(2)}, u32[]{:S(2)}) collective-permute-start(bf16[128,512]{1,0:T(8,128)(2,1)S(1)} %get-tuple-element.41.val_ref), channel_id=1, source_target_pairs={{0,8},{8,16},{16,24},{24,0},{1,9},{9,17},{17,25},{25,1},{2,10},{10... | collective-permute-start | bytes 393224 | tf_op jit(solution)/shard_map/ppermute | solution.py:367
  26.9 1.4 %collective-permute-start.9 = (bf16[1,128,512]{2,1,0:T(8,128)(2,1)S(1)}, bf16[1,128,512]{2,1,0:T(8,128)(2,1)S(1)}, u32[]{:S(2)}, u32[]{:S(2)}) collective-permute-start(bf16[1,128,512]{2,1,0:T(8,128)(2,1)S(1)} %get-tuple-element.48), channel_id=1, source_target_pairs={{0,1},{1,0},{2,3},{3,2},{4,5},{5,4},{6,7},{7,6},{8,9},{9,8},{10,11... | collective-permute-start | bytes 393224 | tf_op jit(solution)/shard_map/ppermute | solution.py:364
  28.3 2.3 %collective-permute-start.10 = (bf16[3,128,512]{2,1,0:T(8,128)(2,1)S(1)}, bf16[3,128,512]{2,1,0:T(8,128)(2,1)S(1)}, u32[]{:S(2)}, u32[]{:S(2)}) collective-permute-start(bf16[3,128,512]{2,1,0:T(8,128)(2,1)S(1)} %get-tuple-element.49), channel_id=1, source_target_pairs={{0,1},{1,0},{2,3},{3,2},{4,5},{5,4},{6,7},{7,6},{8,9},{9,8},{10,11... | collective-permute-start | bytes 1179656 | tf_op jit(solution)/shard_map/ppermute | solution.py:364
  28.5 12.5 %collective-permute-start.11 = (bf16[128,512]{1,0:T(8,128)(2,1)S(1)}, bf16[128,512]{1,0:T(8,128)(2,1)S(1)}, u32[]{:S(2)}, u32[]{:S(2)}) collective-permute-start(bf16[128,512]{1,0:T(8,128)(2,1)S(1)} %add_bitcast_fusion.1), channel_id=1, source_target_pairs={{0,4},{1,5},{2,6},{3,7},{4,0},{5,1},{6,2},{7,3},{8,12},{9,13},{10,... | collective-permute-start | bytes 393224 | tf_op jit(solution)/shard_map/ppermute | solution.py:361
  30.8 10.3 %collective-permute-start.12 = (bf16[128,512]{1,0:T(8,128)(2,1)S(1)}, bf16[128,512]{1,0:T(8,128)(2,1)S(1)}, u32[]{:S(2)}, u32[]{:S(2)}) collective-permute-start(bf16[128,512]{1,0:T(8,128)(2,1)S(1)} %get-tuple-element.52), channel_id=1, source_target_pairs={{0,2},{1,3},{2,4},{3,5},{4,6},{5,7},{6,0},{7,1},{8,10},{9,11},{10,... | collective-permute-start | bytes 393224 | tf_op jit(solution)/shard_map/ppermute | solution.py:361
  33.4 8.3 %collective-permute-start.13 = (bf16[128,512]{1,0:T(8,128)(2,1)S(1)}, bf16[128,512]{1,0:T(8,128)(2,1)S(1)}, u32[]{:S(2)}, u32[]{:S(2)}) collective-permute-start(bf16[128,512]{1,0:T(8,128)(2,1)S(1)} %get-tuple-element.51), channel_id=1, source_target_pairs={{0,6},{1,7},{2,0},{3,1},{4,2},{5,3},{6,4},{7,5},{8,14},{9,15},{10,... | collective-permute-start | bytes 393224 | tf_op jit(solution)/shard_map/ppermute | solution.py:361
